TPU v7x, 32 devices: a whole 2x2x4 slice. The times are simulated.
32 devices in a mesh: frames: 8 (over y, x, core), rows: 4 (over z).
Axes of the slice: x: 2, y: 2, z: 4, core: 2. Of those that a mesh axis runs over, the one named last changes fastest.
Arguments:
- block_in: bfloat16 [8, 2, 32, 32, 1024], P('frames', None, 'rows'), may hold values from -6 to 6
- block_map: int32 [8], replicated, may hold values from 0 to 7, each once
- noise_level: int32 [8, 2], P('frames'), may hold values from 0 to 999
- w_query: bfloat16 [1024, 1024], replicated, may hold values from -0.1875 to 0.1875
- w_key: bfloat16 [1024, 1024], replicated, may hold values from -0.1875 to 0.1875
- w_value: bfloat16 [1024, 1024], replicated, may hold values from -0.1875 to 0.1875
- w_proj: bfloat16 [1024, 1024], replicated, may hold values from -3 to 3
- w_up: bfloat16 [1024, 4096], replicated, may hold values from -0.1875 to 0.1875
- w_down: bfloat16 [4096, 1024], replicated, may hold values from -0.09375 to 0.09375
- w_mod: bfloat16 [1024, 6144], replicated, may hold values from -0.1875 to 0.1875
- cotangent: bfloat16 [8, 2, 32, 32, 1024], P('frames', None, 'rows'), may hold values from -6 to 6
Outputs:
- block_out: bfloat16 [8, 2, 32, 32, 1024], P('frames', None, 'rows')
- grad_input: float32 [8, 2, 32, 32, 1024], P('frames', None, 'rows')
- grad_query: float32 [1024, 1024], P(('frames', 'rows'))
- grad_key: float32 [1024, 1024], P(('frames', 'rows'))
- grad_value: float32 [1024, 1024], P(('frames', 'rows'))
- grad_proj: float32 [1024, 1024], P(('frames', 'rows'))
- grad_up: float32 [1024, 4096], P(('frames', 'rows'))
- grad_down: float32 [4096, 1024], P(('frames', 'rows'))
- grad_mod: float32 [1024, 6144], P(('frames', 'rows'))
Inputs may be any that keep to these rules, and one draw needn't show every extreme that they name: `block_map`: a permutation: no two slots hold the same frame.
All inputs are finite; a program needn't handle non-finite values.
Results may differ from a plain program's by a relative error of at most 0.014.
Values may be sent and summed in bfloat16 or wider, within the bound.
No kernel may reach another device: no remote copies, remote signals or barrier semaphores. Data moves between devices by JAX's collectives and lax.ppermute only.
A program may use at most 320 MiB of HBM per device.

v0:
```python
import math

import jax
import jax.numpy as jnp
from jax import lax
from jax.sharding import PartitionSpec as P

D = 1024
H = 16
HD = 64
PR = 32
PC = 32


norm_eps = 1e-06


def sinusoid(levels):
    half_size = D // 2
    freq_table = 10000.0 ** (-jnp.arange(half_size, dtype=jnp.float32) / half_size)
    angle_table = levels.astype(jnp.float32)[..., None] * freq_table
    return jnp.concatenate([jnp.cos(angle_table), jnp.sin(angle_table)], axis=-1)


def rotate(vector, time_pos, row_pos, col_pos, flip_sign):
    width_all = vector.shape[-1]
    quarter = width_all // 4
    rest_size = 3 * width_all // 8
    pieces = []
    offset = 0
    for position, part_size in ((time_pos, quarter), (row_pos, rest_size), (col_pos, rest_size)):
        half_size = part_size // 2
        first_half = vector[..., offset : offset + half_size]
        second_half = vector[..., offset + half_size : offset + part_size]
        freq_table = 10000.0 ** (-jnp.arange(half_size, dtype=jnp.float32) / half_size)
        angle_table = position[..., None] * freq_table
        cosine = jnp.cos(angle_table)
        sine_part = flip_sign * jnp.sin(angle_table)
        pieces.append(first_half * cosine - second_half * sine_part)
        pieces.append(second_half * cosine + first_half * sine_part)
        offset += part_size
    return jnp.concatenate(pieces, axis=-1)


def normalize(values):
    centered = values - jnp.mean(values, axis=-1, keepdims=True)
    inverse = lax.rsqrt(jnp.mean(centered * centered, axis=-1, keepdims=True) + norm_eps)
    return (centered * inverse, inverse)


def norm_backward(grad_normed, normed, inverse):
    mean_grad = jnp.mean(grad_normed, axis=-1, keepdims=True)
    mean_prod = jnp.mean(grad_normed * normed, axis=-1, keepdims=True)
    return inverse * (grad_normed - mean_grad - normed * mean_prod)


def matmul(left, right):
    return jnp.dot(left, right, preferred_element_type=jnp.float32)


def left_product(left, right):
    return jnp.einsum("td,te->de", left, right, preferred_element_type=jnp.float32)


def right_product(left, right):
    return jnp.einsum("te,de->td", left, right, preferred_element_type=jnp.float32)


def shards(
    block_in,
    block_map,
    noise_level,
    w_query,
    w_key,
    w_value,
    w_proj,
    w_up,
    w_down,
    w_mod,
    cotangent,
):
    row_count = lax.axis_size("rows")
    frame_slot = lax.axis_index("frames")
    row_shard = lax.axis_index("rows")
    my_time = block_map[frame_slot]
    frame_total = block_map.shape[0]
    clips = block_in.shape[1]
    local_rows = block_in.shape[2]
    heads_local = H // row_count
    wide_local = D // row_count
    patches = PR * PC
    scale_factor = 1.0 / math.sqrt(HD)
    token_axes = (1, 2)
    slots = jnp.arange(frame_total)
    source = block_in[0].astype(jnp.float32)
    embed = jax.nn.silu(sinusoid(noise_level[0])).astype(jnp.bfloat16)
    modulation = matmul(embed, w_mod)[:, None, None, :]
    shift_one, scale_one, gate_one, shift_two, scale_two, gate_two = jnp.split(
        modulation, 6, axis=-1
    )
    normed_one, inverse_one = normalize(source)
    hidden_one = (normed_one * (1.0 + scale_one) + shift_one).astype(jnp.bfloat16)
    flat_one = hidden_one.reshape(-1, D)
    time_value = my_time.astype(jnp.float32)
    row_pos = (row_shard * local_rows + jnp.arange(local_rows)).astype(jnp.float32)[
        None, :, None, None
    ]
    col_pos = jnp.arange(PC, dtype=jnp.float32)[None, None, :, None]
    head_shape = (clips, local_rows, PC, H, HD)
    query_pre = matmul(flat_one, w_query).reshape(head_shape)
    key_pre = matmul(flat_one, w_key).reshape(head_shape)
    query_rot = rotate(query_pre, time_value, row_pos, col_pos, 1.0).astype(jnp.bfloat16)
    key_rot = rotate(key_pre, time_value, row_pos, col_pos, 1.0).astype(jnp.bfloat16)
    value_low = matmul(flat_one, w_value).astype(jnp.bfloat16)
    split_shape = (clips, local_rows, PC, row_count, wide_local)
    back_shape = (clips, PR, PC, 1, wide_local)
    query_heads, key_heads, value_heads = (
        lax.all_to_all(
            query_rot.reshape(split_shape), "rows", split_axis=3, concat_axis=1, tiled=True
        ),
        lax.all_to_all(
            key_rot.reshape(split_shape), "rows", split_axis=3, concat_axis=1, tiled=True
        ),
        lax.all_to_all(
            value_low.reshape(split_shape), "rows", split_axis=3, concat_axis=1, tiled=True
        ),
    )
    query_local = query_heads.reshape(clips, patches, heads_local, HD)
    keys_all, values_all = (
        lax.all_gather(
            key_heads.reshape(1, clips, patches, wide_local), "frames", axis=0, tiled=True
        ),
        lax.all_gather(
            value_heads.reshape(1, clips, patches, wide_local), "frames", axis=0, tiled=True
        ),
    )

    def fetch(stack, slot):
        return lax.dynamic_index_in_dim(stack, slot, 0, keepdims=False).reshape(
            clips, patches, heads_local, HD
        )

    def slot_scores(slot):
        return (
            jnp.einsum(
                "cqhd,ckhd->chqk",
                query_local,
                fetch(keys_all, slot),
                preferred_element_type=jnp.float32,
            )
            * scale_factor
        )

    def max_step(carry, slot):

        def max_update(state):
            scores = slot_scores(slot)
            run_max, run_sum = state
            new_max = jnp.maximum(run_max, jnp.max(scores, axis=-1))
            new_sum = run_sum * jnp.exp(run_max - new_max) + jnp.sum(
                jnp.exp(scores - new_max[..., None]), axis=-1
            )
            return (new_max, new_sum)

        return (lax.cond(block_map[slot] <= my_time, max_update, lambda state: state, carry), None)

    start_max = jnp.full((clips, heads_local, patches), -1e30, jnp.float32)
    start_sum = jnp.zeros((clips, heads_local, patches), jnp.float32)
    (run_max, run_sum), unused = lax.scan(max_step, (start_max, start_sum), slots)
    log_total = run_max + jnp.log(run_sum)

    def output_step(carry, slot):

        def output_update(accum):
            probs = jnp.exp(slot_scores(slot) - log_total[..., None]).astype(jnp.bfloat16)
            return accum + jnp.einsum(
                "chqk,ckhd->cqhd",
                probs,
                fetch(values_all, slot),
                preferred_element_type=jnp.float32,
            )

        return (
            lax.cond(block_map[slot] <= my_time, output_update, lambda accum: accum, carry),
            None,
        )

    attended, unused = lax.scan(
        output_step, jnp.zeros((clips, patches, heads_local, HD), jnp.float32), slots
    )
    attn_back = lax.all_to_all(
        attended.astype(jnp.bfloat16).reshape(back_shape),
        "rows",
        split_axis=1,
        concat_axis=3,
        tiled=True,
    )
    attn_rows = attn_back.reshape(-1, D)
    branch_one = matmul(attn_rows, w_proj).reshape(source.shape)
    middle = source + gate_one * branch_one
    normed_two, inverse_two = normalize(middle)
    hidden_two = (normed_two * (1.0 + scale_two) + shift_two).astype(jnp.bfloat16)
    flat_two = hidden_two.reshape(-1, D)
    upward = matmul(flat_two, w_up)
    active = jax.nn.gelu(upward, approximate=True).astype(jnp.bfloat16)
    branch_two = matmul(active, w_down).reshape(source.shape)
    result = middle + gate_two * branch_two
    grad_result = cotangent[0].astype(jnp.float32)
    grad_gate_two = jnp.sum(grad_result * branch_two, axis=token_axes)
    grad_branch_two = (gate_two * grad_result).astype(jnp.bfloat16).reshape(-1, D)
    grad_down = left_product(active, grad_branch_two)
    grad_active = right_product(grad_branch_two, w_down)
    gelu_pull = jax.vjp(lambda inner: jax.nn.gelu(inner, approximate=True), upward)[1]
    grad_upward = gelu_pull(grad_active)[0].astype(jnp.bfloat16)
    grad_up = left_product(flat_two, grad_upward)
    grad_hidden_two = right_product(grad_upward, w_up).reshape(source.shape)
    grad_scale_two = jnp.sum(grad_hidden_two * normed_two, axis=token_axes)
    grad_shift_two = jnp.sum(grad_hidden_two, axis=token_axes)
    grad_middle = grad_result + norm_backward(
        grad_hidden_two * (1.0 + scale_two), normed_two, inverse_two
    )
    grad_gate_one = jnp.sum(grad_middle * branch_one, axis=token_axes)
    grad_branch_one = (gate_one * grad_middle).astype(jnp.bfloat16).reshape(-1, D)
    grad_proj = left_product(attn_rows, grad_branch_one)
    grad_attn = right_product(grad_branch_one, w_proj).astype(jnp.bfloat16)
    grad_heads = lax.all_to_all(
        grad_attn.reshape(split_shape), "rows", split_axis=3, concat_axis=1, tiled=True
    ).reshape(clips, patches, heads_local, HD)
    delta = jnp.transpose(jnp.sum(grad_heads.astype(jnp.float32) * attended, axis=-1), (0, 2, 1))
    zero_query = jnp.zeros((clips, patches, heads_local, HD), jnp.float32)

    def back_step(carry, slot):

        def back_update(accum):
            keys_slot = fetch(keys_all, slot)
            values_slot = fetch(values_all, slot)
            probs = jnp.exp(slot_scores(slot) - log_total[..., None])
            grad_probs = jnp.einsum(
                "cqhd,ckhd->chqk", grad_heads, values_slot, preferred_element_type=jnp.float32
            )
            grad_scores = (probs * (grad_probs - delta[..., None])).astype(jnp.bfloat16)
            new_accum = accum + jnp.einsum(
                "chqk,ckhd->cqhd", grad_scores, keys_slot, preferred_element_type=jnp.float32
            )
            grad_keys = (
                jnp.einsum(
                    "chqk,cqhd->ckhd", grad_scores, query_local, preferred_element_type=jnp.float32
                )
                * scale_factor
            )
            grad_values = jnp.einsum(
                "chqk,cqhd->ckhd",
                probs.astype(jnp.bfloat16),
                grad_heads,
                preferred_element_type=jnp.float32,
            )
            return (
                new_accum,
                grad_keys.reshape(clips, patches, wide_local),
                grad_values.reshape(clips, patches, wide_local),
            )

        def skip(accum):
            zeroed = jnp.zeros((clips, patches, wide_local), jnp.float32)
            return (accum, zeroed, zeroed)

        new_accum, grad_keys, grad_values = lax.cond(
            block_map[slot] <= my_time, back_update, skip, carry
        )
        return (new_accum, (grad_keys, grad_values))

    grad_query_sum, (key_terms, value_terms) = lax.scan(back_step, zero_query, slots)
    key_grad, value_grad = (
        lax.psum_scatter(
            key_terms.astype(jnp.bfloat16), "frames", scatter_dimension=0, tiled=True
        ).astype(jnp.float32),
        lax.psum_scatter(
            value_terms.astype(jnp.bfloat16), "frames", scatter_dimension=0, tiled=True
        ).astype(jnp.float32),
    )
    key_grad = key_grad.reshape(clips, patches, wide_local)
    value_grad = value_grad.reshape(clips, patches, wide_local)
    token_index = jnp.arange(patches)
    row_heads = (token_index // PC).astype(jnp.float32)[None, :, None]
    col_heads = (token_index % PC).astype(jnp.float32)[None, :, None]
    grad_query_pre = rotate(
        grad_query_sum * scale_factor, time_value, row_heads, col_heads, -1.0
    ).astype(jnp.bfloat16)
    grad_key_pre = rotate(
        key_grad.reshape(clips, patches, heads_local, HD), time_value, row_heads, col_heads, -1.0
    ).astype(jnp.bfloat16)
    grad_value_low = value_grad.astype(jnp.bfloat16)
    query_back, key_back, value_back = (
        lax.all_to_all(
            grad_query_pre.reshape(back_shape), "rows", split_axis=1, concat_axis=3, tiled=True
        ),
        lax.all_to_all(
            grad_key_pre.reshape(back_shape), "rows", split_axis=1, concat_axis=3, tiled=True
        ),
        lax.all_to_all(
            grad_value_low.reshape(back_shape), "rows", split_axis=1, concat_axis=3, tiled=True
        ),
    )
    query_rows = query_back.reshape(-1, D)
    key_rows = key_back.reshape(-1, D)
    value_rows = value_back.reshape(-1, D)
    grad_query = left_product(flat_one, query_rows)
    grad_key = left_product(flat_one, key_rows)
    grad_value = left_product(flat_one, value_rows)
    grad_hidden_one = (
        right_product(query_rows, w_query)
        + right_product(key_rows, w_key)
        + right_product(value_rows, w_value)
    ).reshape(source.shape)
    grad_scale_one = jnp.sum(grad_hidden_one * normed_one, axis=token_axes)
    grad_shift_one = jnp.sum(grad_hidden_one, axis=token_axes)
    grad_source = grad_middle + norm_backward(
        grad_hidden_one * (1.0 + scale_one), normed_one, inverse_one
    )
    grad_modulation = jnp.concatenate(
        [
            grad_shift_one,
            grad_scale_one,
            grad_gate_one,
            grad_shift_two,
            grad_scale_two,
            grad_gate_two,
        ],
        axis=-1,
    )
    full_mod = jnp.dot(
        embed.astype(jnp.float32).T, grad_modulation, precision=lax.Precision.HIGHEST
    )
    grad_mod = lax.psum_scatter(full_mod, ("frames", "rows"), scatter_dimension=0, tiled=True)
    grad_query, grad_key, grad_value, grad_proj, grad_up, grad_down = (
        lax.psum_scatter(grad_query, ("frames", "rows"), scatter_dimension=0, tiled=True),
        lax.psum_scatter(grad_key, ("frames", "rows"), scatter_dimension=0, tiled=True),
        lax.psum_scatter(grad_value, ("frames", "rows"), scatter_dimension=0, tiled=True),
        lax.psum_scatter(grad_proj, ("frames", "rows"), scatter_dimension=0, tiled=True),
        lax.psum_scatter(grad_up, ("frames", "rows"), scatter_dimension=0, tiled=True),
        lax.psum_scatter(grad_down, ("frames", "rows"), scatter_dimension=0, tiled=True),
    )
    return (
        result.astype(jnp.bfloat16)[None],
        grad_source[None],
        grad_query,
        grad_key,
        grad_value,
        grad_proj,
        grad_up,
        grad_down,
        grad_mod,
    )


def solution(mesh):
    placed = (
        P("frames", None, "rows", None, None),
        P(),
        P("frames", None),
        P(),
        P(),
        P(),
        P(),
        P(),
        P(),
        P(),
        P("frames", None, "rows", None, None),
    )
    return jax.shard_map(
        shards,
        mesh=mesh,
        in_specs=placed,
        out_specs=(
            P("frames", None, "rows", None, None),
            P("frames", None, "rows", None, None),
            P(("frames", "rows"), None),
            P(("frames", "rows"), None),
            P(("frames", "rows"), None),
            P(("frames", "rows"), None),
            P(("frames", "rows"), None),
            P(("frames", "rows"), None),
            P(("frames", "rows"), None),
        ),
        check_vma=False,
    )
```

profile of v0, /device:TPU:0, one launch (start us, length us, event | category | flops | bytes accessed | tf_op | source)
XLA Modules:
  0.0 3198.7 jit_solution(5640751440356718814)
XLA Ops:
  100.6 31.8 all_to_all.120
  141.4 28.3 all_to_all.121
  210.2 24.8 all-to-all-done.2
  254.6 254.5 %while.42 = (s32[]{:T(128)}, f32[2,4,1024]{2,1,0:T(4,128)S(1)}, f32[2,4,1024]{2,1,0:T(4,128)S(1)}, s32[8]{0:T(128)S(1)}, s32[8]{0:T(128)S(1)}, /*index=5*/s32[]{...) while((s32[]{:T(128)}, f32[2,4,1024]{2,1,0:T(4,128)S(1)}, ...), condition=%wide.region_7.8_spmd, body=%wide.region_2.7_spmd.sunk | while | flops 1115701248 | bytes 71729456 | solution.py:169
  258.9 31.4 conditional.6
  294.7 31.4 conditional.6
  330.4 31.4 conditional.6
  366.1 31.4 conditional.6
  401.9 31.4 conditional.6
  437.6 31.4 conditional.6
  473.3 31.4 conditional.6
  522.2 152.1 %while.43 = (s32[]{:T(128)}, f32[2,1024,4,64]{1,3,2,0:T(8,128)}, s32[8]{0:T(128)S(1)}, s32[8]{0:T(128)S(1)}, s32[]{:T(128)}, /*index=5*/bf16[8,2,1024,256]{2,3,1...) while((s32[]{:T(128)}, f32[2,1024,4,64]{1,3,2,0:T(8,128)}, ...), condition=%wide.region_11.12_spmd, body=%wide.region_8.11_spmd.sunk | while | flops 2173173760 | bytes 11567387 | solution.py:188
  526.7 16.7 conditional.7
  547.8 16.7 conditional.7
  568.9 16.7 conditional.7
  590.0 16.7 conditional.7
  611.0 16.7 conditional.7
  632.1 16.7 conditional.7
  653.2 16.7 conditional.7
  714.1 16.6 fusion.14
  790.8 552.1 %while.44 = (s32[]{:T(128)}, f32[2,1024,4,64]{1,3,2,0:T(8,128)}, bf16[8,2,1024,256]{2,3,1,0:T(8,128)(2,1)}, bf16[8,2,1024,256]{3,2,1,0:T(8,128)(2,1)}, s32[8]{0:...) while((s32[]{:T(128)}, f32[2,1024,4,64]{1,3,2,0:T(8,128)}, ...), condition=%wide.region_20.21_spmd, body=%wide.region_17.20_spmd.sunk | while | flops 5437390848 | bytes 242320768 | solution.py:272
  795.3 69.5 %conditional.8 = (f32[2,1024,4,64]{1,3,2,0:T(8,128)}, bf16[1,2,1024,256]{2,3,1,0:T(8,128)(2,1)S(1)}, bf16[1,2,1024,256]{2,3,1,0:T(8,128)(2,1)}) conditional(s32[]{:T(128)} %convert_element_type.384, f32[2,1024,4,64]{1,3,2,0:T(8,128)} %get-tuple-element.818, (s32[]{:T(128)}, bf16[8,2,1024,256]{2,3,1,0:T(8,128)(2,1)}, ...), branch_computations={%region_18.18_spmd, %region_19.19_spmd} | conditional | flops 5437390848 | bytes 236028000 | solution.py:267
  813.4 18.4 multiply_convert_fusion
  850.1 14.7 fusion.5
  872.7 69.5 %conditional.8 = (f32[2,1024,4,64]{1,3,2,0:T(8,128)}, bf16[1,2,1024,256]{2,3,1,0:T(8,128)(2,1)S(1)}, bf16[1,2,1024,256]{2,3,1,0:T(8,128)(2,1)}) conditional(s32[]{:T(128)} %convert_element_type.384, f32[2,1024,4,64]{1,3,2,0:T(8,128)} %get-tuple-element.818, (s32[]{:T(128)}, bf16[8,2,1024,256]{2,3,1,0:T(8,128)(2,1)}, ...), branch_computations={%region_18.18_spmd, %region_19.19_spmd} | conditional | flops 5437390848 | bytes 236028000 | solution.py:267
  890.9 18.4 multiply_convert_fusion
  927.5 14.7 fusion.5
  950.2 69.5 %conditional.8 = (f32[2,1024,4,64]{1,3,2,0:T(8,128)}, bf16[1,2,1024,256]{2,3,1,0:T(8,128)(2,1)S(1)}, bf16[1,2,1024,256]{2,3,1,0:T(8,128)(2,1)}) conditional(s32[]{:T(128)} %convert_element_type.384, f32[2,1024,4,64]{1,3,2,0:T(8,128)} %get-tuple-element.818, (s32[]{:T(128)}, bf16[8,2,1024,256]{2,3,1,0:T(8,128)(2,1)}, ...), branch_computations={%region_18.18_spmd, %region_19.19_spmd} | conditional | flops 5437390848 | bytes 236028000 | solution.py:267
  968.3 18.4 multiply_convert_fusion
  1027.7 69.5 %conditional.8 = (f32[2,1024,4,64]{1,3,2,0:T(8,128)}, bf16[1,2,1024,256]{2,3,1,0:T(8,128)(2,1)S(1)}, bf16[1,2,1024,256]{2,3,1,0:T(8,128)(2,1)}) conditional(s32[]{:T(128)} %convert_element_type.384, f32[2,1024,4,64]{1,3,2,0:T(8,128)} %get-tuple-element.818, (s32[]{:T(128)}, bf16[8,2,1024,256]{2,3,1,0:T(8,128)(2,1)}, ...), branch_computations={%region_18.18_spmd, %region_19.19_spmd} | conditional | flops 5437390848 | bytes 236028000 | solution.py:267
  1045.8 18.4 multiply_convert_fusion
  1105.2 69.5 %conditional.8 = (f32[2,1024,4,64]{1,3,2,0:T(8,128)}, bf16[1,2,1024,256]{2,3,1,0:T(8,128)(2,1)S(1)}, bf16[1,2,1024,256]{2,3,1,0:T(8,128)(2,1)}) conditional(s32[]{:T(128)} %convert_element_type.384, f32[2,1024,4,64]{1,3,2,0:T(8,128)} %get-tuple-element.818, (s32[]{:T(128)}, bf16[8,2,1024,256]{2,3,1,0:T(8,128)(2,1)}, ...), branch_computations={%region_18.18_spmd, %region_19.19_spmd} | conditional | flops 5437390848 | bytes 236028000 | solution.py:267
  1123.4 18.4 multiply_convert_fusion
  1182.7 69.5 %conditional.8 = (f32[2,1024,4,64]{1,3,2,0:T(8,128)}, bf16[1,2,1024,256]{2,3,1,0:T(8,128)(2,1)S(1)}, bf16[1,2,1024,256]{2,3,1,0:T(8,128)(2,1)}) conditional(s32[]{:T(128)} %convert_element_type.384, f32[2,1024,4,64]{1,3,2,0:T(8,128)} %get-tuple-element.818, (s32[]{:T(128)}, bf16[8,2,1024,256]{2,3,1,0:T(8,128)(2,1)}, ...), branch_computations={%region_18.18_spmd, %region_19.19_spmd} | conditional | flops 5437390848 | bytes 236028000 | solution.py:267
  1200.8 18.4 multiply_convert_fusion
  1260.1 69.5 %conditional.8 = (f32[2,1024,4,64]{1,3,2,0:T(8,128)}, bf16[1,2,1024,256]{2,3,1,0:T(8,128)(2,1)S(1)}, bf16[1,2,1024,256]{2,3,1,0:T(8,128)(2,1)}) conditional(s32[]{:T(128)} %convert_element_type.384, f32[2,1024,4,64]{1,3,2,0:T(8,128)} %get-tuple-element.818, (s32[]{:T(128)}, bf16[8,2,1024,256]{2,3,1,0:T(8,128)(2,1)}, ...), branch_computations={%region_18.18_spmd, %region_19.19_spmd} | conditional | flops 5437390848 | bytes 236028000 | solution.py:267
  1278.3 18.4 multiply_convert_fusion
  1350.2 176.0 %reduce-scatter.10.cloned.1.call-done = bf16[1,2,1024,256]{2,3,1,0:T(8,128)(2,1)} async-done(((bf16[8,2,1024,256]{2,3,1,0:T(8,128)(2,1)}), bf16[1,2,1024,256]{2,3,1,0:T(8,128)(2,1)}) %reduce-scatter.10.cloned.1.call-update) | async-done | bytes 1048592 | tf_op jit(solution)/shard_map/reduce_scatter | solution.py:274
  1573.8 27.4 reduce-scatter.12.cloned.1.call-done
  1613.6 36.7 %all-to-all-done.7 = bf16[2,32,32,1,256]{4,2,0,3,1:T(8,128)(2,1)S(1)} async-done(((bf16[2,32,32,1,256]{4,2,0,3,1:T(8,128)(2,1)}), bf16[2,32,32,1,256]{4,2,0,3,1:T(8,128)(2,1)S(1)}, u32[]{:S(2)}, u32[]{:S(2)}) %all-to-all-start.7) | async-done | bytes 1048608 | tf_op jit(solution)/shard_map/all_to_all | solution.py:300
  1686.7 15.0 fusion.70
  1716.0 47.2 %reduce-scatter.20.cloned.1.call-done = f32[32,1024]{1,0:T(8,128)} async-done(((f32[1024,1024]{1,0:T(8,128)}), f32[32,1024]{1,0:T(8,128)}) %reduce-scatter.20.cloned.1.call-update) | async-done | bytes 131088 | tf_op jit(solution)/shard_map/reduce_scatter | solution.py:339
  1763.2 149.3 %reduce-scatter.18.cloned.1.call-done = f32[32,1024]{1,0:T(8,128)} async-done(((f32[1024,1024]{1,0:T(8,128)}), f32[32,1024]{1,0:T(8,128)}) %reduce-scatter.18.cloned.1.call-update) | async-done | bytes 131088 | tf_op jit(solution)/shard_map/reduce_scatter | solution.py:338
  1912.5 149.1 %reduce-scatter.16.cloned.1.call-done = f32[32,1024]{1,0:T(8,128)} async-done(((f32[1024,1024]{1,0:T(8,128)}), f32[32,1024]{1,0:T(8,128)}) %reduce-scatter.16.cloned.1.call-update) | async-done | bytes 131088 | tf_op jit(solution)/shard_map/reduce_scatter | solution.py:337
  2061.7 149.8 %reduce-scatter.14.cloned.1.call-done = f32[32,1024]{1,0:T(8,128)} async-done(((f32[1024,1024]{1,0:T(8,128)}), f32[32,1024]{1,0:T(8,128)}) %reduce-scatter.14.cloned.1.call-update) | async-done | bytes 131088 | tf_op jit(solution)/shard_map/reduce_scatter | solution.py:336
  2211.5 365.1 %reduce-scatter.22.cloned.1.call-done = f32[32,4096]{1,0:T(8,128)} async-done(((f32[1024,4096]{1,0:T(8,128)}), f32[32,4096]{1,0:T(8,128)}) %reduce-scatter.22.cloned.1.call-update) | async-done | bytes 524304 | tf_op jit(solution)/shard_map/reduce_scatter | solution.py:340
  2576.6 364.9 %reduce-scatter.24.cloned.1.call-done = f32[128,1024]{1,0:T(8,128)} async-done(((f32[4096,1024]{1,0:T(8,128)}), f32[128,1024]{1,0:T(8,128)}) %reduce-scatter.24.cloned.1.call-update) | async-done | bytes 524304 | tf_op jit(solution)/shard_map/reduce_scatter | solution.py:341
  2941.5 250.4 %reduce-scatter.26.cloned.1.call-done = f32[32,6144]{1,0:T(8,128)} async-done(((f32[1024,6144]{1,0:T(8,128)}), f32[32,6144]{1,0:T(8,128)}) %reduce-scatter.26.cloned.1.call-update) | async-done | bytes 786448 | tf_op jit(solution)/shard_map/reduce_scatter | solution.py:334
  (488 shorter events, 1075.4 us)
Async XLA Ops:
  7.2 702.2 %copy-start = (bf16[1024,1024]{1,0:T(8,128)(2,1)S(1)}, bf16[1024,1024]{1,0:T(8,128)(2,1)}, u32[]{:S(2)}) copy-start(bf16[1024,1024]{1,0:T(8,128)(2,1)} %param.29) | copy-start | bytes 6291460
  7.2 235.9 %all-gather.5.cloned.1.call-start = ((), (), s32[]{:S(2)}) async-start(), calls=%async_computation.18 | async-start | bytes 9437184 | tf_op jit(solution)/shard_map/all_gather | solution.py:130
  7.3 50.4 %copy-start.62 = (f32[12]{0:T(128)}, f32[12]{0:T(128)S(1)}, u32[]{:S(2)}) copy-start(f32[12]{0:T(128)S(1)} %multiply_power_fusion.1) | copy-start | bytes 148
  15.3 118.5 %copy-start.39 = (f32[2,1024]{1,0:T(2,128)}, f32[2,1024]{1,0:T(2,128)S(1)}, u32[]{:S(2)}) copy-start(f32[2,1024]{1,0:T(2,128)S(1)} %get-tuple-element.499) | copy-start | bytes 24580
  15.3 118.5 %copy-start.43 = (f32[2,1024]{1,0:T(2,128)}, f32[2,1024]{1,0:T(2,128)S(1)}, u32[]{:S(2)}) copy-start(f32[2,1024]{1,0:T(2,128)S(1)} %get-tuple-element.495) | copy-start | bytes 24580
  15.3 118.5 %copy-start.45 = (f32[2,1024]{1,0:T(2,128)}, f32[2,1024]{1,0:T(2,128)S(1)}, u32[]{:S(2)}) copy-start(f32[2,1024]{1,0:T(2,128)S(1)} %get-tuple-element.498) | copy-start | bytes 24580
  15.5 118.2 %copy-start.41 = (f32[2,8,32]{2,1,0:T(8,128)}, f32[2,8,32]{2,1,0:T(8,128)S(1)}, u32[]{:S(2)}) copy-start(f32[2,8,32]{2,1,0:T(8,128)S(1)} %broadcast_multiply_fusion.3) | copy-start | bytes 6148
  15.9 117.7 %copy-start.47 = (f32[2,8,32]{2,1,0:T(8,128)}, f32[2,8,32]{2,1,0:T(8,128)S(1)}, u32[]{:S(2)}) copy-start(f32[2,8,32]{2,1,0:T(8,128)S(1)} %add_rsqrt_fusion.1) | copy-start | bytes 6148
  133.6 375.6 %all-gather.3.cloned.1.call-start = ((), (), s32[]{:S(2)}) async-start(), calls=%async_computation.17 | async-start | bytes 9437184 | tf_op jit(solution)/shard_map/all_gather | solution.py:133
  141.4 29.4 copy-start.33
  141.4 31.2 copy-start.32
  206.7 28.3 all-to-all-start.2
  683.1 20.4 all-to-all-start.3
  699.2 10.1 copy-start.9
  699.2 10.1 copy-start.37
  713.2 22.1 copy-start.6
  713.2 17.5 slice-start
  714.1 16.6 copy-start.27
  714.1 16.6 slice-start.1
  736.9 10.4 copy-start.7
  736.9 10.4 copy-start.12
  736.9 10.4 copy-start.17
  736.9 10.4 copy-start.18
  736.9 10.4 copy-start.44
  757.2 19.4 all-to-all-start.4
  760.8 765.4 %reduce-scatter.10.cloned.1.call-start = ((), (), s32[]{:S(2)}) async-start(), calls=%async_computation.19 | async-start | bytes 9437184 | tf_op jit(solution)/shard_map/reduce_scatter | solution.py:274
  831.8 11.9 copy-start.2
  909.2 11.9 copy-start.2
  986.7 11.9 copy-start.2
  1064.2 11.9 copy-start.2
  1141.7 11.9 copy-start.2
  1219.2 11.9 copy-start.2
  1296.6 11.9 copy-start.2
  1342.9 258.3 %reduce-scatter.12.cloned.1.call-start = ((), (), s32[]{:S(2)}) async-start(), calls=%async_computation.20 | async-start | bytes 9437184 | tf_op jit(solution)/shard_map/reduce_scatter | solution.py:277
  1343.5 419.7 %reduce-scatter.20.cloned.1.call-start = ((), (), s32[]{:S(2)}) async-start(), calls=%async_computation.24 | async-start | bytes 4325376 | tf_op jit(solution)/shard_map/reduce_scatter | solution.py:339
  1347.9 179.7 %copy-start.65 = (f32[8]{0:T(128)S(1)}, f32[8]{0:T(128)}, u32[]{:S(2)}) copy-start(f32[8]{0:T(128)} %copy-done.64) | copy-start | bytes 100
  1348.5 181.0 %copy-start.35 = (f32[1024,12]{0,1:T(8,128)}, f32[1024,12]{0,1:T(8,128)S(1)}, u32[]{:S(2)}) copy-start(f32[1024,12]{0,1:T(8,128)S(1)} %get-tuple-element.513) | copy-start | bytes 147460
  1348.6 181.0 %copy-start.36 = (f32[1024,12]{0,1:T(8,128)}, f32[1024,12]{0,1:T(8,128)S(1)}, u32[]{:S(2)}) copy-start(f32[1024,12]{0,1:T(8,128)S(1)} %get-tuple-element.514) | copy-start | bytes 147460
  1539.8 30.5 all-to-all-start.6
  1570.2 33.3 %all-to-all-start.5 = ((bf16[2,32,32,1,256]{4,2,0,3,1:T(8,128)(2,1)}), bf16[2,32,32,1,256]{4,2,0,3,1:T(8,128)(2,1)S(1)}, u32[]{:S(2)}, u32[]{:S(2)}) async-start(bf16[2,32,32,1,256]{4,2,0,3,1:T(8,128)(2,1)} %copy.151), calls=%async_computation.5 | async-start | bytes 2097152 | tf_op jit(solution)/shard_map/all_to_all | solution.py:294
  1603.5 46.8 %all-to-all-start.7 = ((bf16[2,32,32,1,256]{4,2,0,3,1:T(8,128)(2,1)}), bf16[2,32,32,1,256]{4,2,0,3,1:T(8,128)(2,1)S(1)}, u32[]{:S(2)}, u32[]{:S(2)}) async-start(bf16[2,32,32,1,256]{4,2,0,3,1:T(8,128)(2,1)} %copy.157), calls=%async_computation.9 | async-start | bytes 2097152 | tf_op jit(solution)/shard_map/all_to_all | solution.py:300
  1608.1 304.4 %reduce-scatter.18.cloned.1.call-start = ((), (), s32[]{:S(2)}) async-start(), calls=%async_computation.23 | async-start | bytes 4325376 | tf_op jit(solution)/shard_map/reduce_scatter | solution.py:338
  1666.9 394.8 %reduce-scatter.16.cloned.1.call-start = ((), (), s32[]{:S(2)}) async-start(), calls=%async_computation.22 | async-start | bytes 4325376 | tf_op jit(solution)/shard_map/reduce_scatter | solution.py:337
  1671.5 540.0 %reduce-scatter.14.cloned.1.call-start = ((), (), s32[]{:S(2)}) async-start(), calls=%async_computation.21 | async-start | bytes 4325376 | tf_op jit(solution)/shard_map/reduce_scatter | solution.py:336
  1674.9 901.7 %reduce-scatter.22.cloned.1.call-start = ((), (), s32[]{:S(2)}) async-start(), calls=%async_computation.25 | async-start | bytes 17301504 | tf_op jit(solution)/shard_map/reduce_scatter | solution.py:340
  1685.5 1256.0 %reduce-scatter.24.cloned.1.call-start = ((), (), s32[]{:S(2)}) async-start(), calls=%async_computation.26 | async-start | bytes 17301504 | tf_op jit(solution)/shard_map/reduce_scatter | solution.py:341
  1701.8 1490.1 %reduce-scatter.26.cloned.1.call-start = ((), (), s32[]{:S(2)}) async-start(), calls=%async_computation.27 | async-start | bytes 25952256 | tf_op jit(solution)/shard_map/reduce_scatter | solution.py:334
  1716.0 1476.0 %copy-start.1 = (bf16[1024,1024]{1,0:T(8,128)(2,1)S(1)}, bf16[1024,1024]{1,0:T(8,128)(2,1)}, u32[]{:S(2)}) copy-start(bf16[1024,1024]{1,0:T(8,128)(2,1)} %param.29) | copy-start | bytes 6291460
  (44 other events, 143.9 us)
Sparse Core Ops, SparseCore 0:
  133.7 53.4 all-gather.4
  189.1 54.3 all-gather.2
  1343.1 183.0 reduce-scatter.9
  1529.9 71.2 reduce-scatter.11
  1603.9 159.2 reduce-scatter.19
  1765.9 146.5 reduce-scatter.17
  1915.4 146.2 reduce-scatter.15
  2064.5 146.8 reduce-scatter.13
  2214.4 362.1 reduce-scatter.21
  2579.3 362.1 reduce-scatter.23
  2948.5 243.3 reduce-scatter.25
where the time goes:
time: 3210 us; the launch traced here: 3200 us
  waiting for transfers between devices  1770 us (55%)
  matrix products  765 us (24%)
  local copies, waits for them, and re-layouts  293 us (9%)
  other arithmetic  151 us (5%)
  loops' own time  118 us (4%)
  blocking collectives  60.1 us (2%)
    reduce_scatter x1, waiting for transfers between devices, shards(): lax.psum_scatter(grad_up, ('frames', 'rows'), scatter_dimension=0, tiled=...  365 us
    reduce_scatter x1, waiting for transfers between devices, shards(): lax.psum_scatter(grad_down, ('frames', 'rows'), scatter_dimension=0, tile...  365 us
    reduce_scatter x1, waiting for transfers between devices, shards(): lax.psum_scatter(full_mod, ('frames', 'rows'), scatter_dimension=0, tiled...  250 us
    dot_general x14, matrix products, slot_scores(): jnp.einsum('cqhd,ckhd->chqk', query_local, fetch(keys_all, slot), preferr...  203 us
    reduce_scatter x1, waiting for transfers between devices, shards(): lax.psum_scatter(key_terms.astype(jnp.bfloat16), 'frames', scatter_dimens...  176 us
    reduce_scatter x1, waiting for transfers between devices, shards(): lax.psum_scatter(grad_query, ('frames', 'rows'), scatter_dimension=0, til...  150 us
    reduce_scatter x1, waiting for transfers between devices, shards(): lax.psum_scatter(grad_value, ('frames', 'rows'), scatter_dimension=0, til...  149 us
    reduce_scatter x1, waiting for transfers between devices, shards(): lax.psum_scatter(grad_key, ('frames', 'rows'), scatter_dimension=0, tiled...  149 us
  transfers between devices with their start and end apart: 17, of which 14 were waited for; matrix products, arithmetic and copies ran while one was open for 12% of the time, Pallas kernels for 0%

commit v1 on v0

v1 whole, which is shorter than its diff:
```python
import functools
import math

import jax
import jax.numpy as jnp
from jax import lax
from jax.experimental import pallas as pl
from jax.experimental.pallas import tpu as pltpu
from jax.sharding import Mesh, PartitionSpec as P

D = 1024
H = 16
HD = 64
FF = 4096
PR = 32
PC = 32

norm_eps = 1e-06
LOW = jnp.bfloat16
WIDE = jnp.float32
MIB = 2**20
SCALE2 = math.log2(math.e) / math.sqrt(HD)
SAFE_LOG2 = 100.0
ROWS_ROWS = (((1,), (1,)), ((), ()))
ROWS_COLS = (((1,), (0,)), ((), ()))
SHIFT_ONE, SCALE_ONE, GATE_ONE, SHIFT_TWO, SCALE_TWO, GATE_TWO = range(6)


def dot(left, right, dims=ROWS_COLS):
    return lax.dot_general(left, right, dims, preferred_element_type=WIDE)


def exact_dot(left, right, dims=ROWS_COLS):
    return lax.dot_general(
        left, right, dims, preferred_element_type=WIDE, precision=lax.Precision.HIGHEST
    )


def vmem():
    return pl.BlockSpec(memory_space=pltpu.VMEM)


def smem():
    return pl.BlockSpec(memory_space=pltpu.SMEM)


def whole(shape):
    return pl.BlockSpec(shape, lambda *unused: (0,) * len(shape))


def column_sum(values):
    return jnp.sum(values, axis=0, keepdims=True)


def head_masks(rows, lanes, heads):
    lane = lax.broadcasted_iota(jnp.int32, (rows, lanes), 1)
    return [lane // HD == h for h in range(heads)]


def square_norm(values, masks):
    squared = values.astype(WIDE)
    squared = squared * squared
    return [
        jnp.max(jnp.sum(jnp.where(mask, squared, 0.0), axis=1, keepdims=True)) for mask in masks
    ]


def forward_kernel(order, flag_in, query, pair, *refs, first, last, heads):
    frames, tokens, lanes = query.shape
    if not first:
        num_in, sum_in, top_in = refs[:3]
        refs = refs[3:]
    if last:
        attn_out, log_out, keys, values = refs
    else:
        flag_out, num_out, sum_out, top_out, keys, values = refs
    masks = head_masks(tokens, lanes, heads)
    one = jnp.ones((tokens, lanes), LOW)
    zero = jnp.zeros((tokens, lanes), LOW)
    width = 2 * HD
    bound = jnp.float32(0.0)
    q_top = [jnp.float32(0.0)] * heads
    k_top = [jnp.float32(0.0)] * heads
    for f in range(frames):
        k = pair[f, 0]
        v = pair[f, 1]
        q_top = [jnp.maximum(a, b) for a, b in zip(q_top, square_norm(query[f], masks))]
        k_top = [jnp.maximum(a, b) for a, b in zip(k_top, square_norm(k, masks))]
        for h in range(heads):
            keys[h, f] = jnp.where(masks[h], k, zero)
            if heads == 2:
                values[h, f] = jnp.where(masks[h], v, one)
            else:
                values[h, f] = jnp.concatenate([v, one], axis=1)
    for a, b in zip(q_top, k_top):
        bound = jnp.maximum(bound, a * b)
    fast = bound * (SCALE2 * SCALE2) <= SAFE_LOG2 * SAFE_LOG2
    if not first:
        fast = jnp.logical_and(fast, flag_in[0] == 1)
    if not last:
        flag_out[0] = jnp.where(fast, 1, 0).astype(jnp.int32)
    low_lane = lax.broadcasted_iota(jnp.int32, (tokens, lanes), 1) < HD
    pick = lax.broadcasted_iota(jnp.int32, (8, lanes), 1) == HD * lax.broadcasted_iota(
        jnp.int32, (8, lanes), 0
    )
    pick = jnp.where(pick, 1.0, 0.0).astype(WIDE)

    def split(num, total):
        if heads == 2:
            turned = pltpu.roll(total, HD, 1)
            return [jnp.where(low_lane, num, turned), jnp.where(low_lane, turned, num)]
        return [jnp.concatenate([num, total], axis=1)]

    def join(accs):
        if heads == 2:
            num = jnp.where(low_lane, accs[0], accs[1])
            total = jnp.where(low_lane, accs[1], accs[0])
            return num, pltpu.roll(total, HD, 1)
        return accs[0][:, :HD], accs[0][:, HD:]

    def start(slot):
        if first:
            return [jnp.zeros((tokens, width), WIDE) for _ in range(heads)]
        return split(num_in[slot], sum_in[slot])

    def store(slot, accs, top):
        num, total = join(accs)
        if last:
            attn_out[slot] = (num / total).astype(LOW)
            logs = jnp.log2(total)
            if top is not None:
                logs = logs + top
            log_out[slot] = exact_dot(pick, logs, ROWS_ROWS)
        else:
            num_out[slot] = num
            sum_out[slot] = total
            top_out[slot] = jnp.zeros((tokens, lanes), WIDE) if top is None else top

    @pl.when(fast)
    def _():
        def outer(t, unused):
            slot = order[t]
            q = query[slot]

            def inner(j, accs):
                other = order[j]
                new = []
                for h in range(heads):
                    s = dot(q, keys[h, other], ROWS_ROWS)
                    p = jnp.exp2(s * SCALE2).astype(LOW)
                    new.append(accs[h] + dot(p, values[h, other]))
                return new

            store(slot, lax.fori_loop(0, t + 1, inner, start(slot)), None)
            return unused

        lax.fori_loop(0, frames, outer, 0)

    @pl.when(jnp.logical_not(fast))
    def _():
        def outer(t, unused):
            slot = order[t]
            q = query[slot]

            def inner(j, state):
                other = order[j]
                accs, tops = state
                new_accs, new_tops = [], []
                for h in range(heads):
                    s = dot(q, keys[h, other], ROWS_ROWS) * SCALE2
                    top = jnp.maximum(tops[h], jnp.max(s, axis=1, keepdims=True))
                    p = jnp.exp2(s - top).astype(LOW)
                    keep = jnp.exp2(tops[h] - top)
                    new_accs.append(accs[h] * keep + dot(p, values[h, other]))
                    new_tops.append(top)
                return new_accs, new_tops

            if first:
                tops = [jnp.full((tokens, 1), -1e30, WIDE)] * heads
            else:
                tops = [top_in[slot][:, h * HD : h * HD + 1] for h in range(heads)]
            accs, tops = lax.fori_loop(0, t + 1, inner, (start(slot), tops))
            top = jnp.broadcast_to(tops[0], (tokens, lanes))
            if heads == 2:
                top = jnp.where(low_lane, top, jnp.broadcast_to(tops[1], (tokens, lanes)))
            store(slot, accs, top)
            return unused

        lax.fori_loop(0, frames, outer, 0)


def attention_forward(order, state, query, pair, last):
    frames, tokens, lanes = query.shape
    heads = lanes // HD
    first = state is None
    wide = jax.ShapeDtypeStruct(query.shape, WIDE)
    if last:
        out_shape = [
            jax.ShapeDtypeStruct(query.shape, LOW),
            jax.ShapeDtypeStruct((frames, 8, tokens), WIDE),
        ]
        out_specs = [vmem()] * 2
    else:
        out_shape = [jax.ShapeDtypeStruct((1,), jnp.int32), wide, wide, wide]
        out_specs = [smem()] + [vmem()] * 3
    flag = jnp.zeros((1,), jnp.int32) if first else state[0]
    rest = () if first else tuple(state[1:])
    pairs = heads * frames * (frames + 1) // 2 * tokens * tokens
    return pl.pallas_call(
        functools.partial(forward_kernel, first=first, last=last, heads=heads),
        out_shape=out_shape,
        in_specs=[smem(), smem()] + [vmem()] * (2 + len(rest)),
        out_specs=out_specs,
        scratch_shapes=[
            pltpu.VMEM((heads, frames, tokens, lanes), LOW),
            pltpu.VMEM((heads, frames, tokens, max(lanes, 2 * HD)), LOW),
        ],
        compiler_params=pltpu.CompilerParams(vmem_limit_bytes=56 * MIB),
        cost_estimate=pl.CostEstimate(
            flops=pairs * 4 * HD * 8, bytes_accessed=16 * MIB, transcendentals=pairs
        ),
        name="attention_forward",
    )(order, flag, query, pair, *rest)


def backward_kernel(
    order, query, pair, grad, out, lse, *refs, first, last, begin, end, came, heads
):
    frames, tokens, lanes = query.shape
    if not first:
        dq_in = refs[0]
        refs = refs[1:]
    if begin > 0:
        pair_in = refs[0]
        refs = refs[1:]
    if came:
        pair_came = refs[0]
        refs = refs[1:]
    if last:
        final, queries, grads, delta, key_turned, dq_sum = refs
        places = (1, 2)
    else:
        dq_sum, final, queries, grads, delta, key_turned = refs
        places = (0, 1)
    masks = head_masks(tokens, lanes, heads)
    zero = jnp.zeros((tokens, lanes), LOW)
    lane8 = lax.broadcasted_iota(jnp.int32, (8, lanes), 1) // HD
    pick = jnp.where(lane8 == lax.broadcasted_iota(jnp.int32, (8, lanes), 0), 1.0, 0.0)
    for f in range(frames):
        q = query[f]
        g = grad[f]
        for h in range(heads):
            queries[h, f] = jnp.where(masks[h], q, zero)
            grads[h, f] = jnp.where(masks[h], g, zero)
        key_turned[f] = pair[f, 0].T
        delta[f] = exact_dot(
            pick.astype(WIDE), g.astype(WIDE) * out[f].astype(WIDE), ROWS_ROWS
        )
        dq_sum[f] = jnp.zeros((lanes, tokens), WIDE) if first else dq_in[f]
        if begin > 0:
            for i in range(2):
                old = pair_in[f, i]
                if came:
                    old = (old.astype(WIDE) + pair_came[f, i].astype(WIDE)).astype(LOW)
                final[f, places[i]] = old

    def outer(t, unused):
        slot = order[t]
        k = pair[slot, 0]
        v = pair[slot, 1]
        ks = [jnp.where(mask, k, zero) for mask in masks]
        vs = [jnp.where(mask, v, zero) for mask in masks]

        def inner(j, carry):
            other = order[j]
            dk, dv = carry
            for h in range(heads):
                q = queries[h, other]
                g = grads[h, other]
                s = dot(ks[h], q, ROWS_ROWS)
                p = jnp.exp2(s * SCALE2 - lse[other, h : h + 1, :])
                dp = dot(vs[h], g, ROWS_ROWS)
                ds = (p * (dp - delta[other, h : h + 1, :])).astype(LOW)
                dv = dv + dot(p.astype(LOW), g)
                dk = dk + dot(ds, q)
                span = slice(h * HD, (h + 1) * HD)
                dq_sum[other, span, :] += dot(key_turned[slot, span, :], ds)
            return dk, dv

        start = jnp.zeros((tokens, lanes), WIDE)
        dk, dv = lax.fori_loop(t, frames, inner, (start, start))
        dk = dk * (1.0 / math.sqrt(HD))
        if came:
            dk = dk + pair_came[slot, 0].astype(WIDE)
            dv = dv + pair_came[slot, 1].astype(WIDE)
        final[slot, places[0]] = dk.astype(LOW)
        final[slot, places[1]] = dv.astype(LOW)
        return unused

    lax.fori_loop(begin, end, outer, 0)
    if last:
        for f in range(frames):
            final[f, 0] = (dq_sum[f].T * (1.0 / math.sqrt(HD))).astype(LOW)


def attention_backward(order, dq, partial, came, query, pair, grad, out, lse, begin, end, last):
    frames, tokens, lanes = query.shape
    heads = lanes // HD
    first = dq is None
    sums = (frames, lanes, tokens)
    extra = tuple(
        array for array in (dq, partial if begin > 0 else None, came) if array is not None
    )
    steps = sum(frames - t for t in range(begin, end))
    work = heads * steps * tokens * tokens
    scratch = [
        pltpu.VMEM((heads, frames, tokens, lanes), LOW),
        pltpu.VMEM((heads, frames, tokens, lanes), LOW),
        pltpu.VMEM((frames, 8, tokens), WIDE),
        pltpu.VMEM((frames, lanes, tokens), LOW),
    ]
    if last:
        out_shape = [jax.ShapeDtypeStruct((frames, 3, tokens, lanes), LOW)]
        scratch.append(pltpu.VMEM(sums, WIDE))
    else:
        out_shape = [
            jax.ShapeDtypeStruct(sums, WIDE), jax.ShapeDtypeStruct((frames, 2, tokens, lanes), LOW)
        ]
    return pl.pallas_call(
        functools.partial(
            backward_kernel, first=first, last=last, begin=begin, end=end,
            came=came is not None, heads=heads,
        ),
        out_shape=out_shape,
        in_specs=[smem()] + [vmem()] * (5 + len(extra)),
        out_specs=[vmem()] * len(out_shape),
        scratch_shapes=scratch,
        compiler_params=pltpu.CompilerParams(vmem_limit_bytes=56 * MIB),
        cost_estimate=pl.CostEstimate(
            flops=work * 10 * HD * 5, bytes_accessed=16 * MIB, transcendentals=work
        ),
        name="attention_backward",
    )(order, query, pair, grad, out, lse, *extra)


def normalize(values):
    centered = values - jnp.mean(values, axis=-1, keepdims=True)
    inverse = lax.rsqrt(jnp.mean(centered * centered, axis=-1, keepdims=True) + norm_eps)
    return (centered * inverse, inverse)


def norm_backward(grad_normed, normed, inverse):
    mean_grad = jnp.mean(grad_normed, axis=-1, keepdims=True)
    mean_prod = jnp.mean(grad_normed * normed, axis=-1, keepdims=True)
    return inverse * (grad_normed - mean_grad - normed * mean_prod)


def part(mod, index):
    return mod[0:1, index * D : (index + 1) * D]


def swap_halves(values):
    lanes = values.shape[1]
    lane = lax.broadcasted_iota(jnp.int32, values.shape, 1) % HD
    eight, twelve = HD // 8, 3 * HD // 16
    quarter, last = HD // 4, HD // 4 + 2 * twelve

    def ahead(step):
        return pltpu.roll(values, lanes - step, 1)

    def behind(step):
        return pltpu.roll(values, step, 1)

    first_half = ((lane >= quarter) & (lane < quarter + twelve)) | (
        (lane >= last) & (lane < last + twelve)
    )
    short = jnp.where(lane < eight, ahead(eight), behind(eight))
    long = jnp.where(first_half, ahead(twelve), behind(twelve))
    return jnp.where(lane < quarter, short, long)


def turned(values, cosine, sine):
    wide = cosine.shape[1]
    pieces = []
    for at in range(0, values.shape[1], wide):
        block = values[:, at : at + wide]
        pieces.append(block * cosine + swap_halves(block) * sine)
    return pieces[0] if len(pieces) == 1 else jnp.concatenate(pieces, axis=1)


def input_kernel(tokens, mod, w_query, w_key, w_value, cosine, sine, hidden, query, pair):
    @pl.when(pl.program_id(0) == 0)
    def _():
        normed, unused = normalize(tokens[...].astype(WIDE))
        hidden[...] = (normed * (1.0 + part(mod, SCALE_ONE)) + part(mod, SHIFT_ONE)).astype(LOW)

    groups, unused, lanes = query.shape
    h = hidden[...]
    cos, sin = cosine[...], sine[...]
    k = turned(dot(h, w_key[...]), cos, sin).astype(LOW)
    v = dot(h, w_value[...]).astype(LOW)
    q = turned(dot(h, w_query[...]), cos, sin).astype(LOW)
    for g in range(groups):
        span = slice(g * lanes, (g + 1) * lanes)
        pair[g, 0] = k[:, span]
        pair[g, 1] = v[:, span]
        query[g] = q[:, span]


def input_projections(tokens, mod, w_query, w_key, w_value, cosine, sine, frames):
    count = tokens.shape[0]
    lanes = D // frames
    wide = 256
    groups = wide // lanes
    weight = pl.BlockSpec((D, wide), lambda c: (0, c))
    heads = pl.BlockSpec((groups, count, lanes), lambda c: (c, 0, 0))
    pairs = pl.BlockSpec((groups, 2, count, lanes), lambda c: (c, 0, 0, 0))
    return pl.pallas_call(
        input_kernel,
        grid=(D // wide,),
        out_shape=[
            jax.ShapeDtypeStruct((count, D), LOW),
            jax.ShapeDtypeStruct((frames, count, lanes), LOW),
            jax.ShapeDtypeStruct((frames, 2, count, lanes), LOW),
        ],
        in_specs=[whole((count, D)), whole((1, 6 * D)), weight, weight, weight]
        + [whole(cosine.shape)] * 2,
        out_specs=[whole((count, D)), heads, pairs],
        compiler_params=pltpu.CompilerParams(vmem_limit_bytes=48 * MIB),
        cost_estimate=pl.CostEstimate(
            flops=6 * count * D * D, bytes_accessed=12 * MIB, transcendentals=0
        ),
        name="input_projections",
    )(tokens, mod, w_query, w_key, w_value, cosine, sine)


def pull_kernel(cotangent, mod, w_down, pulled, scaled_turned, scaled):
    @pl.when(pl.program_id(0) == 0)
    def _():
        scaled[...] = (part(mod, GATE_TWO) * cotangent[...].astype(WIDE)).astype(LOW)
        scaled_turned[...] = scaled[...].T

    pulled[...] = dot(scaled[...], w_down[...], ROWS_ROWS).astype(LOW)


def pull_down(cotangent, mod, w_down):
    count = cotangent.shape[0]
    wide = 512
    return pl.pallas_call(
        pull_kernel,
        grid=(FF // wide,),
        out_shape=[
            jax.ShapeDtypeStruct((count, FF), LOW), jax.ShapeDtypeStruct((D, count), LOW)
        ],
        in_specs=[
            whole((count, D)), whole((1, 6 * D)), pl.BlockSpec((wide, D), lambda c: (c, 0))
        ],
        out_specs=[pl.BlockSpec((count, wide), lambda c: (0, c)), whole((D, count))],
        scratch_shapes=[pltpu.VMEM((count, D), LOW)],
        compiler_params=pltpu.CompilerParams(vmem_limit_bytes=32 * MIB),
        cost_estimate=pl.CostEstimate(
            flops=2 * count * D * FF, bytes_accessed=14 * MIB, transcendentals=0
        ),
        name="pull_down",
    )(cotangent, mod, w_down)


def middle_kernel(
    attn, tokens, cotangent, mod, w_proj, w_up, pulled,
    middle, hidden, active, grad_up_in, grad_middle, grad_branch, grad_attn,
    grad_gate, grad_shift, grad_scale, branch, normed, inverse, total
):
    step = pl.program_id(0)
    frames, count, lanes = attn.shape

    @pl.when(step == 0)
    def _():
        for f in range(frames):
            hidden[:, f * lanes : (f + 1) * lanes] = attn[f]
        product = dot(hidden[...], w_proj[...])
        branch[...] = product
        mid = tokens[...].astype(WIDE) + part(mod, GATE_ONE) * product
        middle[...] = mid
        n, inv = normalize(mid)
        normed[...] = n
        inverse[...] = inv
        hidden[...] = (n * (1.0 + part(mod, SCALE_TWO)) + part(mod, SHIFT_TWO)).astype(LOW)
        total[...] = jnp.zeros(total.shape, WIDE)

    weight = w_up[...]
    u = dot(hidden[...], weight)
    rate = math.sqrt(2.0 / math.pi)
    square = u * u
    bend = jnp.tanh(rate * (u + 0.044715 * (u * square)))
    half = 0.5 * (1.0 + bend)
    active[...] = (u * half).astype(LOW)
    slope = half + (0.5 * rate) * u * (1.0 - bend * bend) * (1.0 + (3 * 0.044715) * square)
    du = (pulled[...].astype(WIDE) * slope).astype(LOW)
    grad_up_in[...] = du
    total[...] += dot(du, weight, ROWS_ROWS)

    @pl.when(step == pl.num_programs(0) - 1)
    def _():
        dh = total[...]
        n = normed[...]
        grad_scale[...] = column_sum(dh * n)
        grad_shift[...] = column_sum(dh)
        dx = cotangent[...].astype(WIDE) + norm_backward(
            dh * (1.0 + part(mod, SCALE_TWO)), n, inverse[...]
        )
        grad_middle[...] = dx
        grad_gate[...] = column_sum(dx * branch[...])
        dy = (part(mod, GATE_ONE) * dx).astype(LOW)
        grad_branch[...] = dy
        back = dot(dy, w_proj[...], ROWS_ROWS).astype(LOW)
        for f in range(frames):
            grad_attn[f] = back[:, f * lanes : (f + 1) * lanes]


def middle_block(attn, tokens, cotangent, mod, w_proj, w_up, pulled):
    frames, count, lanes = attn.shape
    wide = 512
    flat = whole((count, D))
    row = whole((1, D))
    columns = pl.BlockSpec((count, wide), lambda c: (0, c))
    heads = whole(attn.shape)

    def of(shape, kind):
        return jax.ShapeDtypeStruct(shape, kind)

    return pl.pallas_call(
        middle_kernel,
        grid=(FF // wide,),
        out_shape=[
            of((count, D), WIDE), of((count, D), LOW), of((count, FF), LOW), of((count, FF), LOW),
            of((count, D), WIDE), of((count, D), LOW), of(attn.shape, LOW),
            of((1, D), WIDE), of((1, D), WIDE), of((1, D), WIDE),
        ],
        in_specs=[
            heads, flat, flat, whole((1, 6 * D)), whole((D, D)),
            pl.BlockSpec((D, wide), lambda c: (0, c)), columns,
        ],
        out_specs=[flat, flat, columns, columns, flat, flat, heads, row, row, row],
        scratch_shapes=[
            pltpu.VMEM((count, D), WIDE), pltpu.VMEM((count, D), WIDE),
            pltpu.VMEM((count, 1), WIDE), pltpu.VMEM((count, D), WIDE),
        ],
        compiler_params=pltpu.CompilerParams(vmem_limit_bytes=56 * MIB),
        cost_estimate=pl.CostEstimate(
            flops=2 * count * D * (2 * FF + 2 * D), bytes_accessed=30 * MIB,
            transcendentals=count * FF,
        ),
        name="middle_block",
    )(attn, tokens, cotangent, mod, w_proj, w_up, pulled)


def weights_kernel(
    slot, active, grad_up_in, hidden, scaled_turned, attn, grad_branch, *refs, keep
):
    step = pl.program_id(0)
    frames, count, lanes = attn.shape
    half = frames // 2
    wide = D // frames
    if keep:
        activity, middle, cotangent, mod, w_down = refs[:5]
        out, grad_gate, down_out, up_out, hidden_turned, attn_turned, flat, total = refs[5:]
    else:
        down_out, up_out, hidden_turned, attn_turned, flat = refs
    chunks, narrow = down_out.shape[1], down_out.shape[3]

    @pl.when(step == 0)
    def _():
        for f in range(frames):
            flat[:, f * lanes : (f + 1) * lanes] = attn[f]
        for f in range(frames):
            place = lax.bitwise_xor(f, slot[0])

            @pl.when(place % 2 == (0 if keep else 1))
            def _():
                span = slice(f * wide, (f + 1) * wide)
                hidden_turned[place // 2] = hidden[:, span].T
                attn_turned[place // 2] = flat[:, span].T

        if keep:
            total[...] = jnp.zeros(total.shape, WIDE)

    @pl.when(step < half)
    def _():
        if keep:
            total[...] += dot(activity[...], w_down[...])
        down = dot(scaled_turned[...], active[...]).astype(LOW)
        for r in range(chunks):
            down_out[0, r] = down[:, r * narrow : (r + 1) * narrow]
        up = dot(hidden_turned[...].reshape(D // 2, count), grad_up_in[...]).astype(LOW)
        up_out[...] = up.reshape(half, wide, up.shape[1])

    @pl.when(step >= half)
    def _():
        proj = dot(attn_turned[...].reshape(D // 2, count), grad_branch[...]).astype(LOW)
        up_out[...] = proj.reshape(half, wide, proj.shape[1])

    if keep:
        @pl.when(step == half - 1)
        def _():
            z = total[...]
            out[...] = (middle[...] + part(mod, GATE_TWO) * z).astype(LOW)
            grad_gate[...] = column_sum(cotangent[...].astype(WIDE) * z)


def weight_gradients(
    slot, active, grad_up_in, hidden, scaled_turned, attn, grad_branch, rows, finish
):
    frames, count, lanes = attn.shape
    keep = finish is not None
    half = frames // 2
    narrow = FF // frames
    wide = FF // half
    extra = D // wide

    def down_block(i, slot):
        place = 2 * jnp.minimum(i, half - 1) + (0 if keep else 1)
        return lax.bitwise_xor(place, slot[0])

    def up_block(i, slot):
        return jnp.minimum(i, half - 1)

    flat = whole((count, D))
    down = (1, rows, D, narrow // rows)
    in_specs = [
        pl.BlockSpec((count, narrow), lambda i, slot: (0, down_block(i, slot))),
        pl.BlockSpec((count, wide), lambda i, slot: (0, up_block(i, slot))),
        flat, whole((D, count)), whole(attn.shape),
        pl.BlockSpec((count, wide), lambda i, slot: (0, jnp.maximum(i - half, 0))),
    ]
    out_specs = [
        pl.BlockSpec(down, lambda i, slot: (jnp.minimum(i, half - 1), 0, 0, 0)),
        pl.BlockSpec((half, D // frames, wide), lambda i, slot: (0, 0, i)),
    ]
    out_shape = [
        jax.ShapeDtypeStruct((half, rows, D, narrow // rows), LOW),
        jax.ShapeDtypeStruct((half, D // frames, FF + D), LOW),
    ]
    scratch = [
        pltpu.VMEM((half, D // frames, count), LOW), pltpu.VMEM((half, D // frames, count), LOW),
        pltpu.VMEM((count, D), LOW),
    ]
    args = (slot, active, grad_up_in, hidden, scaled_turned, attn, grad_branch)
    if keep:
        args += (active,) + tuple(finish)
        in_specs += [
            pl.BlockSpec((count, wide), lambda i, slot: (0, up_block(i, slot))),
            flat, flat, whole((1, 6 * D)),
            pl.BlockSpec((wide, D), lambda i, slot: (up_block(i, slot), 0)),
        ]
        out_specs = [flat, whole((1, D))] + out_specs
        out_shape = [
            jax.ShapeDtypeStruct((count, D), LOW), jax.ShapeDtypeStruct((1, D), WIDE)
        ] + out_shape
        scratch.append(pltpu.VMEM((count, D), WIDE))
    return pl.pallas_call(
        functools.partial(weights_kernel, keep=keep),
        grid_spec=pltpu.PrefetchScalarGridSpec(
            num_scalar_prefetch=1, grid=(half + extra,),
            in_specs=in_specs, out_specs=out_specs, scratch_shapes=scratch,
        ),
        out_shape=out_shape,
        compiler_params=pltpu.CompilerParams(vmem_limit_bytes=56 * MIB),
        cost_estimate=pl.CostEstimate(
            flops=count * D * (2 * FF + D + (2 * FF if keep else 0)), bytes_accessed=24 * MIB,
            transcendentals=0,
        ),
        name="weight_gradients",
    )(*args)


def turn_kernel(hidden, target):
    target[...] = hidden[...].T


def turn_hidden(hidden):
    return pl.pallas_call(
        turn_kernel,
        out_shape=jax.ShapeDtypeStruct(hidden.shape[::-1], LOW),
        in_specs=[vmem()],
        out_specs=vmem(),
        compiler_params=pltpu.CompilerParams(vmem_limit_bytes=32 * MIB),
        cost_estimate=pl.CostEstimate(flops=0, bytes_accessed=2 * MIB, transcendentals=0),
        name="turn_hidden",
    )(hidden)


def head_kernel(grads, hidden, cosine, sine, time_cosine, time_sine, product, total):
    step = pl.program_id(0)

    @pl.when(step == 0)
    def _():
        total[...] = jnp.zeros(total.shape, WIDE)

    cos = cosine[...] + time_cosine[0]
    sin = -(sine[...] + time_sine[0])
    block = jnp.concatenate(
        [turned(grads[0, i].astype(WIDE), cos, sin).astype(LOW) for i in range(2)] + [grads[0, 2]],
        axis=1,
    )
    total[...] += dot(hidden[0], block)

    @pl.when(step == pl.num_programs(0) - 1)
    def _():
        product[...] = total[...].astype(LOW)


def head_gradients(grads, hidden_all, tables):
    frames, unused, count, lanes = grads.shape
    frame = pl.BlockSpec((1, 1, lanes), lambda f: (f, 0, 0))
    return pl.pallas_call(
        head_kernel,
        grid=(frames,),
        out_shape=jax.ShapeDtypeStruct((D, 3 * lanes), LOW),
        in_specs=[
            pl.BlockSpec((1, 3, count, lanes), lambda f: (f, 0, 0, 0)),
            pl.BlockSpec((1, D, count), lambda f: (f, 0, 0)),
            whole((count, lanes)), whole((count, lanes)), frame, frame,
        ],
        out_specs=whole((D, 3 * lanes)),
        scratch_shapes=[pltpu.VMEM((D, 3 * lanes), WIDE)],
        compiler_params=pltpu.CompilerParams(vmem_limit_bytes=32 * MIB),
        cost_estimate=pl.CostEstimate(
            flops=6 * frames * count * D * lanes, bytes_accessed=12 * MIB, transcendentals=0
        ),
        name="head_gradients",
    )(grads, hidden_all, *tables)


def output_kernel(
    grads, w_query, w_key, w_value, cosine, sine, tokens, mod, grad_middle,
    grad_tokens, grad_shift, grad_scale, total
):
    step = pl.program_id(0)
    groups = grads.shape[0]

    @pl.when(step == 0)
    def _():
        total[...] = jnp.zeros(total.shape, WIDE)

    dh = total[...]
    for i, weight in enumerate((w_query, w_key, w_value)):
        block = jnp.concatenate([grads[g, i] for g in range(groups)], axis=1)
        if i < 2:
            block = turned(block.astype(WIDE), cosine[...], -sine[...]).astype(LOW)
        dh = dh + dot(block, weight[...], ROWS_ROWS)
    total[...] = dh

    @pl.when(step == pl.num_programs(0) - 1)
    def _():
        dh = total[...]
        n, inverse = normalize(tokens[...].astype(WIDE))
        grad_scale[...] = column_sum(dh * n)
        grad_shift[...] = column_sum(dh)
        grad_tokens[...] = (
            grad_middle[...] + norm_backward(dh * (1.0 + part(mod, SCALE_ONE)), n, inverse)
        ).astype(LOW)


def input_gradients(grads, w_query, w_key, w_value, cosine, sine, tokens, mod, grad_middle):
    frames, unused, count, lanes = grads.shape
    wide = 256
    groups = wide // lanes
    flat = whole((count, D))
    row = whole((1, D))
    weight = pl.BlockSpec((D, wide), lambda c: (0, c))
    rows = jax.ShapeDtypeStruct((1, D), WIDE)
    return pl.pallas_call(
        output_kernel,
        grid=(D // wide,),
        out_shape=[jax.ShapeDtypeStruct((count, D), LOW), rows, rows],
        in_specs=[
            pl.BlockSpec((groups, 3, count, lanes), lambda c: (c, 0, 0, 0)),
            weight, weight, weight, whole(cosine.shape), whole(sine.shape),
            flat, whole((1, 6 * D)), flat,
        ],
        out_specs=[flat, row, row],
        scratch_shapes=[pltpu.VMEM((count, D), WIDE)],
        compiler_params=pltpu.CompilerParams(vmem_limit_bytes=48 * MIB),
        cost_estimate=pl.CostEstimate(
            flops=6 * count * D * D, bytes_accessed=14 * MIB, transcendentals=0
        ),
        name="input_gradients",
    )(grads, w_query, w_key, w_value, cosine, sine, tokens, mod, grad_middle)


def sinusoid(levels):
    half_size = D // 2
    freq_table = 10000.0 ** (-jnp.arange(half_size, dtype=WIDE) / half_size)
    angle_table = levels.astype(WIDE)[..., None] * freq_table
    return jnp.concatenate([jnp.cos(angle_table), jnp.sin(angle_table)], axis=-1)


def turn_tables(positions, heads):
    count = next(position.shape[0] for position in positions if position is not None)
    cosines, sines = [], []
    for position, part_size in zip(positions, (HD // 4, 3 * HD // 8, 3 * HD // 8)):
        half_size = part_size // 2
        if position is None:
            cosine = sine = jnp.zeros((count, half_size), WIDE)
        else:
            freq_table = 10000.0 ** (-jnp.arange(half_size, dtype=WIDE) / half_size)
            angle_table = position[:, None] * freq_table
            cosine = jnp.cos(angle_table)
            sine = jnp.sin(angle_table)
        cosines += [cosine, cosine]
        sines += [-sine, sine]
    return (
        jnp.concatenate(cosines * heads, axis=-1),
        jnp.concatenate(sines * heads, axis=-1),
    )


def shards(
    block_in, block_map, noise_level, w_query, w_key, w_value, w_proj, w_up, w_down, w_mod, cotangent
):
    frames = lax.axis_size("frames")
    sides = lax.axis_size("side")
    row_total = lax.axis_size("half") * sides
    frame_slot = lax.axis_index("frames")
    half = lax.axis_index("half")
    side = lax.axis_index("side")
    across = ("half", "side")
    everyone = ("frames",) + across
    devices = frames * row_total
    clips = block_in.shape[1]
    local_rows = block_in.shape[2]
    lanes = D // frames
    heads = max(lanes // HD, 1)
    order = jnp.argsort(block_map).astype(jnp.int32)
    slot = frame_slot.astype(jnp.int32).reshape(1)

    def tie(*arrays):
        return lax.optimization_barrier(arrays)

    def clip_tokens(tokens, clip):
        return lax.dynamic_index_in_dim(tokens[0], clip, 0, keepdims=False).reshape(-1, D)

    def other_half(array):
        return lax.ppermute(array, "half", [(0, 1), (1, 0)])

    def return_clip(own, came, kind):
        first = jnp.where(half == 0, own, came).astype(kind)
        second = jnp.where(half == 0, came, own).astype(kind)
        return jnp.stack([first, second]).reshape(1, clips, local_rows, PC, D)

    def swap_groups(grouped):
        return lax.all_to_all(grouped, "frames", split_axis=0, concat_axis=0, tiled=True)

    def pass_on(array, step):
        return lax.ppermute(array, "side", [(i, (i + step) % sides) for i in range(sides)])

    def flip(array, bit):
        return lax.ppermute(array, "frames", [(i, i ^ (1 << bit)) for i in range(frames)])

    def add(left, right):
        return (left.astype(WIDE) + right.astype(WIDE)).astype(LOW)

    def swap_rows(total):
        return lax.all_to_all(total, across, split_axis=0, concat_axis=0, tiled=True)

    class Reduction:
        def __init__(self, send, bits):
            self.came = flip(send, 0)
            self.bits = list(bits)
            self.left = sorted(bits, reverse=True)
            self.over_rows = False

        def start(self, keep):
            shape = (2,) * len(self.bits) + keep.shape[1:]
            self.keep = keep.reshape(shape)

        def advance(self):
            came = self.came.reshape(self.keep.shape)
            if not self.bits:
                rows = add(self.keep, came)
                self.came = swap_rows(rows.reshape((row_total, -1) + rows.shape[-1:]))
                self.keep = rows
                self.over_rows = True
                return
            bit = self.bits.pop(0)
            axis = self.left.index(bit)
            self.left.remove(bit)

            def cut(array, which):
                return lax.index_in_dim(array, which, axis, keepdims=False)

            going = add(cut(self.keep, 1), cut(came, 1))
            self.keep = add(cut(self.keep, 0), cut(came, 0))
            self.going = going
            self.came = flip(going, bit)

        def finish(self):
            while not self.over_rows:
                self.advance()
            return jnp.sum(self.came.astype(WIDE), axis=0)

    high_bits = list(range(1, frames.bit_length() - 1))

    source_own = clip_tokens(block_in, half)
    source_came = other_half(clip_tokens(block_in, 1 - half))
    grad_going, source_came = tie(clip_tokens(cotangent, 1 - half), source_came)
    grad_came = other_half(grad_going)
    source = jnp.concatenate([source_own, source_came])
    half_count = source_own.shape[0]

    level = jnp.where(half == 0, noise_level[:, 0], noise_level[:, -1])
    embed = jax.nn.silu(sinusoid(level)).astype(LOW)
    mod = jnp.dot(embed, w_mod, preferred_element_type=WIDE)

    blocks = jnp.stack([half, 1 - half])[:, None, None]
    rows = (blocks * sides + side) * local_rows + jnp.arange(local_rows)[None, :, None]
    row_pos = jnp.broadcast_to(rows, (clips, local_rows, PC)).reshape(-1).astype(WIDE)
    col_pos = jnp.broadcast_to(jnp.arange(PC), (clips, local_rows, PC)).reshape(-1).astype(WIDE)
    place_cosine, place_sine = turn_tables((None, row_pos, col_pos), heads)
    time_cosine, time_sine = turn_tables((block_map.astype(WIDE), None, None), heads)
    cosine = place_cosine + time_cosine[frame_slot]
    sine = place_sine + time_sine[frame_slot]
    tables = (place_cosine, place_sine, time_cosine[:, None], time_sine[:, None])

    hidden_one, query, pair = input_projections(
        source, mod, w_query, w_key, w_value, cosine, sine, frames
    )
    pair = swap_groups(pair)
    query = swap_groups(query)
    hidden_all = lax.all_gather(turn_hidden(hidden_one), "frames", axis=0)
    grad_result = jnp.concatenate([clip_tokens(cotangent, half), grad_came])
    pulled, scaled_turned = pull_down(grad_result, mod, w_down)

    pairs = [pair] + [pass_on(pair, step) for step in range(1, sides)]
    state = None
    for step in range(sides):
        state = attention_forward(order, state, query, pairs[step], step == sides - 1)
    attn_heads, log_total = state
    attn = swap_groups(attn_heads)

    (
        middle, hidden_two, active, grad_up_in, grad_middle, grad_branch, grad_attn,
        grad_gate_one, grad_shift_two, grad_scale_two,
    ) = middle_block(attn, source, grad_result, mod, w_proj, w_up, pulled)
    grad_attn = swap_groups(grad_attn)
    inputs = (slot, active, grad_up_in, hidden_two, scaled_turned, attn, grad_branch, row_total)
    down_send, up_send = weight_gradients(*inputs, None)
    down = Reduction(down_send, high_bits)
    up = Reduction(up_send, high_bits[::-1])
    result, grad_gate_two, down_keep, up_keep = weight_gradients(
        *inputs, (middle, grad_result, mod, w_down)
    )
    down.start(down_keep)
    up.start(up_keep)

    def spread(vectors, codes):
        wide = jnp.concatenate(vectors, axis=-1)
        share_of = D // devices
        codes = codes.reshape(devices, share_of)
        packed = jnp.concatenate(
            [jnp.broadcast_to(wide, (devices, wide.shape[-1])), codes], axis=-1
        )
        return lax.all_to_all(packed, everyone, split_axis=0, concat_axis=0, tiled=True)

    def mod_gradient(came):
        share_of = D // devices
        return jnp.einsum(
            "nd,ne->de",
            came[:, -share_of:],
            came[:, :-share_of],
            precision=lax.Precision.HIGHEST,
        )

    codes = embed.astype(WIDE)
    dq = None
    arrived = []
    cut = frames * 3 // 8
    calls = [(step, span) for step in range(sides - 1, -1, -1) for span in (0, 1)]
    for index, (step, span) in enumerate(calls):
        if index == 0:
            down.advance()
            up.advance()
            grad_attn, *ready = tie(grad_attn, down.going, down.keep, up.going, up.keep, result)
            out_came = other_half(result[half_count:])
        elif index == 1:
            dq, partial, down.came = tie(dq, partial, down.came)
            down.advance()
            mod_came = spread([grad_gate_one, grad_shift_two, grad_scale_two, grad_gate_two], codes)
            dq, partial, out_came, *ready = tie(dq, partial, out_came, down.came)
        elif index == 2:
            dq, down.came, up.came, mod_came = tie(dq, down.came, up.came, mod_came)
            down.advance()
            up.advance()
        elif index == 3:
            dq, partial, down.came, up.came = tie(dq, partial, down.came, up.came)
            up.advance()
        begin, end = ((0, cut), (cut, frames))[span]
        last = index == len(calls) - 1
        came = None
        if last and arrived:
            came = arrived[0]
            for more in arrived[1:]:
                came = add(came, more)
        answer = attention_backward(
            order, dq, None if span == 0 else partial, came, query, pairs[step], grad_attn,
            attn_heads, log_total, begin, end, last,
        )
        if last:
            grads = answer[0]
        else:
            dq, partial = answer
            if span == 1:
                arrived.append(pass_on(partial, -step))

    grads_back = swap_groups(grads)
    product = head_gradients(grads, hidden_all, tables)
    product = lax.all_to_all(
        product.reshape(devices, D // devices, 3 * lanes),
        everyone, split_axis=0, concat_axis=0, tiled=True,
    )
    product = jnp.sum(
        product.reshape(frames, row_total, D // devices, 3, lanes).astype(WIDE), axis=1
    )
    product = jnp.transpose(product, (2, 1, 0, 3)).reshape(3, D // devices, D)
    grad_source, grad_shift_one, grad_scale_one = input_gradients(
        grads_back, w_query, w_key, w_value, cosine, sine, source, mod, grad_middle
    )
    in_came = other_half(grad_source[half_count:])
    late_came = spread([grad_shift_one, grad_scale_one], codes)

    grad_down = down.finish().T
    up_proj = up.finish()
    grad_mod = jnp.concatenate([mod_gradient(late_came), mod_gradient(mod_came)], axis=-1)
    return (
        return_clip(result[:half_count], out_came, LOW),
        return_clip(grad_source[:half_count], in_came, WIDE),
        product[0], product[1], product[2],
        up_proj[:, FF:], up_proj[:, :FF], grad_down, grad_mod,
    )


def solution(mesh):
    frames, rows = mesh.shape["frames"], mesh.shape["rows"]
    clips = 2
    split = Mesh(
        mesh.devices.reshape(frames, clips, rows // clips), ("frames", "half", "side")
    )
    tokens = P("frames", None, ("half", "side"), None, None)
    shared = P(("frames", "half", "side"), None)
    return jax.shard_map(
        shards,
        mesh=split,
        in_specs=(tokens, P(), P("frames", None), P(), P(), P(), P(), P(), P(), P(), tokens),
        out_specs=(tokens, tokens) + (shared,) * 7,
        check_vma=False,
    )
```

time: 3210 us -> 694 us (0.22)
  waiting for transfers between devices: 1770 us -> 172 us
  matrix products: 765 us -> 8.29 us
  Pallas kernels: 0 us -> 309 us
  local copies, waits for them, and re-layouts: 293 us -> 32.2 us
  loops' own time: 118 us -> 0 us
  other arithmetic: 151 us -> 37.3 us
    reduce_scatter x9 -> x0, waiting for transfers between devices: 1680 us -> none  [the longest x1 365 us: shards(): lax.psum_scatter(grad_up, ('frames', 'rows'), scatter_dimension=0, tiled=...]
    dot_general x69 -> x3, matrix products: 765 us -> 8.29 us  [the longest x1 6.46 us: shards(): mod = jnp.dot(embed, w_mod, preferred_element_type=WIDE)]
    pallas_call x0 -> x14, Pallas kernels: none -> 309 us  [the longest x4 140 us: attention_backward(): pl.pallas_call(functools.partial(backward_kernel, first=first, last=last,...]
    another operation x27 -> x0, loops' own time: 118 us -> none  [the longest x1 26 us: shards(): lax.scan(back_step, zero_query, slots)]
    reduce_sum x14 -> x3, other arithmetic: 109 us -> 3.16 us  [the longest x2 1.72 us: finish(): return jnp.sum(self.came.astype(WIDE), axis=0)]
    ppermute x0 -> x12, waiting for transfers between devices: none -> 87.5 us  [the longest x4 41.8 us: other_half(): return lax.ppermute(array, 'half', [(0, 1), (1, 0)])]
    dynamic_slice x70 -> x1, local copies, waits for them, and re-layouts: 69.2 us -> 2.71 us  [clip_tokens(): lax.dynamic_index_in_dim(tokens[0], clip, 0, keepdims=False).reshape(-1, D)]
    concatenate x9 -> x7, local copies, waits for them, and re-layouts: 47.6 us -> 2.39 us  [the longest x2 1.24 us: turn_tables(): jnp.concatenate(sines * heads, axis=-1)]
  transfers between devices with their start and end apart: 17 -> 21, of which waited for: 14 -> 12; matrix products, arithmetic and copies ran while one was open for 12% -> 9% of each run, Pallas kernels for 0% -> 37%
where the time goes in v1:
time: 694 us; the launch traced here: 684 us
  Pallas kernels  309 us (45%)
  waiting for transfers between devices  172 us (25%)
  starting transfers between devices  55.3 us (8%)
  blocking collectives  53.5 us (8%)
  other arithmetic  37.3 us (5%)
  local copies, waits for them, and re-layouts  32.2 us (5%)
  between operations  16.5 us (2%)
  matrix products  8.29 us (1%)
    pallas_call x4, Pallas kernels, attention_backward(): pl.pallas_call(functools.partial(backward_kernel, first=first, last=last,...  140 us
    pallas_call x2, Pallas kernels, attention_forward(): pl.pallas_call(functools.partial(forward_kernel, first=first, last=last,...  77 us
    all_to_all x4, waiting for transfers between devices, swap_groups(): lax.all_to_all(grouped, 'frames', split_axis=0, concat_axis=0, tiled=True)  45.4 us
    ppermute x4, waiting for transfers between devices, other_half(): return lax.ppermute(array, 'half', [(0, 1), (1, 0)])  41.8 us
    ppermute x6, waiting for transfers between devices, flip(): lax.ppermute(array, 'frames', [(i, i ^ 1 << bit) for i in range(frames)])  36.2 us
    pallas_call x2, Pallas kernels, weight_gradients(): pl.pallas_call(functools.partial(weights_kernel, keep=keep), grid_spec=pl...  32.9 us
    all_to_all x1, blocking collectives, swap_groups(): lax.all_to_all(grouped, 'frames', split_axis=0, concat_axis=0, tiled=True)  30.2 us
    pallas_call x1, Pallas kernels, middle_block(): pl.pallas_call(middle_kernel, grid=(FF // wide,), out_shape=[of((count, D...  25 us
  transfers between devices with their start and end apart: 21, of which 12 were waited for; matrix products, arithmetic and copies ran while one was open for 9% of the time, Pallas kernels for 37%

profile of v1, /device:TPU:0, one launch (start us, length us, event | category | flops | bytes accessed | tf_op | source)
XLA Modules:
  0.0 684.0 jit_solution(3171639479415072730)
XLA Ops:
  7.2 2.7 constant_dynamic-slice_fusion
  9.9 4.0 collective-permute-start
  21.5 6.5 fusion.29.mod.refs_3_
  27.9 9.5 %collective-permute-done = bf16[256,1024]{1,0:T(8,128)(2,1)} collective-permute-done((bf16[256,1024]{1,0:T(8,128)(2,1)}, bf16[256,1024]{1,0:T(8,128)(2,1)}, u32[]{:S(2)}, u32[]{:S(2)}) %collective-permute-start) | collective-permute-done | bytes 524320 | tf_op jit(solution)/shard_map/ppermute | solution.py:844
  38.6 9.2 %input_projections.1 = (bf16[512,1024]{1,0:T(8,128)(2,1)S(1)}, bf16[8,512,128]{2,1,0:T(8,128)(2,1)}, bf16[8,2,512,128]{3,2,1,0:T(8,128)(2,1)S(1)}) custom-call(bf16[512,1024]{1,0:T(8,128)(2,1)S(1)} %pad_maximum_fusion.tokens, f32[1,6144]{1,0:T(1,128)S(1)} %fusion.29.mod.refs_3_, bf16[1024,1024]{1,0:T(8,128)(2,1)} %w_query.3, bf16[1024,1024]{1,0:T(8,128)(2,1)} %w_key.3, ...), custom_call_target="tpu_custom_call" | custom-call | flops 3221225472 | bytes 12582912 | tf_op jit(solution)/shard_map/input_projections/pallas_call | solution.py:418
  47.7 30.2 %all_to_all.64.pair = bf16[8,2,512,128]{3,2,1,0:T(8,128)(2,1)S(1)} all-to-all(bf16[8,2,512,128]{3,2,1,0:T(8,128)(2,1)S(1)} %get-tuple-element.66), channel_id=1, replica_groups=mesh['frames'=8,'half'=2,'side'=2] {'frames'}, dimensions={0} | all-to-all | bytes 4194304 | tf_op jit(solution)/shard_map/all_to_all | solution.py:852
  77.9 4.2 all-to-all-start
  83.1 4.1 collective-permute-start.1
  87.2 10.3 %all-to-all-done.query = bf16[8,512,128]{2,1,0:T(8,128)(2,1)} async-done(((bf16[8,512,128]{2,1,0:T(8,128)(2,1)}), bf16[8,512,128]{2,1,0:T(8,128)(2,1)}, u32[]{:S(2)}, u32[]{:S(2)}) %all-to-all-start) | async-done | bytes 1048608 | tf_op jit(solution)/shard_map/all_to_all | solution.py:852
  97.5 36.5 %attention_forward.2 = (s32[1]{0:T(128)}, f32[8,512,128]{2,1,0:T(8,128)}, f32[8,512,128]{2,1,0:T(8,128)}, f32[8,512,128]{2,1,0:T(8,128)}) custom-call(s32[8]{0:T(128)} %get-tuple-element.63.order, s32[1]{0:T(128)} %constant.52.clone.1.flag_in, bf16[8,512,128]{2,1,0:T(8,128)(2,1)} %all-to-all-done.query, bf16[8,2,512,128]{3,2,1,0:T(8,128)(2,1)} %copy-done.28), custom_call_target="tpu_custom_call" | custom-call | flops 38654705664 | bytes 16777216 | tf_op jit(solution)/shard_map/attention_forward/pallas_call | solution.py:209
  134.0 9.5 %collective-permute-done.1.pair = bf16[8,2,512,128]{3,2,1,0:T(8,128)(2,1)} collective-permute-done((bf16[8,2,512,128]{3,2,1,0:T(8,128)(2,1)S(1)}, bf16[8,2,512,128]{3,2,1,0:T(8,128)(2,1)}, u32[]{:S(2)}, u32[]{:S(2)}) %collective-permute-start.1) | collective-permute-done | bytes 2097184 | tf_op jit(solution)/shard_map/ppermute | solution.py:855
  143.5 40.5 %attention_forward.3 = (bf16[8,512,128]{2,1,0:T(8,128)(2,1)}, f32[8,8,512]{2,1,0:T(8,128)}) custom-call(s32[8]{0:T(128)} %get-tuple-element.63.order, s32[1]{0:T(128)} %get-tuple-element.67.flag_in, bf16[8,512,128]{2,1,0:T(8,128)(2,1)} %all-to-all-done.query, bf16[8,2,512,128]{3,2,1,0:T(8,128)(2,1)} %collective-permute-done.1.pair, ...), custom_call_target="tpu_custom_call" | custom-call | flops 38654705664 | bytes 16777216 | tf_op jit(solution)/shard_map/attention_forward/pallas_call | solution.py:209
  184.0 4.4 all-to-all-start.2
  190.0 3.4 copy-done.17
  193.3 6.6 pull_down.1
  203.8 25.0 %middle_block.1 = (f32[512,1024]{1,0:T(8,128)}, bf16[512,1024]{1,0:T(8,128)(2,1)}, bf16[512,4096]{1,0:T(8,128)(2,1)}, bf16[512,4096]{1,0:T(8,128)(2,1)}, f32[512...) custom-call(bf16[8,512,128]{2,1,0:T(8,128)(2,1)} %all-to-all-done.2., ...), custom_call_target="tpu_custom_call" | custom-call | flops 10737418240 | bytes 31457280 | tf_op jit(solution)/shard_map/middle_block/pallas_call | solution.py:531
  228.8 12.2 %weight_gradients.3 = (bf16[4,4,1024,128]{3,2,1,0:T(8,128)(2,1)}, bf16[4,128,5120]{2,1,0:T(8,128)(2,1)}) custom-call(s32[1]{0:T(128)} %bitcast.slot, bf16[512,4096]{1,0:T(8,128)(2,1)} %get-tuple-element.74.active.refs_0_, bf16[512,4096]{1,0:T(8,128)(2,1)} %get-tuple-element.75.grad_up_in, bf16[512,1024]{1,0:T(8,128)(2,1)} %get-tuple-element.76.hidden, ...), custom_call_target="tpu_custom_call" | custom-call | flops 4831838208 | bytes 25165824 | tf_op jit(solution)/shard_map/weight_gradients/pallas_call | solution.py:660
  243.0 4.4 all-to-all-start.3
  247.5 20.7 %weight_gradients.2 = (bf16[512,1024]{1,0:T(8,128)(2,1)}, f32[1,1024]{1,0:T(1,128)}, bf16[4,4,1024,128]{3,2,1,0:T(8,128)(2,1)}, bf16[4,128,5120]{2,1,0:T(8,128)(2,1)}) custom-call(s32[1]{0:T(128)} %bitcast.slot, bf16[512,4096]{1,0:T(8,128)(2,1)} %get-tuple-element.74.active.refs_0_, bf16[512,4096]{1,0:T(8,128)(2,1)} %get-tuple-element.75.grad_up_in, ...), custom_call_target="tpu_custom_call" | custom-call | flops 9126805504 | bytes 25165824 | tf_op jit(solution)/shard_map/weight_gradients/pallas_call | solution.py:660
  268.9 5.4 add_convert_fusion.2
  276.3 5.6 add_convert_fusion
  281.9 38.7 %attention_backward.4 = (f32[8,128,512]{2,1,0:T(8,128)}, bf16[8,2,512,128]{3,2,1,0:T(8,128)(2,1)}) custom-call(s32[8]{0:T(128)} %get-tuple-element.63.order, bf16[8,512,128]{2,1,0:T(8,128)(2,1)} %all-to-all-done.query, bf16[8,2,512,128]{3,2,1,0:T(8,128)(2,1)} %collective-permute-done.1.pair, bf16[8,512,128]{2,1,0:T(8,128)(2,1)} %all-to-all-done.3.grad, ...), custom_call_target="tpu_custom_call" | custom-call | flops 35232153600 | bytes 16777216 | tf_op jit(solution)/shard_map/attention_backward/pallas_call | solution.py:329
  320.6 24.5 %collective-permute-done.5 = bf16[2,4,1024,128]{3,2,1,0:T(8,128)(2,1)} collective-permute-done((bf16[2,4,1024,128]{3,2,1,0:T(8,128)(2,1)}, bf16[2,4,1024,128]{3,2,1,0:T(8,128)(2,1)}, u32[]{:S(2)}, u32[]{:S(2)}) %collective-permute-start.5) | collective-permute-done | bytes 2097184 | tf_op jit(solution)/shard_map/ppermute | solution.py:858
  345.1 2.5 fusion.7
  350.4 3.8 all-to-all-start.4
  356.2 2.8 collective-permute-start.6
  360.4 19.8 %all-to-all-done.4 = f32[32,1,4128]{2,1,0:T(1,128)S(1)} async-done(((f32[32,1,4128]{2,1,0:T(1,128)}), f32[32,1,4128]{2,1,0:T(1,128)S(1)}, u32[]{:S(2)}, u32[]{:S(2)}) %all-to-all-start.4) | async-done | bytes 528416 | tf_op jit(solution)/shard_map/all_to_all | solution.py:963
  381.0 11.2 %collective-permute-done.6 = bf16[256,1024]{1,0:T(8,128)(2,1)} collective-permute-done((bf16[256,1024]{1,0:T(8,128)(2,1)}, bf16[256,1024]{1,0:T(8,128)(2,1)}, u32[]{:S(2)}, u32[]{:S(2)}) %collective-permute-start.6) | collective-permute-done | bytes 524320 | tf_op jit(solution)/shard_map/ppermute | solution.py:844
  392.2 30.6 %attention_backward.5 = (f32[8,128,512]{2,1,0:T(8,128)}, bf16[8,2,512,128]{3,2,1,0:T(8,128)(2,1)}) custom-call(s32[8]{0:T(128)} %get-tuple-element.63.order, bf16[8,512,128]{2,1,0:T(8,128)(2,1)} %all-to-all-done.query, bf16[8,2,512,128]{3,2,1,0:T(8,128)(2,1)} %collective-permute-done.1.pair, bf16[8,512,128]{2,1,0:T(8,128)(2,1)} %all-to-all-done.3.grad, ...), custom_call_target="tpu_custom_call" | custom-call | flops 25165824000 | bytes 16777216 | tf_op jit(solution)/shard_map/attention_backward/pallas_call | solution.py:329
  422.8 11.7 %collective-permute-done.8 = bf16[2,128,5120]{2,1,0:T(8,128)(2,1)} collective-permute-done((bf16[2,128,5120]{2,1,0:T(8,128)(2,1)}, bf16[2,128,5120]{2,1,0:T(8,128)(2,1)}, u32[]{:S(2)}, u32[]{:S(2)}) %collective-permute-start.8) | collective-permute-done | bytes 2621472 | tf_op jit(solution)/shard_map/ppermute | solution.py:858
  434.5 2.8 fusion.5
  438.6 2.9 fusion.2
  441.6 3.6 all-to-all-start.5
  445.2 38.3 %attention_backward.6 = (f32[8,128,512]{2,1,0:T(8,128)}, bf16[8,2,512,128]{3,2,1,0:T(8,128)(2,1)}) custom-call(s32[8]{0:T(128)} %get-tuple-element.63.order, bf16[8,512,128]{2,1,0:T(8,128)(2,1)} %all-to-all-done.query, bf16[8,2,512,128]{3,2,1,0:T(8,128)(2,1)} %copy-done.28, bf16[8,512,128]{2,1,0:T(8,128)(2,1)} %all-to-all-done.3.grad, ...), custom_call_target="tpu_custom_call" | custom-call | flops 35232153600 | bytes 16777216 | tf_op jit(solution)/shard_map/attention_backward/pallas_call | solution.py:329
  483.5 3.5 all-to-all-done.5
  488.1 32.2 %attention_backward.7.grads = bf16[8,3,512,128]{3,2,1,0:T(8,128)(2,1)} custom-call(s32[8]{0:T(128)} %get-tuple-element.63.order, bf16[8,512,128]{2,1,0:T(8,128)(2,1)} %all-to-all-done.query, bf16[8,2,512,128]{3,2,1,0:T(8,128)(2,1)} %copy-done.28, bf16[8,512,128]{2,1,0:T(8,128)(2,1)} %all-to-all-done.3.grad, bf16[8,512,128]{2,1,0:T(8,128)(2,1)} %get-tuple-element.71.out, ...), custom_call_target="tpu_custom_call" | custom-call | flops 25165824000 | bytes 16777216 | tf_op jit(solution)/shard_map/attention_backward/pallas_call | solution.py:329
  520.3 3.4 copy-done
  523.6 8.6 %head_gradients.1 = bf16[1024,384]{1,0:T(8,128)(2,1)S(1)} custom-call(bf16[8,3,512,128]{3,2,1,0:T(8,128)(2,1)} %attention_backward.7.grads, bf16[8,1024,512]{2,1,0:T(8,128)(2,1)S(1)} %bitcast.80, f32[512,128]{1,0:T(8,128)S(1)} %copy-done.6, f32[512,128]{1,0:T(8,128)S(1)} %copy-done.4, f32[8,1,128]{2,1,0:T(1,128)S(1)} %bitcast.82, f32[8,1,128]{2,1,0:T(1,128)S(1)} %bitcast.83), custom_call_target="tpu_custom_call" | custom-call | flops 3221225472 | bytes 12582912 | tf_op jit(solution)/shard_map/head_gradients/pallas_call | solution.py:715
  532.3 23.3 %all_to_all.65 = bf16[32,32,384]{2,1,0:T(8,128)(2,1)} all-to-all(bf16[32,32,384]{2,1,0:T(8,128)(2,1)S(1)} %bitcast.81), channel_id=1, replica_groups=mesh['frames'=8,'half'=2,'side'=2] {'frames','half','side'}, dimensions={0} | all-to-all | bytes 1572864 | tf_op jit(solution)/shard_map/all_to_all | solution.py:1017
  555.6 3.8 all-to-all-start.6
  559.5 3.8 fusion
  563.2 34.1 %all-to-all-done.6.grads = bf16[8,3,512,128]{3,2,1,0:T(8,128)(2,1)S(1)} async-done(((bf16[8,3,512,128]{3,2,1,0:T(8,128)(2,1)}), bf16[8,3,512,128]{3,2,1,0:T(8,128)(2,1)S(1)}, u32[]{:S(2)}, u32[]{:S(2)}) %all-to-all-start.6) | async-done | bytes 3145760 | tf_op jit(solution)/shard_map/all_to_all | solution.py:852
  597.4 4.6 all-to-all-start.8
  605.8 9.0 %input_gradients.1 = (bf16[512,1024]{1,0:T(8,128)(2,1)S(1)}, f32[1,1024]{1,0:T(1,128)S(1)}, f32[1,1024]{1,0:T(1,128)S(1)}) custom-call(bf16[8,3,512,128]{3,2,1,0:T(8,128)(2,1)} %copy-done.20, bf16[1024,1024]{1,0:T(8,128)(2,1)S(1)} %copy-done.7, bf16[1024,1024]{1,0:T(8,128)(2,1)} %w_key.3, bf16[1024,1024]{1,0:T(8,128)(2,1)} %w_value.3, ...), custom_call_target="tpu_custom_call" | custom-call | flops 3221225472 | bytes 14680064 | tf_op jit(solution)/shard_map/input_gradients/pallas_call | solution.py:772
  615.9 15.3 %all-to-all-done.8 = bf16[4,32,5120]{2,1,0:T(8,128)(2,1)} async-done(((bf16[4,32,5120]{2,1,0:T(8,128)(2,1)}), bf16[4,32,5120]{2,1,0:T(8,128)(2,1)}, u32[]{:S(2)}, u32[]{:S(2)}) %all-to-all-start.8) | async-done | bytes 1310752 | tf_op jit(solution)/shard_map/all_to_all | solution.py:864
  631.2 5.4 all-to-all-start.9
  648.9 2.7 collective-permute-start.11
  653.9 21.2 %collective-permute-done.11 = bf16[256,1024]{1,0:T(8,128)(2,1)S(1)} collective-permute-done((bf16[256,1024]{1,0:T(8,128)(2,1)S(1)}, bf16[256,1024]{1,0:T(8,128)(2,1)S(1)}, u32[]{:S(2)}, u32[]{:S(2)}) %collective-permute-start.11) | collective-permute-done | bytes 524320 | tf_op jit(solution)/shard_map/ppermute | solution.py:844
  (165 shorter events, 48.6 us)
Async XLA Ops:
  7.2 7.2 %copy-start.35 = (s32[8]{0:T(128)S(1)}, s32[8]{0:T(128)}, u32[]{:S(2)}) copy-start(s32[8]{0:T(128)} %param.12) | copy-start | bytes 100
  7.2 7.2 %copy-start.34 = (s32[1,2]{1,0:T(1,128)S(1)}, s32[1,2]{1,0:T(1,128)}, u32[]{:S(2)}) copy-start(s32[1,2]{1,0:T(1,128)} %param.13) | copy-start | bytes 28
  9.9 27.5 %collective-permute-start = (bf16[256,1024]{1,0:T(8,128)(2,1)}, bf16[256,1024]{1,0:T(8,128)(2,1)}, u32[]{:S(2)}, u32[]{:S(2)}) collective-permute-start(bf16[256,1024]{1,0:T(8,128)(2,1)} %bitcast.3), channel_id=1, source_target_pairs={{0,2},{2,0},{1,3},{3,1},{4,6},{6,4},{5,7},{7,5},{8,10},{10,8},{9,1... | collective-permute-start | bytes 1572872 | tf_op jit(solution)/shard_map/ppermute | solution.py:844
  21.4 6.5 copy-start.5
  21.5 17.1 %copy-start.8 = (f32[512,128]{1,0:T(8,128)}, f32[512,128]{1,0:T(8,128)S(1)}, u32[]{:S(2)}) copy-start(f32[512,128]{1,0:T(8,128)S(1)} %broadcast_add_fusion.1.cosine) | copy-start | bytes 786436
  27.9 162.0 %copy-start.11 = (f32[1,6144]{1,0:T(1,128)}, f32[1,6144]{1,0:T(1,128)S(1)}, u32[]{:S(2)}) copy-start(f32[1,6144]{1,0:T(1,128)S(1)} %fusion.29.mod.refs_3_) | copy-start | bytes 73732
  38.5 9.2 %copy-start.1 = (bf16[512,1024]{1,0:T(8,128)(2,1)}, bf16[512,1024]{1,0:T(8,128)(2,1)S(1)}, u32[]{:S(2)}) copy-start(bf16[512,1024]{1,0:T(8,128)(2,1)S(1)} %pad_maximum_fusion.tokens) | copy-start | bytes 3145732
  77.9 19.7 %copy-start.28 = (bf16[8,2,512,128]{3,2,1,0:T(8,128)(2,1)}, bf16[8,2,512,128]{3,2,1,0:T(8,128)(2,1)S(1)}, u32[]{:S(2)}) copy-start(bf16[8,2,512,128]{3,2,1,0:T(8,128)(2,1)S(1)} %all_to_all.64.pair) | copy-start | bytes 6291460
  77.9 19.7 %all-to-all-start = ((bf16[8,512,128]{2,1,0:T(8,128)(2,1)}), bf16[8,512,128]{2,1,0:T(8,128)(2,1)}, u32[]{:S(2)}, u32[]{:S(2)}) async-start(bf16[8,512,128]{2,1,0:T(8,128)(2,1)} %get-tuple-element.65), calls=%async_computation | async-start | bytes 2097152 | tf_op jit(solution)/shard_map/all_to_all | solution.py:852
  83.1 105.7 %collective-permute-start.2 = (bf16[256,1024]{1,0:T(8,128)(2,1)}, bf16[256,1024]{1,0:T(8,128)(2,1)}, u32[]{:S(2)}, u32[]{:S(2)}) collective-permute-start(bf16[256,1024]{1,0:T(8,128)(2,1)} %bitcast.98), channel_id=1, source_target_pairs={{0,2},{2,0},{1,3},{3,1},{4,6},{6,4},{5,7},{7,5},{8,10},{10,8},{9,1... | collective-permute-start | bytes 1572872 | tf_op jit(solution)/shard_map/ppermute | solution.py:844
  83.1 60.4 %collective-permute-start.1 = (bf16[8,2,512,128]{3,2,1,0:T(8,128)(2,1)S(1)}, bf16[8,2,512,128]{3,2,1,0:T(8,128)(2,1)}, u32[]{:S(2)}, u32[]{:S(2)}) collective-permute-start(bf16[8,2,512,128]{3,2,1,0:T(8,128)(2,1)S(1)} %all_to_all.64.pair), channel_id=1, source_target_pairs={{0,1},{1,0},{2,3},{3,2},{4,5},{5,4},{6,7},{7,6},{8,9},{9,8},{10,11... | collective-permute-start | bytes 6291464 | tf_op jit(solution)/shard_map/ppermute | solution.py:855
  184.0 4.8 copy-start.29
  184.0 19.8 %all-to-all-start.2 = ((bf16[8,512,128]{2,1,0:T(8,128)(2,1)}), bf16[8,512,128]{2,1,0:T(8,128)(2,1)}, u32[]{:S(2)}, u32[]{:S(2)}) async-start(bf16[8,512,128]{2,1,0:T(8,128)(2,1)} %get-tuple-element.71.out), calls=%async_computation.2 | async-start | bytes 2097152 | tf_op jit(solution)/shard_map/all_to_all | solution.py:852
  188.4 331.9 %all-gather.3.cloned.1.call-start = ((), (), s32[]{:S(2)}) async-start(), calls=%async_computation.10 | async-start | bytes 9437184 | tf_op jit(solution)/shard_map/all_gather | solution.py:930
  190.0 3.4 copy-start.17
  193.3 6.6 copy-start.10
  241.0 35.3 %collective-permute-start.4 = (bf16[4,128,5120]{2,1,0:T(8,128)(2,1)}, bf16[4,128,5120]{2,1,0:T(8,128)(2,1)}, u32[]{:S(2)}, u32[]{:S(2)}) collective-permute-start(bf16[4,128,5120]{2,1,0:T(8,128)(2,1)} %get-tuple-element.85), channel_id=1, source_target_pairs={{0,4},{4,0},{8,12},{12,8},{16,20},{20,16},{24,28},{28,24},{1,5},{5... | collective-permute-start | bytes 15728648 | tf_op jit(solution)/shard_map/ppermute | solution.py:858
  241.0 27.9 %collective-permute-start.3 = (bf16[4,4,1024,128]{3,2,1,0:T(8,128)(2,1)}, bf16[4,4,1024,128]{3,2,1,0:T(8,128)(2,1)}, u32[]{:S(2)}, u32[]{:S(2)}) collective-permute-start(bf16[4,4,1024,128]{3,2,1,0:T(8,128)(2,1)} %get-tuple-element.83), channel_id=1, source_target_pairs={{0,4},{4,0},{8,12},{12,8},{16,20},{20,16},{24,28},{28,24},{1,5},{5... | collective-permute-start | bytes 12582920 | tf_op jit(solution)/shard_map/ppermute | solution.py:858
  243.0 38.9 %all-to-all-start.3 = ((bf16[8,512,128]{2,1,0:T(8,128)(2,1)}), bf16[8,512,128]{2,1,0:T(8,128)(2,1)}, u32[]{:S(2)}, u32[]{:S(2)}) async-start(bf16[8,512,128]{2,1,0:T(8,128)(2,1)} %get-tuple-element.81), calls=%async_computation.3 | async-start | bytes 2097152 | tf_op jit(solution)/shard_map/all_to_all | solution.py:852
  247.4 20.7 %copy-start.31 = (f32[1,1024]{1,0:T(1,128)S(1)}, f32[1,1024]{1,0:T(1,128)}, u32[]{:S(2)}) copy-start(f32[1,1024]{1,0:T(1,128)} %get-tuple-element.97) | copy-start | bytes 12292
  247.5 20.7 %copy-start.32 = (f32[1,1024]{1,0:T(1,128)S(1)}, f32[1,1024]{1,0:T(1,128)}, u32[]{:S(2)}) copy-start(f32[1,1024]{1,0:T(1,128)} %get-tuple-element.98) | copy-start | bytes 12292
  247.5 20.7 %copy-start.33 = (f32[1,1024]{1,0:T(1,128)S(1)}, f32[1,1024]{1,0:T(1,128)}, u32[]{:S(2)}) copy-start(f32[1,1024]{1,0:T(1,128)} %get-tuple-element.99) | copy-start | bytes 12292
  268.9 7.4 %slice-start = ((s8[5242880]{0:T(1024)(128)(4,1)}), s8[4194304]{0:T(1024)(128)(4,1)S(1)}, s32[]{:S(2)}) async-start(s8[5242880]{0:T(1024)(128)(4,1)} %bitcast.85), calls=%async_computation.11 | async-start | bytes 8388608
  268.9 7.4 %slice-start.1 = ((s8[5242880]{0:T(1024)(128)(4,1)}), s8[1048576]{0:T(1024)(128)(4,1)S(1)}, s32[]{:S(2)}) async-start(s8[5242880]{0:T(1024)(128)(4,1)} %bitcast.85), calls=%async_computation.12 | async-start | bytes 2097152
  274.3 70.8 %collective-permute-start.5 = (bf16[2,4,1024,128]{3,2,1,0:T(8,128)(2,1)}, bf16[2,4,1024,128]{3,2,1,0:T(8,128)(2,1)}, u32[]{:S(2)}, u32[]{:S(2)}) collective-permute-start(bf16[2,4,1024,128]{3,2,1,0:T(8,128)(2,1)} %get-tuple-element.147), channel_id=1, source_target_pairs={{0,8},{4,12},{8,0},{12,4},{16,24},{20,28},{24,16},{28,20},{1,9},{5... | collective-permute-start | bytes 6291464 | tf_op jit(solution)/shard_map/ppermute | solution.py:858
  281.9 152.7 %copy-start.21 = (bf16[2,128,5120]{2,1,0:T(8,128)(2,1)}, bf16[2,128,5120]{2,1,0:T(8,128)(2,1)S(1)}, u32[]{:S(2)}) copy-start(bf16[2,128,5120]{2,1,0:T(8,128)(2,1)S(1)} %get-tuple-element.144) | copy-start | bytes 7864324
  281.9 63.2 %copy-start.22 = (bf16[2,1,4,1024,128]{4,3,2,1,0:T(8,128)(2,1)S(1)}, bf16[2,1,4,1024,128]{4,3,2,1,0:T(8,128)(2,1)}, u32[]{:S(2)}) copy-start(bf16[2,1,4,1024,128]{4,3,2,1,0:T(8,128)(2,1)} %get-tuple-element.146) | copy-start | bytes 6291460
  347.5 44.7 %collective-permute-start.7 = (bf16[4,1024,128]{2,1,0:T(8,128)(2,1)}, bf16[4,1024,128]{2,1,0:T(8,128)(2,1)}, u32[]{:S(2)}, u32[]{:S(2)}) collective-permute-start(bf16[4,1024,128]{2,1,0:T(8,128)(2,1)} %fusion.7), channel_id=1, source_target_pairs={{0,16},{4,20},{8,24},{12,28},{16,0},{20,4},{24,8},{28,12},{1,17},{... | collective-permute-start | bytes 3145736 | tf_op jit(solution)/shard_map/ppermute | solution.py:858
  350.4 29.8 %all-to-all-start.4 = ((f32[32,1,4128]{2,1,0:T(1,128)}), f32[32,1,4128]{2,1,0:T(1,128)S(1)}, u32[]{:S(2)}, u32[]{:S(2)}) async-start(f32[32,1,4128]{2,1,0:T(1,128)} %all_to_all.44), calls=%async_computation.4 | async-start | bytes 1081344 | tf_op jit(solution)/shard_map/all_to_all | solution.py:963
  356.2 36.0 %collective-permute-start.6 = (bf16[256,1024]{1,0:T(8,128)(2,1)}, bf16[256,1024]{1,0:T(8,128)(2,1)}, u32[]{:S(2)}, u32[]{:S(2)}) collective-permute-start(bf16[256,1024]{1,0:T(8,128)(2,1)} %slice.111), channel_id=1, source_target_pairs={{0,2},{2,0},{1,3},{3,1},{4,6},{6,4},{5,7},{7,5},{8,10},{10,8},{9,1... | collective-permute-start | bytes 1572872 | tf_op jit(solution)/shard_map/ppermute | solution.py:844
  358.9 75.6 %collective-permute-start.8 = (bf16[2,128,5120]{2,1,0:T(8,128)(2,1)}, bf16[2,128,5120]{2,1,0:T(8,128)(2,1)}, u32[]{:S(2)}, u32[]{:S(2)}) collective-permute-start(bf16[2,128,5120]{2,1,0:T(8,128)(2,1)} %get-tuple-element.145), channel_id=1, source_target_pairs={{0,16},{4,20},{8,24},{12,28},{16,0},{20,4},{24,8},{28,12},{1,17},{... | collective-permute-start | bytes 7864328 | tf_op jit(solution)/shard_map/ppermute | solution.py:858
  422.8 15.8 %copy-start.23 = (bf16[2,1,4,1024,128]{4,3,2,1,0:T(8,128)(2,1)S(1)}, bf16[2,1,4,1024,128]{4,3,2,1,0:T(8,128)(2,1)}, u32[]{:S(2)}) copy-start(bf16[2,1,4,1024,128]{4,3,2,1,0:T(8,128)(2,1)} %get-tuple-element.146) | copy-start | bytes 6291460
  422.8 65.3 %collective-permute-start.10 = (bf16[8,2,512,128]{3,2,1,0:T(8,128)(2,1)}, bf16[8,2,512,128]{3,2,1,0:T(8,128)(2,1)}, u32[]{:S(2)}, u32[]{:S(2)}) collective-permute-start(bf16[8,2,512,128]{3,2,1,0:T(8,128)(2,1)} %get-tuple-element.108), channel_id=1, source_target_pairs={{0,1},{1,0},{2,3},{3,2},{4,5},{5,4},{6,7},{7,6},{8,9},{9,8},{10,11... | collective-permute-start | bytes 6291464 | tf_op jit(solution)/shard_map/ppermute | solution.py:855
  437.3 46.2 %collective-permute-start.9 = (bf16[128,5120]{1,0:T(8,128)(2,1)}, bf16[128,5120]{1,0:T(8,128)(2,1)S(1)}, u32[]{:S(2)}, u32[]{:S(2)}) collective-permute-start(bf16[128,5120]{1,0:T(8,128)(2,1)} %fusion.5), channel_id=1, source_target_pairs={{0,8},{4,12},{8,0},{12,4},{16,24},{20,28},{24,16},{28,20},{1,9},{5... | collective-permute-start | bytes 3932168 | tf_op jit(solution)/shard_map/ppermute | solution.py:858
  441.6 45.5 %all-to-all-start.5 = ((bf16[4,1024,128]{2,1,0:T(8,128)(2,1)}), bf16[4,1024,128]{2,1,0:T(8,128)(2,1)S(1)}, u32[]{:S(2)}, u32[]{:S(2)}) async-start(bf16[4,1024,128]{2,1,0:T(8,128)(2,1)} %fusion.2), calls=%async_computation.5 | async-start | bytes 2097152 | tf_op jit(solution)/shard_map/all_to_all | solution.py:864
  483.5 36.7 %copy-start.30 = (bf16[128,5120]{1,0:T(8,128)(2,1)}, bf16[128,5120]{1,0:T(8,128)(2,1)S(1)}, u32[]{:S(2)}) copy-start(bf16[128,5120]{1,0:T(8,128)(2,1)S(1)} %collective-permute-done.9) | copy-start | bytes 3932164
  488.1 32.2 %copy-start.4 = (f32[512,128]{1,0:T(8,128)S(1)}, f32[512,128]{1,0:T(8,128)}, u32[]{:S(2)}) copy-start(f32[512,128]{1,0:T(8,128)} %copy-done.3) | copy-start | bytes 786436
  488.1 32.2 %copy-start.6 = (f32[512,128]{1,0:T(8,128)S(1)}, f32[512,128]{1,0:T(8,128)}, u32[]{:S(2)}) copy-start(f32[512,128]{1,0:T(8,128)} %copy-done.5) | copy-start | bytes 786436
  488.1 32.2 %copy-start.14 = (f32[8,128]{1,0:T(8,128)S(1)}, f32[8,128]{1,0:T(8,128)}, u32[]{:S(2)}) copy-start(f32[8,128]{1,0:T(8,128)} %copy-done.13) | copy-start | bytes 12292
  488.1 32.2 %copy-start.16 = (f32[8,128]{1,0:T(8,128)S(1)}, f32[8,128]{1,0:T(8,128)}, u32[]{:S(2)}) copy-start(f32[8,128]{1,0:T(8,128)} %copy-done.15) | copy-start | bytes 12292
  555.6 41.7 %all-to-all-start.6 = ((bf16[8,3,512,128]{3,2,1,0:T(8,128)(2,1)}), bf16[8,3,512,128]{3,2,1,0:T(8,128)(2,1)S(1)}, u32[]{:S(2)}, u32[]{:S(2)}) async-start(bf16[8,3,512,128]{3,2,1,0:T(8,128)(2,1)} %attention_backward.7.grads), calls=%async_computation.6 | async-start | bytes 6291456 | tf_op jit(solution)/shard_map/all_to_all | solution.py:852
  597.4 5.9 copy-start.20
  597.4 33.8 %all-to-all-start.8 = ((bf16[4,32,5120]{2,1,0:T(8,128)(2,1)}), bf16[4,32,5120]{2,1,0:T(8,128)(2,1)}, u32[]{:S(2)}, u32[]{:S(2)}) async-start(bf16[4,32,5120]{2,1,0:T(8,128)(2,1)} %bitcast.84), calls=%async_computation.8 | async-start | bytes 2621440 | tf_op jit(solution)/shard_map/all_to_all | solution.py:864
  601.9 3.9 copy-start.9
  614.9 21.8 %copy-start.25 = (bf16[4,1024,128]{2,1,0:T(8,128)(2,1)S(1)}, bf16[4,1024,128]{2,1,0:T(8,128)(2,1)}, u32[]{:S(2)}) copy-start(bf16[4,1024,128]{2,1,0:T(8,128)(2,1)} %copy-done.24) | copy-start | bytes 3145732
  631.2 20.4 %all-to-all-start.9 = ((f32[32,1,2080]{2,1,0:T(1,128)}), f32[32,1,2080]{2,1,0:T(1,128)}, u32[]{:S(2)}, u32[]{:S(2)}) async-start(f32[32,1,2080]{2,1,0:T(1,128)} %all_to_all.51), calls=%async_computation.9 | async-start | bytes 557056 | tf_op jit(solution)/shard_map/all_to_all | solution.py:963
  647.4 5.6 copy-start.27
  648.9 26.2 %collective-permute-start.11 = (bf16[256,1024]{1,0:T(8,128)(2,1)S(1)}, bf16[256,1024]{1,0:T(8,128)(2,1)S(1)}, u32[]{:S(2)}, u32[]{:S(2)}) collective-permute-start(bf16[256,1024]{1,0:T(8,128)(2,1)S(1)} %slice.121), channel_id=1, source_target_pairs={{0,2},{2,0},{1,3},{3,1},{4,6},{6,4},{5,7},{7,5},{8,10},{10,8},{9,1... | collective-permute-start | bytes 1572872 | tf_op jit(solution)/shard_map/ppermute | solution.py:844
  (11 other events, 21.1 us)
Sparse Core Ops, SparseCore 0:
  243.1 83.3 all-gather.2

commit v2 on v1

--- a/solution.py
+++ b/solution.py
@@ -46,6 +46,17 @@
 
 def whole(shape):
     return pl.BlockSpec(shape, lambda *unused: (0,) * len(shape))
+
+
+def behind(kernel, count):
+    def ordered(*refs):
+        return kernel(*refs[count:])
+
+    return ordered
+
+
+def anywhere(count):
+    return [pl.BlockSpec(memory_space=pl.ANY)] * count
 
 
 def column_sum(values):
@@ -303,7 +314,9 @@
             final[f, 0] = (dq_sum[f].T * (1.0 / math.sqrt(HD))).astype(LOW)
 
 
-def attention_backward(order, dq, partial, came, query, pair, grad, out, lse, begin, end, last):
+def attention_backward(
+    order, dq, partial, came, query, pair, grad, out, lse, begin, end, last, after
+):
     frames, tokens, lanes = query.shape
     heads = lanes // HD
     first = dq is None
@@ -327,12 +340,15 @@
             jax.ShapeDtypeStruct(sums, WIDE), jax.ShapeDtypeStruct((frames, 2, tokens, lanes), LOW)
         ]
     return pl.pallas_call(
-        functools.partial(
-            backward_kernel, first=first, last=last, begin=begin, end=end,
-            came=came is not None, heads=heads,
+        behind(
+            functools.partial(
+                backward_kernel, first=first, last=last, begin=begin, end=end,
+                came=came is not None, heads=heads,
+            ),
+            len(after),
         ),
         out_shape=out_shape,
-        in_specs=[smem()] + [vmem()] * (5 + len(extra)),
+        in_specs=anywhere(len(after)) + [smem()] + [vmem()] * (5 + len(extra)),
         out_specs=[vmem()] * len(out_shape),
         scratch_shapes=scratch,
         compiler_params=pltpu.CompilerParams(vmem_limit_bytes=56 * MIB),
@@ -340,7 +356,7 @@
             flops=work * 10 * HD * 5, bytes_accessed=16 * MIB, transcendentals=work
         ),
         name="attention_backward",
-    )(order, query, pair, grad, out, lse, *extra)
+    )(*after, order, query, pair, grad, out, lse, *extra)
 
 
 def normalize(values):
@@ -709,14 +725,14 @@
         product[...] = total[...].astype(LOW)
 
 
-def head_gradients(grads, hidden_all, tables):
+def head_gradients(grads, hidden_all, tables, after):
     frames, unused, count, lanes = grads.shape
     frame = pl.BlockSpec((1, 1, lanes), lambda f: (f, 0, 0))
     return pl.pallas_call(
-        head_kernel,
+        behind(head_kernel, len(after)),
         grid=(frames,),
         out_shape=jax.ShapeDtypeStruct((D, 3 * lanes), LOW),
-        in_specs=[
+        in_specs=anywhere(len(after)) + [
             pl.BlockSpec((1, 3, count, lanes), lambda f: (f, 0, 0, 0)),
             pl.BlockSpec((1, D, count), lambda f: (f, 0, 0)),
             whole((count, lanes)), whole((count, lanes)), frame, frame,
@@ -728,7 +744,7 @@
             flops=6 * frames * count * D * lanes, bytes_accessed=12 * MIB, transcendentals=0
         ),
         name="head_gradients",
-    )(grads, hidden_all, *tables)
+    )(*after, grads, hidden_all, *tables)
 
 
 def output_kernel(
@@ -761,7 +777,7 @@
         ).astype(LOW)
 
 
-def input_gradients(grads, w_query, w_key, w_value, cosine, sine, tokens, mod, grad_middle):
+def input_gradients(grads, w_query, w_key, w_value, cosine, sine, tokens, mod, grad_middle, after):
     frames, unused, count, lanes = grads.shape
     wide = 256
     groups = wide // lanes
@@ -770,10 +786,10 @@
     weight = pl.BlockSpec((D, wide), lambda c: (0, c))
     rows = jax.ShapeDtypeStruct((1, D), WIDE)
     return pl.pallas_call(
-        output_kernel,
+        behind(output_kernel, len(after)),
         grid=(D // wide,),
         out_shape=[jax.ShapeDtypeStruct((count, D), LOW), rows, rows],
-        in_specs=[
+        in_specs=anywhere(len(after)) + [
             pl.BlockSpec((groups, 3, count, lanes), lambda c: (c, 0, 0, 0)),
             weight, weight, weight, whole(cosine.shape), whole(sine.shape),
             flat, whole((1, 6 * D)), flat,
@@ -785,7 +801,97 @@
             flops=6 * count * D * D, bytes_accessed=14 * MIB, transcendentals=0
         ),
         name="input_gradients",
-    )(grads, w_query, w_key, w_value, cosine, sine, tokens, mod, grad_middle)
+    )(*after, grads, w_query, w_key, w_value, cosine, sine, tokens, mod, grad_middle)
+
+
+def halves_kernel(mine, keep_give, came_give, keep_hold, came_hold, give, hold):
+    give[0, 0] = (keep_give[0, 0, 0].astype(WIDE) + came_give[0, 0, 0].astype(WIDE)).astype(LOW)
+    hold[0, 0] = (keep_hold[0, 0, 0].astype(WIDE) + came_hold[0, 0, 0].astype(WIDE)).astype(LOW)
+
+
+def add_halves(keep, came, axis, mine, after):
+    shape = keep.shape
+    lead, trail = math.prod(shape[:axis]), math.prod(shape[axis + 1 : -2])
+    rest = shape[:axis] + shape[axis + 1 :]
+    block = (1, 1, 1) + shape[-2:]
+    view = (lead, 2, trail) + shape[-2:]
+
+    def part_of(other):
+        def index(a, b, mine, *unused):
+            return (a, 1 - mine[0] if other else mine[0], b, 0, 0)
+
+        return pl.BlockSpec(block, index)
+
+    out = pl.BlockSpec((1, 1) + shape[-2:], lambda a, b, *unused: (a, b, 0, 0))
+    out_shape = jax.ShapeDtypeStruct((lead, trail) + shape[-2:], LOW)
+
+    def ordered(mine, *refs):
+        halves_kernel(mine, *refs[len(after) :])
+
+    keep, came = keep.reshape(view), came.reshape(view)
+    give, hold = pl.pallas_call(
+        ordered,
+        grid_spec=pltpu.PrefetchScalarGridSpec(
+            num_scalar_prefetch=1,
+            grid=(lead, trail),
+            in_specs=anywhere(len(after)) + [part_of(True)] * 2 + [part_of(False)] * 2,
+            out_specs=[out, out],
+        ),
+        out_shape=[out_shape, out_shape],
+        cost_estimate=pl.CostEstimate(
+            flops=keep.size, bytes_accessed=6 * keep.size, transcendentals=0
+        ),
+        name="add_halves",
+    )(mine, *after, keep, came, keep, came)
+    return give.reshape(rest), hold.reshape(rest)
+
+
+def total_kernel(keep, came, total):
+    total[...] = keep[...].astype(WIDE) + came[...].astype(WIDE)
+
+
+def add_last(keep, came, after):
+    return pl.pallas_call(
+        behind(total_kernel, len(after)),
+        out_shape=jax.ShapeDtypeStruct(keep.shape, WIDE),
+        in_specs=anywhere(len(after)) + [vmem()] * 2,
+        out_specs=vmem(),
+        name="add_last",
+    )(*after, keep, came)
+
+
+def same_kernel(*unused):
+    pass
+
+
+def order_after(array, after):
+    return pl.pallas_call(
+        same_kernel,
+        out_shape=jax.ShapeDtypeStruct(array.shape, array.dtype),
+        in_specs=anywhere(len(after) + 1),
+        out_specs=anywhere(1)[0],
+        input_output_aliases={len(after): 0},
+        name="order_after",
+    )(*after, array)
+
+
+def pack_kernel(*refs):
+    *vectors, codes, packed = refs
+    at = 0
+    for vector in vectors:
+        packed[:, at : at + D] = jnp.broadcast_to(vector[...], (packed.shape[0], D))
+        at += D
+    packed[:, at:] = codes[...]
+
+
+def pack(vectors, codes, after):
+    return pl.pallas_call(
+        behind(pack_kernel, len(after)),
+        out_shape=jax.ShapeDtypeStruct((codes.shape[0], len(vectors) * D + codes.shape[1]), WIDE),
+        in_specs=anywhere(len(after)) + [vmem()] * (len(vectors) + 1),
+        out_specs=vmem(),
+        name="pack",
+    )(*after, *vectors, codes)
 
 
 def sinusoid(levels):
@@ -860,44 +966,42 @@
     def add(left, right):
         return (left.astype(WIDE) + right.astype(WIDE)).astype(LOW)
 
-    def swap_rows(total):
-        return lax.all_to_all(total, across, split_axis=0, concat_axis=0, tiled=True)
-
     class Reduction:
         def __init__(self, send, bits):
             self.came = flip(send, 0)
             self.bits = list(bits)
             self.left = sorted(bits, reverse=True)
-            self.over_rows = False
+            self.row_bits = [("side", bit) for bit in range(sides.bit_length() - 1)] + [("half", 0)]
+            self.row_left = [("half", 0)] + self.row_bits[:-1][::-1]
+            self.going = None
 
         def start(self, keep):
-            shape = (2,) * len(self.bits) + keep.shape[1:]
-            self.keep = keep.reshape(shape)
-
-        def advance(self):
+            rest = (row_total, -1) + keep.shape[-1:]
+            self.shape = (2,) * (len(self.left) + len(self.row_left))
+            self.keep = keep.reshape(self.shape + rest[1:])
+
+        def advance(self, after=()):
             came = self.came.reshape(self.keep.shape)
-            if not self.bits:
-                rows = add(self.keep, came)
-                self.came = swap_rows(rows.reshape((row_total, -1) + rows.shape[-1:]))
-                self.keep = rows
-                self.over_rows = True
-                return
-            bit = self.bits.pop(0)
-            axis = self.left.index(bit)
-            self.left.remove(bit)
-
-            def cut(array, which):
-                return lax.index_in_dim(array, which, axis, keepdims=False)
-
-            going = add(cut(self.keep, 1), cut(came, 1))
-            self.keep = add(cut(self.keep, 0), cut(came, 0))
-            self.going = going
-            self.came = flip(going, bit)
-
-        def finish(self):
-            while not self.over_rows:
-                self.advance()
-            return jnp.sum(self.came.astype(WIDE), axis=0)
+            if self.bits:
+                bit = self.bits.pop(0)
+                axis = self.left.index(bit)
+                self.left.remove(bit)
+                name, mine = "frames", 0
+            else:
+                name, bit = self.row_bits.pop(0)
+                axis = self.row_left.index((name, bit))
+                self.row_left.remove((name, bit))
+                mine = (lax.axis_index(name) >> bit) & 1
+
+            mine = jnp.asarray(mine, jnp.int32).reshape(1)
+            self.going, self.keep = add_halves(self.keep, came, axis, mine, after)
+            size = lax.axis_size(name)
+            self.came = lax.ppermute(self.going, name, [(i, i ^ (1 << bit)) for i in range(size)])
+
+        def finish(self, after):
+            while self.bits or self.row_bits:
+                self.advance(after)
+            return add_last(self.keep, self.came, after)
 
     high_bits = list(range(1, frames.bit_length() - 1))
 
@@ -953,13 +1057,8 @@
     down.start(down_keep)
     up.start(up_keep)
 
-    def spread(vectors, codes):
-        wide = jnp.concatenate(vectors, axis=-1)
-        share_of = D // devices
-        codes = codes.reshape(devices, share_of)
-        packed = jnp.concatenate(
-            [jnp.broadcast_to(wide, (devices, wide.shape[-1])), codes], axis=-1
-        )
+    def spread(vectors, after):
+        packed = pack(vectors, codes, after)
         return lax.all_to_all(packed, everyone, split_axis=0, concat_axis=0, tiled=True)
 
     def mod_gradient(came):
@@ -971,29 +1070,30 @@
             precision=lax.Precision.HIGHEST,
         )
 
-    codes = embed.astype(WIDE)
+    codes = embed.astype(WIDE).reshape(devices, D // devices)
     dq = None
     arrived = []
     cut = frames * 3 // 8
     calls = [(step, span) for step in range(sides - 1, -1, -1) for span in (0, 1)]
     for index, (step, span) in enumerate(calls):
+        after = ()
         if index == 0:
             down.advance()
             up.advance()
-            grad_attn, *ready = tie(grad_attn, down.going, down.keep, up.going, up.keep, result)
+            after = (down.going, up.going)
             out_came = other_half(result[half_count:])
         elif index == 1:
-            dq, partial, down.came = tie(dq, partial, down.came)
-            down.advance()
-            mod_came = spread([grad_gate_one, grad_shift_two, grad_scale_two, grad_gate_two], codes)
-            dq, partial, out_came, *ready = tie(dq, partial, out_came, down.came)
+            mod_came = spread(
+                [grad_gate_one, grad_shift_two, grad_scale_two, grad_gate_two], (dq, partial)
+            )
         elif index == 2:
-            dq, down.came, up.came, mod_came = tie(dq, down.came, up.came, mod_came)
-            down.advance()
-            up.advance()
+            down.advance((dq,))
+            up.advance((dq,))
+            after = (down.going, up.going, mod_came, out_came)
         elif index == 3:
-            dq, partial, down.came, up.came = tie(dq, partial, down.came, up.came)
-            up.advance()
+            down.advance((dq,))
+            up.advance((dq,))
+            after = (down.going, up.going)
         begin, end = ((0, cut), (cut, frames))[span]
         last = index == len(calls) - 1
         came = None
@@ -1003,7 +1103,7 @@
                 came = add(came, more)
         answer = attention_backward(
             order, dq, None if span == 0 else partial, came, query, pairs[step], grad_attn,
-            attn_heads, log_total, begin, end, last,
+            attn_heads, log_total, begin, end, last, after,
         )
         if last:
             grads = answer[0]
@@ -1011,11 +1111,14 @@
             dq, partial = answer
             if span == 1:
                 arrived.append(pass_on(partial, -step))
-
+    grads = order_after(grads, (down.came, up.came))
     grads_back = swap_groups(grads)
-    product = head_gradients(grads, hidden_all, tables)
+    down.advance((grads,))
+    up.advance((grads,))
+    head_product = head_gradients(grads, hidden_all, tables, (down.going, up.going))
+    head_product = order_after(head_product, (grads_back, down.came, up.came))
     product = lax.all_to_all(
-        product.reshape(devices, D // devices, 3 * lanes),
+        head_product.reshape(devices, D // devices, 3 * lanes),
         everyone, split_axis=0, concat_axis=0, tiled=True,
     )
     product = jnp.sum(
@@ -1023,13 +1126,14 @@
     )
     product = jnp.transpose(product, (2, 1, 0, 3)).reshape(3, D // devices, D)
     grad_source, grad_shift_one, grad_scale_one = input_gradients(
-        grads_back, w_query, w_key, w_value, cosine, sine, source, mod, grad_middle
+        grads_back, w_query, w_key, w_value, cosine, sine, source, mod, grad_middle,
+        (head_product,),
     )
     in_came = other_half(grad_source[half_count:])
-    late_came = spread([grad_shift_one, grad_scale_one], codes)
-
-    grad_down = down.finish().T
-    up_proj = up.finish()
+    late_came = spread([grad_shift_one, grad_scale_one], (product,))
+
+    grad_down = down.finish((grad_source,)).reshape(D, FF // devices).T
+    up_proj = up.finish((grad_source,)).reshape(D // devices, FF + D)
     grad_mod = jnp.concatenate([mod_gradient(late_came), mod_gradient(mod_came)], axis=-1)
     return (
         return_clip(result[:half_count], out_came, LOW),

time: 694 us -> 579 us (0.83)
  waiting for transfers between devices: 172 us -> 54.7 us
  Pallas kernels: 309 us -> 348 us
  other arithmetic: 37.3 us -> 12.5 us
  blocking collectives: 53.5 us -> 30.2 us
  local copies, waits for them, and re-layouts: 32.2 us -> 43.6 us
    pallas_call x6 -> x20, Pallas kernels: 157 us -> 197 us  [the longest x4 139 us: attention_backward(): pl.pallas_call(behind(functools.partial(backward_kernel, first=first, las...]
    ppermute x6 -> x2, waiting for transfers between devices: 36.2 us -> 0.01 us  [flip(): lax.ppermute(array, 'frames', [(i, i ^ 1 << bit) for i in range(frames)])]
    ppermute x4, waiting for transfers between devices: 41.8 us -> 11.5 us  [other_half(): return lax.ppermute(array, 'half', [(0, 1), (1, 0)])]
    all_to_all x4, waiting for transfers between devices: 45.4 us -> 17.5 us  [swap_groups(): lax.all_to_all(grouped, 'frames', split_axis=0, concat_axis=0, tiled=True)]
    all_to_all x1 -> x0, blocking collectives: 23.3 us -> none  [shards(): lax.all_to_all(product.reshape(devices, D // devices, 3 * lanes), everyon...]
    convert_element_type x7 -> x1, other arithmetic: 22.9 us -> 0.62 us  [shards(): codes = embed.astype(WIDE).reshape(devices, D // devices)]
    all_to_all x2, waiting for transfers between devices: 19.8 us -> 2.99 us  [spread(): lax.all_to_all(packed, everyone, split_axis=0, concat_axis=0, tiled=True)]
    all_to_all x2 -> x1, waiting for transfers between devices: 18.9 us -> 3.51 us  [shards(): lax.all_to_all(head_product.reshape(devices, D // devices, 3 * lanes), ev...]
  transfers between devices with their start and end apart: 21 -> 24, of which waited for: 12 -> 9; matrix products, arithmetic and copies ran while one was open for 9% -> 7% of each run, Pallas kernels for 37% -> 53%
where the time goes in v2:
time: 579 us; the launch traced here: 568 us
  Pallas kernels  348 us (60%)
  waiting for transfers between devices  54.7 us (9%)
  starting transfers between devices  54 us (9%)
  local copies, waits for them, and re-layouts  43.6 us (8%)
  blocking collectives  30.2 us (5%)
  between operations  16.4 us (3%)
  other arithmetic  12.5 us (2%)
  matrix products  8.3 us (1%)
    pallas_call x4, Pallas kernels, attention_backward(): pl.pallas_call(behind(functools.partial(backward_kernel, first=first, las...  139 us
    pallas_call x2, Pallas kernels, attention_forward(): pl.pallas_call(functools.partial(forward_kernel, first=first, last=last,...  76.9 us
    pallas_call x8, Pallas kernels, add_halves(): pl.pallas_call(ordered, grid_spec=pltpu.PrefetchScalarGridSpec(num_scalar...  34.2 us
    pallas_call x2, Pallas kernels, weight_gradients(): pl.pallas_call(functools.partial(weights_kernel, keep=keep), grid_spec=pl...  32.7 us
    all_to_all x1, blocking collectives, swap_groups(): lax.all_to_all(grouped, 'frames', split_axis=0, concat_axis=0, tiled=True)  30.2 us
    pallas_call x1, Pallas kernels, middle_block(): pl.pallas_call(middle_kernel, grid=(FF // wide,), out_shape=[of((count, D...  25.1 us
    unnamed x90, local copies, waits for them, and re-layouts  24.8 us
    all_to_all x4, starting transfers between devices, swap_groups(): lax.all_to_all(grouped, 'frames', split_axis=0, concat_axis=0, tiled=True)  17.5 us
  transfers between devices with their start and end apart: 24, of which 9 were waited for; matrix products, arithmetic and copies ran while one was open for 7% of the time, Pallas kernels for 53%

profile of v2, /device:TPU:0, one launch (start us, length us, event | category | flops | bytes accessed | tf_op | source)
XLA Modules:
  0.0 568.2 jit_solution(18076573318941072411)
XLA Ops:
  7.2 2.7 constant_dynamic-slice_fusion
  9.9 4.0 collective-permute-start
  21.5 6.5 %fusion.20.mod.refs_3_.refs_8_ = f32[1,6144]{1,0:T(1,128)S(1)} fusion(bf16[1024,1]{0,1:T(2,128)(2,1)S(1)} %reshape.289, bf16[1024,6144]{1,0:T(8,128)(2,1)} %param.20), kind=kOutput, calls=%fused_computation.59 | convolution fusion | flops 12582912 | bytes 12609536 | tf_op jit(solution)/shard_map/dot_general | solution.py:1017
  27.9 9.3 %collective-permute-done = bf16[256,1024]{1,0:T(8,128)(2,1)} collective-permute-done((bf16[256,1024]{1,0:T(8,128)(2,1)S(1)}, bf16[256,1024]{1,0:T(8,128)(2,1)}, u32[]{:S(2)}, u32[]{:S(2)}) %collective-permute-start) | collective-permute-done | bytes 524320 | tf_op jit(solution)/shard_map/ppermute | solution.py:950
  38.3 9.3 %input_projections.1 = (bf16[512,1024]{1,0:T(8,128)(2,1)S(1)}, bf16[8,512,128]{2,1,0:T(8,128)(2,1)}, bf16[8,2,512,128]{3,2,1,0:T(8,128)(2,1)S(1)}) custom-call(bf16[512,1024]{1,0:T(8,128)(2,1)S(1)} %pad_maximum_fusion.tokens.refs_7_, f32[1,6144]{1,0:T(1,128)S(1)} %fusion.20.mod.refs_3_.refs_8_, bf16[1024,1024]{1,0:T(8,128)(2,1)} %refs_2_.1, ...), custom_call_target="tpu_custom_call" | custom-call | flops 3221225472 | bytes 12582912 | tf_op jit(solution)/shard_map/input_projections/pallas_call | solution.py:434
  47.7 30.2 %all_to_all.53.pair.refs_6_.refs_4_ = bf16[8,2,512,128]{3,2,1,0:T(8,128)(2,1)S(1)} all-to-all(bf16[8,2,512,128]{3,2,1,0:T(8,128)(2,1)S(1)} %get-tuple-element.67), channel_id=1, replica_groups=mesh['frames'=8,'half'=2,'side'=2] {'frames'}, dimensions={0} | all-to-all | bytes 4194304 | tf_op jit(solution)/shard_map/all_to_all | solution.py:958
  77.8 4.2 all-to-all-start
  83.1 4.1 collective-permute-start.1
  87.1 10.4 %all-to-all-done.query.refs_3_.refs_1_.refs_5_ = bf16[8,512,128]{2,1,0:T(8,128)(2,1)} async-done(((bf16[8,512,128]{2,1,0:T(8,128)(2,1)}), bf16[8,512,128]{2,1,0:T(8,128)(2,1)}, u32[]{:S(2)}, u32[]{:S(2)}) %all-to-all-start) | async-done | bytes 1048608 | tf_op jit(solution)/shard_map/all_to_all | solution.py:958
  97.5 36.5 %attention_forward.2 = (s32[1]{0:T(128)}, f32[8,512,128]{2,1,0:T(8,128)}, f32[8,512,128]{2,1,0:T(8,128)}, f32[8,512,128]{2,1,0:T(8,128)}) custom-call(s32[8]{0:T(128)} %get-tuple-element.64.order.refs_2_.refs_0_.refs_4_, s32[1]{0:T(128)} %constant.52.clone.1.flag_in.mine, bf16[8,512,128]{2,1,0:T(8,128)(2,1)} %all-to-all-done.query.refs_3_.refs_1_.refs_5_, ...), custom_call_target="tpu_custom_call" | custom-call | flops 38654705664 | bytes 16777216 | tf_op jit(solution)/shard_map/attention_forward/pallas_call | solution.py:220
  134.0 9.5 %collective-permute-done.1.pair.refs_4_.refs_2_ = bf16[8,2,512,128]{3,2,1,0:T(8,128)(2,1)} collective-permute-done((bf16[8,2,512,128]{3,2,1,0:T(8,128)(2,1)S(1)}, bf16[8,2,512,128]{3,2,1,0:T(8,128)(2,1)}, u32[]{:S(2)}, u32[]{:S(2)}) %collective-permute-start.1) | collective-permute-done | bytes 2097184 | tf_op jit(solution)/shard_map/ppermute | solution.py:961
  143.4 40.5 %attention_forward.3 = (bf16[8,512,128]{2,1,0:T(8,128)(2,1)}, f32[8,8,512]{2,1,0:T(8,128)}) custom-call(s32[8]{0:T(128)} %get-tuple-element.64.order.refs_2_.refs_0_.refs_4_, s32[1]{0:T(128)} %get-tuple-element.68.flag_in, bf16[8,512,128]{2,1,0:T(8,128)(2,1)} %all-to-all-done.query.refs_3_.refs_1_.refs_5_, ...), custom_call_target="tpu_custom_call" | custom-call | flops 38654705664 | bytes 16777216 | tf_op jit(solution)/shard_map/attention_forward/pallas_call | solution.py:220
  183.9 4.4 all-to-all-start.2
  189.9 3.4 copy-done.28
  193.3 6.6 %pull_down.1 = (bf16[512,4096]{1,0:T(8,128)(2,1)S(1)}, bf16[1024,512]{1,0:T(8,128)(2,1)S(1)}) custom-call(bf16[512,1024]{1,0:T(8,128)(2,1)S(1)} %pad_maximum_fusion.1.cotangent.refs_2_, f32[1,6144]{1,0:T(1,128)S(1)} %fusion.20.mod.refs_3_.refs_8_, bf16[4096,1024]{1,0:T(8,128)(2,1)S(1)} %copy-done.28), custom_call_target="tpu_custom_call" | custom-call | flops 4294967296 | bytes 14680064 | tf_op jit(solution)/shard_map/pull_down/pallas_call | solution.py:465
  199.9 2.0 copy-done.29
  203.7 25.1 %middle_block.1 = (f32[512,1024]{1,0:T(8,128)}, bf16[512,1024]{1,0:T(8,128)(2,1)}, bf16[512,4096]{1,0:T(8,128)(2,1)}, bf16[512,4096]{1,0:T(8,128)(2,1)}, f32[512...) custom-call(bf16[8,512,128]{2,1,0:T(8,128)(2,1)} %all-to-all-done.2., ...), custom_call_target="tpu_custom_call" | custom-call | flops 10737418240 | bytes 31457280 | tf_op jit(solution)/shard_map/middle_block/pallas_call | solution.py:547
  228.8 12.2 %weight_gradients.3 = (bf16[4,4,1024,128]{3,2,1,0:T(8,128)(2,1)}, bf16[4,128,5120]{2,1,0:T(8,128)(2,1)}) custom-call(s32[1]{0:T(128)} %bitcast.slot, bf16[512,4096]{1,0:T(8,128)(2,1)} %get-tuple-element.75.active.refs_0_, bf16[512,4096]{1,0:T(8,128)(2,1)} %get-tuple-element.76.grad_up_in, bf16[512,1024]{1,0:T(8,128)(2,1)} %get-tuple-element.77.hidden, ...), custom_call_target="tpu_custom_call" | custom-call | flops 4831838208 | bytes 25165824 | tf_op jit(solution)/shard_map/weight_gradients/pallas_call | solution.py:676
  242.9 4.4 all-to-all-start.3
  248.0 20.5 %weight_gradients.2 = (bf16[512,1024]{1,0:T(8,128)(2,1)}, f32[1,1024]{1,0:T(1,128)}, bf16[4,4,1024,128]{3,2,1,0:T(8,128)(2,1)}, bf16[4,128,5120]{2,1,0:T(8,128)(2,1)}) custom-call(s32[1]{0:T(128)} %bitcast.slot, bf16[512,4096]{1,0:T(8,128)(2,1)} %get-tuple-element.75.active.refs_0_, bf16[512,4096]{1,0:T(8,128)(2,1)} %get-tuple-element.76.grad_up_in, ...), custom_call_target="tpu_custom_call" | custom-call | flops 9126805504 | bytes 25165824 | tf_op jit(solution)/shard_map/weight_gradients/pallas_call | solution.py:676
  271.9 7.8 %add_halves.8 = (bf16[2,4,1024,128]{3,2,1,0:T(8,128)(2,1)}, bf16[2,4,1024,128]{3,2,1,0:T(8,128)(2,1)}) custom-call(s32[1]{0:T(128)} %constant.52.clone.1.flag_in.mine, bf16[2,2,4,1024,128]{4,3,2,1,0:T(8,128)(2,1)} %bitcast.91, bf16[2,2,4,1024,128]{4,3,2,1,0:T(8,128)(2,1)} %bitcast.18.refs_1_.refs_3_, bf16[2,2,4,1024,128]{4,3,2,1,0:T(8,128)(2,1)} %bitcast.92, ...), custom_call_target="tpu_custom_call" | custom-call | flops 2097152 | bytes 12582912 | tf_op jit(solution)/shard_map/add_halves/pallas_call | solution.py:832
  281.7 8.3 %add_halves.9 = (bf16[1,8,32,5120]{3,2,1,0:T(8,128)(2,1)}, bf16[1,8,32,5120]{3,2,1,0:T(8,128)(2,1)}) custom-call(s32[1]{0:T(128)} %constant.52.clone.1.flag_in.mine, bf16[1,2,8,32,5120]{4,3,2,1,0:T(8,128)(2,1)} %bitcast.89, bf16[1,2,8,32,5120]{4,3,2,1,0:T(8,128)(2,1)} %bitcast.21.refs_1_.refs_3_, bf16[1,2,8,32,5120]{4,3,2,1,0:T(8,128)(2,1)} %bitcast.90, ...), custom_call_target="tpu_custom_call" | custom-call | flops 2621440 | bytes 15728640 | tf_op jit(solution)/shard_map/add_halves/pallas_call | solution.py:832
  291.5 37.7 %attention_backward.4 = (f32[8,128,512]{2,1,0:T(8,128)}, bf16[8,2,512,128]{3,2,1,0:T(8,128)(2,1)}) custom-call(bf16[2,2,2,1024,128]{4,3,2,1,0:T(8,128)(2,1)} %bitcast.140, bf16[2,2,2,32,5120]{4,3,2,1,0:T(8,128)(2,1)} %bitcast.138, s32[8]{0:T(128)} %get-tuple-element.64.order.refs_2_.refs_0_.refs_4_, ...), custom_call_target="tpu_custom_call" | custom-call | flops 35232153600 | bytes 16777216 | tf_op jit(solution)/shard_map/attention_backward/pallas_call | solution.py:342
  330.8 2.4 copy.37
  333.2 2.8 all-to-all-start.4
  336.0 30.6 %attention_backward.5 = (f32[8,128,512]{2,1,0:T(8,128)}, bf16[8,2,512,128]{3,2,1,0:T(8,128)(2,1)}) custom-call(s32[8]{0:T(128)} %get-tuple-element.64.order.refs_2_.refs_0_.refs_4_, bf16[8,512,128]{2,1,0:T(8,128)(2,1)} %all-to-all-done.query.refs_3_.refs_1_.refs_5_, bf16[8,2,512,128]{3,2,1,0:T(8,128)(2,1)} %collective-permute-done.1.pair.refs_4_.refs_2_, ...), custom_call_target="tpu_custom_call" | custom-call | flops 25165824000 | bytes 16777216 | tf_op jit(solution)/shard_map/attention_backward/pallas_call | solution.py:342
  369.3 4.2 add_halves.10
  376.4 4.5 add_halves.11
  382.4 38.3 %attention_backward.6 = (f32[8,128,512]{2,1,0:T(8,128)}, bf16[8,2,512,128]{3,2,1,0:T(8,128)(2,1)}) custom-call(bf16[2,2,1024,128]{3,2,1,0:T(8,128)(2,1)} %bitcast.144, bf16[2,2,32,5120]{3,2,1,0:T(8,128)(2,1)} %bitcast.142, f32[32,4128]{1,0:T(8,128)} %bitcast.114, bf16[256,1024]{1,0:T(8,128)(2,1)} %collective-permute-done.3.refs_3_, ...), custom_call_target="tpu_custom_call" | custom-call | flops 35232153600 | bytes 16777216 | tf_op jit(solution)/shard_map/attention_backward/pallas_call | solution.py:342
  420.7 2.4 add_halves.12
  424.7 2.6 add_halves.13
  428.8 32.4 %attention_backward.7.unused_2_ = bf16[8,3,512,128]{3,2,1,0:T(8,128)(2,1)} custom-call(bf16[2,1024,128]{2,1,0:T(8,128)(2,1)} %bitcast.148, bf16[2,32,5120]{2,1,0:T(8,128)(2,1)} %bitcast.146, s32[8]{0:T(128)} %get-tuple-element.64.order.refs_2_.refs_0_.refs_4_, bf16[8,512,128]{2,1,0:T(8,128)(2,1)} %all-to-all-done.query.refs_3_.refs_1_.refs_5_, ...), custom_call_target="tpu_custom_call" | custom-call | flops 25165824000 | bytes 16777216 | tf_op jit(solution)/shard_map/attention_backward/pallas_call | solution.py:342
  462.8 4.5 all-to-all-start.5
  467.3 2.2 add_halves.15
  469.5 2.5 collective-permute-start.14
  472.0 2.2 add_halves.14
  474.7 3.4 copy-done.5
  481.0 7.2 %head_gradients.1.unused_3_ = bf16[1024,384]{1,0:T(8,128)(2,1)S(1)} custom-call(bf16[1024,128]{1,0:T(8,128)(2,1)S(1)} %bitcast.86, bf16[32,5120]{1,0:T(8,128)(2,1)S(1)} %bitcast.84, bf16[8,3,512,128]{3,2,1,0:T(8,128)(2,1)S(1)} %copy-done, bf16[8,1024,512]{2,1,0:T(8,128)(2,1)S(1)} %bitcast.82, f32[512,128]{1,0:T(8,128)S(1)} %copy-done.9, ...), custom_call_target="tpu_custom_call" | custom-call | flops 3221225472 | bytes 12582912 | tf_op jit(solution)/shard_map/head_gradients/pallas_call | solution.py:731
  489.1 9.8 %collective-permute-done.13.unused_1_.refs_2_ = bf16[1024,128]{1,0:T(8,128)(2,1)} collective-permute-done((bf16[1024,128]{1,0:T(8,128)(2,1)}, bf16[1024,128]{1,0:T(8,128)(2,1)}, u32[]{:S(2)}, u32[]{:S(2)}) %collective-permute-start.13) | collective-permute-done | bytes 262176 | tf_op jit(solution)/shard_map/ppermute | solution.py:999
  498.9 6.3 %all-to-all-done.5.unused_0_.refs_1_ = bf16[8,3,512,128]{3,2,1,0:T(8,128)(2,1)} async-done(((bf16[8,3,512,128]{3,2,1,0:T(8,128)(2,1)}), bf16[8,3,512,128]{3,2,1,0:T(8,128)(2,1)}, u32[]{:S(2)}, u32[]{:S(2)}) %all-to-all-start.5) | async-done | bytes 3145760 | tf_op jit(solution)/shard_map/all_to_all | solution.py:958
  505.2 2.9 all-to-all-start.6
  509.7 9.1 %input_gradients.1 = (bf16[512,1024]{1,0:T(8,128)(2,1)S(1)}, f32[1,1024]{1,0:T(1,128)S(1)}, f32[1,1024]{1,0:T(1,128)S(1)}) custom-call(bf16[1024,384]{1,0:T(8,128)(2,1)S(1)} %copy-done.2, bf16[8,3,512,128]{3,2,1,0:T(8,128)(2,1)} %all-to-all-done.5.unused_0_.refs_1_, bf16[1024,1024]{1,0:T(8,128)(2,1)S(1)} %copy-done.12, bf16[1024,1024]{1,0:T(8,128)(2,1)} %refs_3_.1, ...), custom_call_target="tpu_custom_call" | custom-call | flops 3221225472 | bytes 14680064 | tf_op jit(solution)/shard_map/input_gradients/pallas_call | solution.py:788
  519.8 2.7 collective-permute-start.15
  533.4 2.0 copy.43
  535.4 3.5 all-to-all-done.6
  544.7 4.4 all-to-all-start.7
  549.1 2.2 collective-permute-done.15
  556.5 3.0 all-to-all-done.7
  (179 shorter events, 64.3 us)
Async XLA Ops:
  7.2 6.8 %copy-start.40 = (s32[1,2]{1,0:T(1,128)S(1)}, s32[1,2]{1,0:T(1,128)}, u32[]{:S(2)}) copy-start(s32[1,2]{1,0:T(1,128)} %param.13) | copy-start | bytes 28
  7.2 9.2 %copy-start.41 = (s32[8]{0:T(128)S(1)}, s32[8]{0:T(128)}, u32[]{:S(2)}) copy-start(s32[8]{0:T(128)} %param.12) | copy-start | bytes 100
  9.9 27.3 %collective-permute-start = (bf16[256,1024]{1,0:T(8,128)(2,1)S(1)}, bf16[256,1024]{1,0:T(8,128)(2,1)}, u32[]{:S(2)}, u32[]{:S(2)}) collective-permute-start(bf16[256,1024]{1,0:T(8,128)(2,1)S(1)} %bitcast.128), channel_id=1, source_target_pairs={{0,2},{2,0},{1,3},{3,1},{4,6},{6,4},{5,7},{7,5},{8,10},{10,8},{9,1... | collective-permute-start | bytes 1572872 | tf_op jit(solution)/shard_map/ppermute | solution.py:950
  16.6 3.1 copy-start.22
  19.7 18.6 %copy-start.13 = (f32[512,128]{1,0:T(8,128)}, f32[512,128]{1,0:T(8,128)S(1)}, u32[]{:S(2)}) copy-start(f32[512,128]{1,0:T(8,128)S(1)} %broadcast_add_fusion.1.cosine.refs_5_) | copy-start | bytes 786436
  21.4 6.5 %copy-start.10 = (f32[512,128]{1,0:T(8,128)}, f32[512,128]{1,0:T(8,128)S(1)}, u32[]{:S(2)}) copy-start(f32[512,128]{1,0:T(8,128)S(1)} %concatenate.47.refs_5_) | copy-start | bytes 786436
  21.4 16.9 %copy-start.15 = (f32[512,128]{1,0:T(8,128)}, f32[512,128]{1,0:T(8,128)S(1)}, u32[]{:S(2)}) copy-start(f32[512,128]{1,0:T(8,128)S(1)} %broadcast_add_fusion.sine.refs_6_) | copy-start | bytes 786436
  27.9 161.9 %copy-start.20 = (f32[1,6144]{1,0:T(1,128)}, f32[1,6144]{1,0:T(1,128)S(1)}, u32[]{:S(2)}) copy-start(f32[1,6144]{1,0:T(1,128)S(1)} %fusion.20.mod.refs_3_.refs_8_) | copy-start | bytes 73732
  38.3 9.3 %copy-start.6 = (bf16[512,1024]{1,0:T(8,128)(2,1)}, bf16[512,1024]{1,0:T(8,128)(2,1)S(1)}, u32[]{:S(2)}) copy-start(bf16[512,1024]{1,0:T(8,128)(2,1)S(1)} %pad_maximum_fusion.tokens.refs_7_) | copy-start | bytes 3145732
  77.8 19.7 %copy-start.37 = (bf16[8,2,512,128]{3,2,1,0:T(8,128)(2,1)}, bf16[8,2,512,128]{3,2,1,0:T(8,128)(2,1)S(1)}, u32[]{:S(2)}) copy-start(bf16[8,2,512,128]{3,2,1,0:T(8,128)(2,1)S(1)} %all_to_all.53.pair.refs_6_.refs_4_) | copy-start | bytes 6291460
  77.8 19.7 %all-to-all-start = ((bf16[8,512,128]{2,1,0:T(8,128)(2,1)}), bf16[8,512,128]{2,1,0:T(8,128)(2,1)}, u32[]{:S(2)}, u32[]{:S(2)}) async-start(bf16[8,512,128]{2,1,0:T(8,128)(2,1)} %get-tuple-element.66), calls=%async_computation | async-start | bytes 2097152 | tf_op jit(solution)/shard_map/all_to_all | solution.py:958
  83.1 105.7 %collective-permute-start.2 = (bf16[256,1024]{1,0:T(8,128)(2,1)}, bf16[256,1024]{1,0:T(8,128)(2,1)}, u32[]{:S(2)}, u32[]{:S(2)}) collective-permute-start(bf16[256,1024]{1,0:T(8,128)(2,1)} %bitcast.127), channel_id=1, source_target_pairs={{0,2},{2,0},{1,3},{3,1},{4,6},{6,4},{5,7},{7,5},{8,10},{10,8},{9,1... | collective-permute-start | bytes 1572872 | tf_op jit(solution)/shard_map/ppermute | solution.py:950
  83.1 60.4 %collective-permute-start.1 = (bf16[8,2,512,128]{3,2,1,0:T(8,128)(2,1)S(1)}, bf16[8,2,512,128]{3,2,1,0:T(8,128)(2,1)}, u32[]{:S(2)}, u32[]{:S(2)}) collective-permute-start(bf16[8,2,512,128]{3,2,1,0:T(8,128)(2,1)S(1)} %all_to_all.53.pair.refs_6_.refs_4_), channel_id=1, source_target_pairs={{0,1},{1,0},{2,3},{3,2},{4,5},{5,4},{6,7},{7,6},{8,9},{9,8},{10,11... | collective-permute-start | bytes 6291464 | tf_op jit(solution)/shard_map/ppermute | solution.py:961
  183.9 4.8 copy-start.38
  183.9 19.8 %all-to-all-start.2 = ((bf16[8,512,128]{2,1,0:T(8,128)(2,1)}), bf16[8,512,128]{2,1,0:T(8,128)(2,1)}, u32[]{:S(2)}, u32[]{:S(2)}) async-start(bf16[8,512,128]{2,1,0:T(8,128)(2,1)} %get-tuple-element.72.refs_6_.refs_4_.refs_8_), calls=%async_computation.2 | async-start | bytes 2097152 | tf_op jit(solution)/shard_map/all_to_all | solution.py:958
  188.3 286.4 %all-gather.3.cloned.1.call-start = ((), (), s32[]{:S(2)}) async-start(), calls=%async_computation.8 | async-start | bytes 9437184 | tf_op jit(solution)/shard_map/all_gather | solution.py:1034
  189.9 3.4 copy-start.28
  193.3 6.6 %copy-start.17 = (bf16[512,1024]{1,0:T(8,128)(2,1)}, bf16[512,1024]{1,0:T(8,128)(2,1)S(1)}, u32[]{:S(2)}) copy-start(bf16[512,1024]{1,0:T(8,128)(2,1)S(1)} %pad_maximum_fusion.1.cotangent.refs_2_) | copy-start | bytes 3145732
  240.9 40.7 %collective-permute-start.5 = (bf16[4,128,5120]{2,1,0:T(8,128)(2,1)}, bf16[4,128,5120]{2,1,0:T(8,128)(2,1)}, u32[]{:S(2)}, u32[]{:S(2)}) collective-permute-start(bf16[4,128,5120]{2,1,0:T(8,128)(2,1)} %get-tuple-element.88), channel_id=1, source_target_pairs={{0,4},{4,0},{8,12},{12,8},{16,20},{20,16},{24,28},{28,24},{1,5},{5... | collective-permute-start | bytes 15728648 | tf_op jit(solution)/shard_map/ppermute | solution.py:964
  240.9 30.9 %collective-permute-start.4 = (bf16[4,4,1024,128]{3,2,1,0:T(8,128)(2,1)}, bf16[4,4,1024,128]{3,2,1,0:T(8,128)(2,1)}, u32[]{:S(2)}, u32[]{:S(2)}) collective-permute-start(bf16[4,4,1024,128]{3,2,1,0:T(8,128)(2,1)} %get-tuple-element.85), channel_id=1, source_target_pairs={{0,4},{4,0},{8,12},{12,8},{16,20},{20,16},{24,28},{28,24},{1,5},{5... | collective-permute-start | bytes 12582920 | tf_op jit(solution)/shard_map/ppermute | solution.py:964
  242.9 48.5 %all-to-all-start.3 = ((bf16[8,512,128]{2,1,0:T(8,128)(2,1)}), bf16[8,512,128]{2,1,0:T(8,128)(2,1)}, u32[]{:S(2)}, u32[]{:S(2)}) async-start(bf16[8,512,128]{2,1,0:T(8,128)(2,1)} %get-tuple-element.82), calls=%async_computation.3 | async-start | bytes 2097152 | tf_op jit(solution)/shard_map/all_to_all | solution.py:958
  270.4 112.0 %collective-permute-start.3 = (bf16[256,1024]{1,0:T(8,128)(2,1)}, bf16[256,1024]{1,0:T(8,128)(2,1)}, u32[]{:S(2)}, u32[]{:S(2)}) collective-permute-start(bf16[256,1024]{1,0:T(8,128)(2,1)} %slice.51), channel_id=1, source_target_pairs={{0,2},{2,0},{1,3},{3,1},{4,6},{6,4},{5,7},{7,5},{8,10},{10,8},{9,1... | collective-permute-start | bytes 1572872 | tf_op jit(solution)/shard_map/ppermute | solution.py:950
  279.7 89.6 %collective-permute-start.6 = (bf16[2,2,2,1024,128]{4,3,2,1,0:T(8,128)(2,1)}, bf16[2,2,2,1024,128]{4,3,2,1,0:T(8,128)(2,1)}, u32[]{:S(2)}, u32[]{:S(2)}) collective-permute-start(bf16[2,2,2,1024,128]{4,3,2,1,0:T(8,128)(2,1)} %bitcast.139), channel_id=1, source_target_pairs={{0,8},{4,12},{8,0},{12,4},{16,24},{20,28},{24,16},{28,20},{1,9},{5... | collective-permute-start | bytes 6291464 | tf_op jit(solution)/shard_map/ppermute | solution.py:999
  289.9 85.0 %collective-permute-start.7 = (bf16[2,2,2,32,5120]{4,3,2,1,0:T(8,128)(2,1)}, bf16[2,2,2,32,5120]{4,3,2,1,0:T(8,128)(2,1)S(1)}, u32[]{:S(2)}, u32[]{:S(2)}) collective-permute-start(bf16[2,2,2,32,5120]{4,3,2,1,0:T(8,128)(2,1)} %bitcast.137), channel_id=1, source_target_pairs={{0,16},{4,20},{8,24},{12,28},{16,0},{20,4},{24,8},{28,12},{1,17},{... | collective-permute-start | bytes 7864328 | tf_op jit(solution)/shard_map/ppermute | solution.py:999
  333.2 35.3 %all-to-all-start.4 = ((f32[32,1,4128]{2,1,0:T(1,128)}), f32[32,1,4128]{2,1,0:T(1,128)S(1)}, u32[]{:S(2)}, u32[]{:S(2)}) async-start(f32[32,1,4128]{2,1,0:T(1,128)} %copy.37), calls=%async_computation.4 | async-start | bytes 1081344 | tf_op jit(solution)/shard_map/all_to_all | solution.py:1062
  366.6 62.2 %collective-permute-start.12 = (bf16[8,2,512,128]{3,2,1,0:T(8,128)(2,1)}, bf16[8,2,512,128]{3,2,1,0:T(8,128)(2,1)}, u32[]{:S(2)}, u32[]{:S(2)}) collective-permute-start(bf16[8,2,512,128]{3,2,1,0:T(8,128)(2,1)} %get-tuple-element.107), channel_id=1, source_target_pairs={{0,1},{1,0},{2,3},{3,2},{4,5},{5,4},{6,7},{7,6},{8,9},{9,8},{10,11... | collective-permute-start | bytes 6291464 | tf_op jit(solution)/shard_map/ppermute | solution.py:961
  373.5 47.3 %collective-permute-start.8 = (bf16[2,2,1024,128]{3,2,1,0:T(8,128)(2,1)}, bf16[2,2,1024,128]{3,2,1,0:T(8,128)(2,1)}, u32[]{:S(2)}, u32[]{:S(2)}) collective-permute-start(bf16[2,2,1024,128]{3,2,1,0:T(8,128)(2,1)} %bitcast.143), channel_id=1, source_target_pairs={{0,16},{4,20},{8,24},{12,28},{16,0},{20,4},{24,8},{28,12},{1,17},{... | collective-permute-start | bytes 3145736 | tf_op jit(solution)/shard_map/ppermute | solution.py:999
  381.0 42.7 %collective-permute-start.10 = (bf16[2,2,32,5120]{3,2,1,0:T(8,128)(2,1)}, bf16[2,2,32,5120]{3,2,1,0:T(8,128)(2,1)S(1)}, u32[]{:S(2)}, u32[]{:S(2)}) collective-permute-start(bf16[2,2,32,5120]{3,2,1,0:T(8,128)(2,1)} %bitcast.141), channel_id=1, source_target_pairs={{0,8},{4,12},{8,0},{12,4},{16,24},{20,28},{24,16},{28,20},{1,9},{5... | collective-permute-start | bytes 3932168 | tf_op jit(solution)/shard_map/ppermute | solution.py:999
  423.1 38.0 %collective-permute-start.9 = (bf16[2,1024,128]{2,1,0:T(8,128)(2,1)}, bf16[2,1024,128]{2,1,0:T(8,128)(2,1)S(1)}, u32[]{:S(2)}, u32[]{:S(2)}) collective-permute-start(bf16[2,1024,128]{2,1,0:T(8,128)(2,1)} %bitcast.147), channel_id=1, source_target_pairs={{0,1},{1,0},{2,3},{3,2},{4,5},{5,4},{6,7},{7,6},{8,9},{9,8},{10,11... | collective-permute-start | bytes 1572872 | tf_op jit(solution)/shard_map/ppermute | solution.py:999
  427.3 33.9 %collective-permute-start.11 = (bf16[2,32,5120]{2,1,0:T(8,128)(2,1)}, bf16[2,32,5120]{2,1,0:T(8,128)(2,1)S(1)}, u32[]{:S(2)}, u32[]{:S(2)}) collective-permute-start(bf16[2,32,5120]{2,1,0:T(8,128)(2,1)} %bitcast.145), channel_id=1, source_target_pairs={{0,1},{1,0},{2,3},{3,2},{4,5},{5,4},{6,7},{7,6},{8,9},{9,8},{10,11... | collective-permute-start | bytes 1966088 | tf_op jit(solution)/shard_map/ppermute | solution.py:999
  462.8 42.4 %all-to-all-start.5 = ((bf16[8,3,512,128]{3,2,1,0:T(8,128)(2,1)}), bf16[8,3,512,128]{3,2,1,0:T(8,128)(2,1)}, u32[]{:S(2)}, u32[]{:S(2)}) async-start(bf16[8,3,512,128]{3,2,1,0:T(8,128)(2,1)} %order_after.2.refs_0_.refs_2_), calls=%async_computation.5 | async-start | bytes 6291456 | tf_op jit(solution)/shard_map/all_to_all | solution.py:958
  469.5 29.4 %collective-permute-start.14 = (bf16[32,5120]{1,0:T(8,128)(2,1)}, bf16[32,5120]{1,0:T(8,128)(2,1)}, u32[]{:S(2)}, u32[]{:S(2)}) collective-permute-start(bf16[32,5120]{1,0:T(8,128)(2,1)} %bitcast.83), channel_id=1, source_target_pairs={{0,2},{2,0},{1,3},{3,1},{4,6},{6,4},{5,7},{7,5},{8,10},{10,8},{9,1... | collective-permute-start | bytes 983048 | tf_op jit(solution)/shard_map/ppermute | solution.py:999
  474.2 24.6 %collective-permute-start.13 = (bf16[1024,128]{1,0:T(8,128)(2,1)}, bf16[1024,128]{1,0:T(8,128)(2,1)}, u32[]{:S(2)}, u32[]{:S(2)}) collective-permute-start(bf16[1024,128]{1,0:T(8,128)(2,1)} %bitcast.85), channel_id=1, source_target_pairs={{0,2},{2,0},{1,3},{3,1},{4,6},{6,4},{5,7},{7,5},{8,10},{10,8},{9,1... | collective-permute-start | bytes 786440 | tf_op jit(solution)/shard_map/ppermute | solution.py:999
  474.7 3.4 copy-start.5
  489.1 19.0 %copy-start.14 = (f32[512,128]{1,0:T(8,128)S(1)}, f32[512,128]{1,0:T(8,128)}, u32[]{:S(2)}) copy-start(f32[512,128]{1,0:T(8,128)} %copy-done.13) | copy-start | bytes 786436
  489.1 19.0 %copy-start.16 = (f32[512,128]{1,0:T(8,128)S(1)}, f32[512,128]{1,0:T(8,128)}, u32[]{:S(2)}) copy-start(f32[512,128]{1,0:T(8,128)} %copy-done.15) | copy-start | bytes 786436
  489.1 19.0 %copy-start.21 = (f32[1,6144]{1,0:T(1,128)S(1)}, f32[1,6144]{1,0:T(1,128)}, u32[]{:S(2)}) copy-start(f32[1,6144]{1,0:T(1,128)} %copy-done.20) | copy-start | bytes 73732
  505.2 2.9 copy-start.2
  505.2 33.7 %all-to-all-start.6 = ((bf16[32,32,384]{2,1,0:T(8,128)(2,1)}), bf16[32,32,384]{2,1,0:T(8,128)(2,1)S(1)}, u32[]{:S(2)}, u32[]{:S(2)}) async-start(bf16[32,32,384]{2,1,0:T(8,128)(2,1)} %bitcast.81), calls=%async_computation.6 | async-start | bytes 1572864 | tf_op jit(solution)/shard_map/all_to_all | solution.py:1120
  509.7 12.7 %copy-start.39 = (bf16[512,1024]{1,0:T(8,128)(2,1)S(1)}, bf16[512,1024]{1,0:T(8,128)(2,1)}, u32[]{:S(2)}) copy-start(bf16[512,1024]{1,0:T(8,128)(2,1)} %get-tuple-element.81) | copy-start | bytes 3145732
  518.8 5.8 %copy-start.3 = (bf16[512,1024]{1,0:T(8,128)(2,1)}, bf16[512,1024]{1,0:T(8,128)(2,1)S(1)}, u32[]{:S(2)}) copy-start(bf16[512,1024]{1,0:T(8,128)(2,1)S(1)} %get-tuple-element.114.refs_0_) | copy-start | bytes 3145732
  518.8 5.8 %copy-start.26 = (f32[1,1024]{1,0:T(1,128)}, f32[1,1024]{1,0:T(1,128)S(1)}, u32[]{:S(2)}) copy-start(f32[1,1024]{1,0:T(1,128)S(1)} %get-tuple-element.117.refs_1_) | copy-start | bytes 12292
  518.8 5.8 %copy-start.27 = (f32[1,1024]{1,0:T(1,128)}, f32[1,1024]{1,0:T(1,128)S(1)}, u32[]{:S(2)}) copy-start(f32[1,1024]{1,0:T(1,128)S(1)} %get-tuple-element.118.refs_2_) | copy-start | bytes 12292
  519.8 4.9 copy-start.35
  519.8 31.5 %collective-permute-start.15 = (bf16[256,1024]{1,0:T(8,128)(2,1)}, bf16[256,1024]{1,0:T(8,128)(2,1)}, u32[]{:S(2)}, u32[]{:S(2)}) collective-permute-start(bf16[256,1024]{1,0:T(8,128)(2,1)} %slice.53), channel_id=1, source_target_pairs={{0,2},{2,0},{1,3},{3,1},{4,6},{6,4},{5,7},{7,5},{8,10},{10,8},{9,1... | collective-permute-start | bytes 1572872 | tf_op jit(solution)/shard_map/ppermute | solution.py:950
  540.2 11.1 %copy-start.4 = (bf16[512,1024]{1,0:T(8,128)(2,1)S(1)}, bf16[512,1024]{1,0:T(8,128)(2,1)}, u32[]{:S(2)}) copy-start(bf16[512,1024]{1,0:T(8,128)(2,1)} %copy-done.3) | copy-start | bytes 3145732
  544.7 14.8 %all-to-all-start.7 = ((f32[32,1,2080]{2,1,0:T(1,128)}), f32[32,1,2080]{2,1,0:T(1,128)S(1)}, u32[]{:S(2)}, u32[]{:S(2)}) async-start(f32[32,1,2080]{2,1,0:T(1,128)} %copy.42), calls=%async_computation.7 | async-start | bytes 557056 | tf_op jit(solution)/shard_map/all_to_all | solution.py:1062
  553.8 6.1 %copy-start.36 = (f32[32,4096]{1,0:T(8,128)S(1)}, f32[32,4096]{1,0:T(8,128)}, u32[]{:S(2)}) copy-start(f32[32,4096]{1,0:T(8,128)} %fusion) | copy-start | bytes 1572868
  (18 other events, 28.6 us)
Sparse Core Ops, SparseCore 0:
  243.1 80.3 all-gather.2

commit v3 on v2

--- a/solution.py
+++ b/solution.py
@@ -3,6 +3,7 @@
 
 import jax
 import jax.numpy as jnp
+import numpy as np
 from jax import lax
 from jax.experimental import pallas as pl
 from jax.experimental.pallas import tpu as pltpu
@@ -21,6 +22,8 @@
 MIB = 2**20
 SCALE2 = math.log2(math.e) / math.sqrt(HD)
 SAFE_LOG2 = 100.0
+FORWARD_GROUP = 4
+BACKWARD_GROUP = 2
 ROWS_ROWS = (((1,), (1,)), ((), ()))
 ROWS_COLS = (((1,), (0,)), ((), ()))
 SHIFT_ONE, SCALE_ONE, GATE_ONE, SHIFT_TWO, SCALE_TWO, GATE_TWO = range(6)
@@ -76,15 +79,32 @@
     ]
 
 
-def forward_kernel(order, flag_in, query, pair, *refs, first, last, heads):
-    frames, tokens, lanes = query.shape
+def split_sources(refs, parts, own):
+    trios, refs = refs[:parts], refs[parts:]
+    if own:
+        return trios, trios, refs
+    return trios, refs[:parts], refs[parts:]
+
+
+def joined(refs, slot, place):
+    return jnp.concatenate([ref[slot, place] for ref in refs], axis=0)
+
+
+def forward_kernel(order, flag_in, *refs, parts, own, first, last, heads):
+    trios, pairs, refs = split_sources(refs, parts, own)
+    frames, unused, few, lanes = trios[0].shape
+    tokens = few * parts
     if not first:
         num_in, sum_in, top_in = refs[:3]
         refs = refs[3:]
     if last:
-        attn_out, log_out, keys, values = refs
+        attn_out, log_out = refs[:2]
+        refs = refs[2:]
     else:
-        flag_out, num_out, sum_out, top_out, keys, values = refs
+        flag_out, num_out, sum_out, top_out = refs[:4]
+        refs = refs[4:]
+    queries, keys, values, accs = refs
+    group = accs.shape[1] // tokens
     masks = head_masks(tokens, lanes, heads)
     one = jnp.ones((tokens, lanes), LOW)
     zero = jnp.zeros((tokens, lanes), LOW)
@@ -92,17 +112,19 @@
     bound = jnp.float32(0.0)
     q_top = [jnp.float32(0.0)] * heads
     k_top = [jnp.float32(0.0)] * heads
-    for f in range(frames):
-        k = pair[f, 0]
-        v = pair[f, 1]
-        q_top = [jnp.maximum(a, b) for a, b in zip(q_top, square_norm(query[f], masks))]
+    for t in range(frames):
+        slot = order[t]
+        k = joined(pairs, slot, 0)
+        v = joined(pairs, slot, 1)
+        queries[t] = joined(trios, slot, 2)
+        q_top = [jnp.maximum(a, b) for a, b in zip(q_top, square_norm(queries[t], masks))]
         k_top = [jnp.maximum(a, b) for a, b in zip(k_top, square_norm(k, masks))]
         for h in range(heads):
-            keys[h, f] = jnp.where(masks[h], k, zero)
+            keys[h, t] = jnp.where(masks[h], k, zero)
             if heads == 2:
-                values[h, f] = jnp.where(masks[h], v, one)
+                values[h, t] = jnp.where(masks[h], v, one)
             else:
-                values[h, f] = jnp.concatenate([v, one], axis=1)
+                values[h, t] = jnp.concatenate([v, one], axis=1)
     for a, b in zip(q_top, k_top):
         bound = jnp.maximum(bound, a * b)
     fast = bound * (SCALE2 * SCALE2) <= SAFE_LOG2 * SAFE_LOG2
@@ -149,40 +171,49 @@
 
     @pl.when(fast)
     def _():
-        def outer(t, unused):
-            slot = order[t]
-            q = query[slot]
-
-            def inner(j, accs):
-                other = order[j]
-                new = []
+        def outer(g, unused):
+            base = g * group
+            q = queries[pl.ds(base, group)].reshape(group * tokens, lanes)
+            for i in range(group):
+                for h, value in enumerate(start(order[base + i])):
+                    accs[h, i * tokens : (i + 1) * tokens] = value
+
+            def tile(j, skip):
+                rows = slice(skip * tokens, group * tokens)
                 for h in range(heads):
-                    s = dot(q, keys[h, other], ROWS_ROWS)
+                    s = dot(q[rows], keys[h, j], ROWS_ROWS)
                     p = jnp.exp2(s * SCALE2).astype(LOW)
-                    new.append(accs[h] + dot(p, values[h, other]))
-                return new
-
-            store(slot, lax.fori_loop(0, t + 1, inner, start(slot)), None)
+                    accs[h, rows] += dot(p, values[h, j])
+
+            def inner(j, unused):
+                tile(j, 0)
+                return unused
+
+            lax.fori_loop(0, base + 1, inner, 0)
+            for skip in range(1, group):
+                tile(base + skip, skip)
+            for i in range(group):
+                rows = slice(i * tokens, (i + 1) * tokens)
+                store(order[base + i], [accs[h, rows] for h in range(heads)], None)
             return unused
 
-        lax.fori_loop(0, frames, outer, 0)
+        lax.fori_loop(0, frames // group, outer, 0)
 
     @pl.when(jnp.logical_not(fast))
     def _():
         def outer(t, unused):
             slot = order[t]
-            q = query[slot]
+            q = queries[t]
 
             def inner(j, state):
-                other = order[j]
-                accs, tops = state
+                sums, tops = state
                 new_accs, new_tops = [], []
                 for h in range(heads):
-                    s = dot(q, keys[h, other], ROWS_ROWS) * SCALE2
+                    s = dot(q, keys[h, j], ROWS_ROWS) * SCALE2
                     top = jnp.maximum(tops[h], jnp.max(s, axis=1, keepdims=True))
                     p = jnp.exp2(s - top).astype(LOW)
                     keep = jnp.exp2(tops[h] - top)
-                    new_accs.append(accs[h] * keep + dot(p, values[h, other]))
+                    new_accs.append(sums[h] * keep + dot(p, values[h, j]))
                     new_tops.append(top)
                 return new_accs, new_tops
 
@@ -190,24 +221,27 @@
                 tops = [jnp.full((tokens, 1), -1e30, WIDE)] * heads
             else:
                 tops = [top_in[slot][:, h * HD : h * HD + 1] for h in range(heads)]
-            accs, tops = lax.fori_loop(0, t + 1, inner, (start(slot), tops))
+            sums, tops = lax.fori_loop(0, t + 1, inner, (start(slot), tops))
             top = jnp.broadcast_to(tops[0], (tokens, lanes))
             if heads == 2:
                 top = jnp.where(low_lane, top, jnp.broadcast_to(tops[1], (tokens, lanes)))
-            store(slot, accs, top)
+            store(slot, sums, top)
             return unused
 
         lax.fori_loop(0, frames, outer, 0)
 
 
-def attention_forward(order, state, query, pair, last):
-    frames, tokens, lanes = query.shape
+def attention_forward(order, state, trios, pairs, last, after):
+    frames, unused, few, lanes = trios[0].shape
+    parts, own = len(trios), pairs is None
+    tokens = few * parts
+    sources = tuple(trios) + (() if own else tuple(pairs))
     heads = lanes // HD
     first = state is None
-    wide = jax.ShapeDtypeStruct(query.shape, WIDE)
+    wide = jax.ShapeDtypeStruct((frames, tokens, lanes), WIDE)
     if last:
         out_shape = [
-            jax.ShapeDtypeStruct(query.shape, LOW),
+            jax.ShapeDtypeStruct((frames, tokens, lanes), LOW),
             jax.ShapeDtypeStruct((frames, 8, tokens), WIDE),
         ]
         out_specs = [vmem()] * 2
@@ -216,28 +250,37 @@
         out_specs = [smem()] + [vmem()] * 3
     flag = jnp.zeros((1,), jnp.int32) if first else state[0]
     rest = () if first else tuple(state[1:])
-    pairs = heads * frames * (frames + 1) // 2 * tokens * tokens
+    work = heads * frames * (frames + 1) // 2 * tokens * tokens
     return pl.pallas_call(
-        functools.partial(forward_kernel, first=first, last=last, heads=heads),
+        behind(
+            functools.partial(
+                forward_kernel, parts=parts, own=own, first=first, last=last, heads=heads
+            ),
+            len(after),
+        ),
         out_shape=out_shape,
-        in_specs=[smem(), smem()] + [vmem()] * (2 + len(rest)),
+        in_specs=anywhere(len(after)) + [smem(), smem()]
+        + [vmem()] * (len(sources) + len(rest)),
         out_specs=out_specs,
         scratch_shapes=[
+            pltpu.VMEM((frames, tokens, lanes), LOW),
             pltpu.VMEM((heads, frames, tokens, lanes), LOW),
             pltpu.VMEM((heads, frames, tokens, max(lanes, 2 * HD)), LOW),
+            pltpu.VMEM((heads, FORWARD_GROUP * tokens, max(lanes, 2 * HD)), WIDE),
         ],
         compiler_params=pltpu.CompilerParams(vmem_limit_bytes=56 * MIB),
         cost_estimate=pl.CostEstimate(
-            flops=pairs * 4 * HD * 8, bytes_accessed=16 * MIB, transcendentals=pairs
+            flops=work * 4 * HD * 8, bytes_accessed=16 * MIB, transcendentals=work
         ),
         name="attention_forward",
-    )(order, flag, query, pair, *rest)
+    )(*after, order, flag, *sources, *rest)
 
 
 def backward_kernel(
-    order, query, pair, grad, out, lse, *refs, first, last, begin, end, came, heads
+    order, grad, out, lse, *refs, parts, own, first, last, begin, end, came, heads
 ):
-    frames, tokens, lanes = query.shape
+    trios, pairs, refs = split_sources(refs, parts, own)
+    frames, tokens, lanes = grad.shape
     if not first:
         dq_in = refs[0]
         refs = refs[1:]
@@ -248,76 +291,95 @@
         pair_came = refs[0]
         refs = refs[1:]
     if last:
-        final, queries, grads, delta, key_turned, dq_sum = refs
+        final, queries, grads, delta, logs, keys, values, key_turned, dk, dv, dq_sum = refs
         places = (1, 2)
     else:
-        dq_sum, final, queries, grads, delta, key_turned = refs
+        dq_sum, final, queries, grads, delta, logs, keys, values, key_turned, dk, dv = refs
         places = (0, 1)
+    group = dk.shape[0] // tokens
     masks = head_masks(tokens, lanes, heads)
     zero = jnp.zeros((tokens, lanes), LOW)
     lane8 = lax.broadcasted_iota(jnp.int32, (8, lanes), 1) // HD
     pick = jnp.where(lane8 == lax.broadcasted_iota(jnp.int32, (8, lanes), 0), 1.0, 0.0)
-    for f in range(frames):
-        q = query[f]
-        g = grad[f]
+    for t in range(frames):
+        slot = order[t]
+        q = joined(trios, slot, 2)
+        g = grad[slot]
+        k = joined(pairs, slot, 0)
         for h in range(heads):
-            queries[h, f] = jnp.where(masks[h], q, zero)
-            grads[h, f] = jnp.where(masks[h], g, zero)
-        key_turned[f] = pair[f, 0].T
-        delta[f] = exact_dot(
-            pick.astype(WIDE), g.astype(WIDE) * out[f].astype(WIDE), ROWS_ROWS
+            queries[h, t] = jnp.where(masks[h], q, zero)
+            grads[h, t] = jnp.where(masks[h], g, zero)
+        keys[t] = k
+        values[t] = joined(pairs, slot, 1)
+        key_turned[t // group, :, (t % group) * tokens : (t % group + 1) * tokens] = k.T
+        logs[t] = lse[slot]
+        delta[t] = exact_dot(
+            pick.astype(WIDE), g.astype(WIDE) * out[slot].astype(WIDE), ROWS_ROWS
         )
-        dq_sum[f] = jnp.zeros((lanes, tokens), WIDE) if first else dq_in[f]
+        dq_sum[t] = jnp.zeros((lanes, tokens), WIDE) if first else dq_in[t]
         if begin > 0:
             for i in range(2):
-                old = pair_in[f, i]
+                old = pair_in[t, i]
                 if came:
-                    old = (old.astype(WIDE) + pair_came[f, i].astype(WIDE)).astype(LOW)
-                final[f, places[i]] = old
-
-    def outer(t, unused):
-        slot = order[t]
-        k = pair[slot, 0]
-        v = pair[slot, 1]
-        ks = [jnp.where(mask, k, zero) for mask in masks]
-        vs = [jnp.where(mask, v, zero) for mask in masks]
-
-        def inner(j, carry):
-            other = order[j]
-            dk, dv = carry
+                    old = (old.astype(WIDE) + pair_came[t, i].astype(WIDE)).astype(LOW)
+                final[t, places[i]] = old
+    group_masks = head_masks(group * tokens, lanes, heads)
+    group_zero = jnp.zeros((group * tokens, lanes), LOW)
+
+    def outer(index, unused):
+        base = index * group
+        k = keys[pl.ds(base, group)].reshape(group * tokens, lanes)
+        v = values[pl.ds(base, group)].reshape(group * tokens, lanes)
+        ks = [jnp.where(mask, k, group_zero) for mask in group_masks]
+        vs = [jnp.where(mask, v, group_zero) for mask in group_masks]
+        dk[...] = jnp.zeros(dk.shape, WIDE)
+        dv[...] = jnp.zeros(dv.shape, WIDE)
+
+        def tile(j, count):
+            rows = slice(0, count * tokens)
             for h in range(heads):
-                q = queries[h, other]
-                g = grads[h, other]
-                s = dot(ks[h], q, ROWS_ROWS)
-                p = jnp.exp2(s * SCALE2 - lse[other, h : h + 1, :])
-                dp = dot(vs[h], g, ROWS_ROWS)
-                ds = (p * (dp - delta[other, h : h + 1, :])).astype(LOW)
-                dv = dv + dot(p.astype(LOW), g)
-                dk = dk + dot(ds, q)
+                q = queries[h, j]
+                g = grads[h, j]
+                s = dot(ks[h][rows], q, ROWS_ROWS)
+                p = jnp.exp2(s * SCALE2 - logs[j, h : h + 1, :])
+                dp = dot(vs[h][rows], g, ROWS_ROWS)
+                ds = (p * (dp - delta[j, h : h + 1, :])).astype(LOW)
+                dv[rows] += dot(p.astype(LOW), g)
+                dk[rows] += dot(ds, q)
                 span = slice(h * HD, (h + 1) * HD)
-                dq_sum[other, span, :] += dot(key_turned[slot, span, :], ds)
-            return dk, dv
-
-        start = jnp.zeros((tokens, lanes), WIDE)
-        dk, dv = lax.fori_loop(t, frames, inner, (start, start))
-        dk = dk * (1.0 / math.sqrt(HD))
-        if came:
-            dk = dk + pair_came[slot, 0].astype(WIDE)
-            dv = dv + pair_came[slot, 1].astype(WIDE)
-        final[slot, places[0]] = dk.astype(LOW)
-        final[slot, places[1]] = dv.astype(LOW)
+                dq_sum[j, span, :] += dot(key_turned[index, span, rows], ds)
+
+        def inner(j, unused):
+            tile(j, group)
+            return unused
+
+        for count in range(1, group):
+            tile(base + count - 1, count)
+        lax.fori_loop(base + group - 1, frames, inner, 0)
+        for i in range(group):
+            rows = slice(i * tokens, (i + 1) * tokens)
+            slot = order[base + i]
+            part_k = dk[rows] * (1.0 / math.sqrt(HD))
+            part_v = dv[rows]
+            if came:
+                part_k = part_k + pair_came[slot, 0].astype(WIDE)
+                part_v = part_v + pair_came[slot, 1].astype(WIDE)
+            final[slot, places[0]] = part_k.astype(LOW)
+            final[slot, places[1]] = part_v.astype(LOW)
         return unused
 
-    lax.fori_loop(begin, end, outer, 0)
+    lax.fori_loop(begin // group, end // group, outer, 0)
     if last:
-        for f in range(frames):
-            final[f, 0] = (dq_sum[f].T * (1.0 / math.sqrt(HD))).astype(LOW)
+        for t in range(frames):
+            final[order[t], 0] = (dq_sum[t].T * (1.0 / math.sqrt(HD))).astype(LOW)
 
 
 def attention_backward(
-    order, dq, partial, came, query, pair, grad, out, lse, begin, end, last, after
+    order, dq, partial, came, trios, pairs, grad, out, lse, begin, end, last, after
 ):
-    frames, tokens, lanes = query.shape
+    frames, tokens, lanes = grad.shape
+    parts, own = len(trios), pairs is None
+    sources = tuple(trios) + (() if own else tuple(pairs))
     heads = lanes // HD
     first = dq is None
     sums = (frames, lanes, tokens)
@@ -330,7 +392,12 @@
         pltpu.VMEM((heads, frames, tokens, lanes), LOW),
         pltpu.VMEM((heads, frames, tokens, lanes), LOW),
         pltpu.VMEM((frames, 8, tokens), WIDE),
-        pltpu.VMEM((frames, lanes, tokens), LOW),
+        pltpu.VMEM((frames, 8, tokens), WIDE),
+        pltpu.VMEM((frames, tokens, lanes), LOW),
+        pltpu.VMEM((frames, tokens, lanes), LOW),
+        pltpu.VMEM((frames // BACKWARD_GROUP, lanes, BACKWARD_GROUP * tokens), LOW),
+        pltpu.VMEM((BACKWARD_GROUP * tokens, lanes), WIDE),
+        pltpu.VMEM((BACKWARD_GROUP * tokens, lanes), WIDE),
     ]
     if last:
         out_shape = [jax.ShapeDtypeStruct((frames, 3, tokens, lanes), LOW)]
@@ -342,13 +409,14 @@
     return pl.pallas_call(
         behind(
             functools.partial(
-                backward_kernel, first=first, last=last, begin=begin, end=end,
-                came=came is not None, heads=heads,
+                backward_kernel, parts=parts, own=own, first=first, last=last, begin=begin,
+                end=end, came=came is not None, heads=heads,
             ),
             len(after),
         ),
         out_shape=out_shape,
-        in_specs=anywhere(len(after)) + [smem()] + [vmem()] * (5 + len(extra)),
+        in_specs=anywhere(len(after)) + [smem()]
+        + [vmem()] * (3 + len(sources) + len(extra)),
         out_specs=[vmem()] * len(out_shape),
         scratch_shapes=scratch,
         compiler_params=pltpu.CompilerParams(vmem_limit_bytes=56 * MIB),
@@ -356,7 +424,7 @@
             flops=work * 10 * HD * 5, bytes_accessed=16 * MIB, transcendentals=work
         ),
         name="attention_backward",
-    )(*after, order, query, pair, grad, out, lse, *extra)
+    )(*after, order, grad, out, lse, *sources, *extra)
 
 
 def normalize(values):
@@ -404,13 +472,13 @@
     return pieces[0] if len(pieces) == 1 else jnp.concatenate(pieces, axis=1)
 
 
-def input_kernel(tokens, mod, w_query, w_key, w_value, cosine, sine, hidden, query, pair):
+def input_kernel(tokens, mod, w_query, w_key, w_value, cosine, sine, hidden, trio):
     @pl.when(pl.program_id(0) == 0)
     def _():
         normed, unused = normalize(tokens[...].astype(WIDE))
         hidden[...] = (normed * (1.0 + part(mod, SCALE_ONE)) + part(mod, SHIFT_ONE)).astype(LOW)
 
-    groups, unused, lanes = query.shape
+    groups, unused, unused, lanes = trio.shape
     h = hidden[...]
     cos, sin = cosine[...], sine[...]
     k = turned(dot(h, w_key[...]), cos, sin).astype(LOW)
@@ -418,9 +486,9 @@
     q = turned(dot(h, w_query[...]), cos, sin).astype(LOW)
     for g in range(groups):
         span = slice(g * lanes, (g + 1) * lanes)
-        pair[g, 0] = k[:, span]
-        pair[g, 1] = v[:, span]
-        query[g] = q[:, span]
+        trio[g, 0] = k[:, span]
+        trio[g, 1] = v[:, span]
+        trio[g, 2] = q[:, span]
 
 
 def input_projections(tokens, mod, w_query, w_key, w_value, cosine, sine, frames):
@@ -429,19 +497,17 @@
     wide = 256
     groups = wide // lanes
     weight = pl.BlockSpec((D, wide), lambda c: (0, c))
-    heads = pl.BlockSpec((groups, count, lanes), lambda c: (c, 0, 0))
-    pairs = pl.BlockSpec((groups, 2, count, lanes), lambda c: (c, 0, 0, 0))
+    trio = pl.BlockSpec((groups, 3, count, lanes), lambda c: (c, 0, 0, 0))
     return pl.pallas_call(
         input_kernel,
         grid=(D // wide,),
         out_shape=[
             jax.ShapeDtypeStruct((count, D), LOW),
-            jax.ShapeDtypeStruct((frames, count, lanes), LOW),
-            jax.ShapeDtypeStruct((frames, 2, count, lanes), LOW),
+            jax.ShapeDtypeStruct((frames, 3, count, lanes), LOW),
         ],
         in_specs=[whole((count, D)), whole((1, 6 * D)), weight, weight, weight]
         + [whole(cosine.shape)] * 2,
-        out_specs=[whole((count, D)), heads, pairs],
+        out_specs=[whole((count, D)), trio],
         compiler_params=pltpu.CompilerParams(vmem_limit_bytes=48 * MIB),
         cost_estimate=pl.CostEstimate(
             flops=6 * count * D * D, bytes_accessed=12 * MIB, transcendentals=0
@@ -689,20 +755,22 @@
     )(*args)
 
 
-def turn_kernel(hidden, target):
-    target[...] = hidden[...].T
-
-
-def turn_hidden(hidden):
+def turn_kernel(*refs):
+    *parts, target = refs
+    target[...] = jnp.concatenate([part[...] for part in parts], axis=0).T
+
+
+def turn_hidden(parts):
+    count = sum(part.shape[0] for part in parts)
     return pl.pallas_call(
         turn_kernel,
-        out_shape=jax.ShapeDtypeStruct(hidden.shape[::-1], LOW),
-        in_specs=[vmem()],
+        out_shape=jax.ShapeDtypeStruct((D, count), LOW),
+        in_specs=[vmem()] * len(parts),
         out_specs=vmem(),
         compiler_params=pltpu.CompilerParams(vmem_limit_bytes=32 * MIB),
         cost_estimate=pl.CostEstimate(flops=0, bytes_accessed=2 * MIB, transcendentals=0),
         name="turn_hidden",
-    )(hidden)
+    )(*parts)
 
 
 def head_kernel(grads, hidden, cosine, sine, time_cosine, time_sine, product, total):
@@ -805,15 +873,16 @@
 
 
 def halves_kernel(mine, keep_give, came_give, keep_hold, came_hold, give, hold):
-    give[0, 0] = (keep_give[0, 0, 0].astype(WIDE) + came_give[0, 0, 0].astype(WIDE)).astype(LOW)
-    hold[0, 0] = (keep_hold[0, 0, 0].astype(WIDE) + came_hold[0, 0, 0].astype(WIDE)).astype(LOW)
+    give[0] = (keep_give[0, 0].astype(WIDE) + came_give[0, 0].astype(WIDE)).astype(LOW)
+    hold[0] = (keep_hold[0, 0].astype(WIDE) + came_hold[0, 0].astype(WIDE)).astype(LOW)
 
 
 def add_halves(keep, came, axis, mine, after):
     shape = keep.shape
     lead, trail = math.prod(shape[:axis]), math.prod(shape[axis + 1 : -2])
     rest = shape[:axis] + shape[axis + 1 :]
-    block = (1, 1, 1) + shape[-2:]
+    many = 2 if trail % 2 == 0 else 1
+    block = (1, 1, many) + shape[-2:]
     view = (lead, 2, trail) + shape[-2:]
 
     def part_of(other):
@@ -822,7 +891,7 @@
 
         return pl.BlockSpec(block, index)
 
-    out = pl.BlockSpec((1, 1) + shape[-2:], lambda a, b, *unused: (a, b, 0, 0))
+    out = pl.BlockSpec((1, many) + shape[-2:], lambda a, b, *unused: (a, b, 0, 0))
     out_shape = jax.ShapeDtypeStruct((lead, trail) + shape[-2:], LOW)
 
     def ordered(mine, *refs):
@@ -833,7 +902,7 @@
         ordered,
         grid_spec=pltpu.PrefetchScalarGridSpec(
             num_scalar_prefetch=1,
-            grid=(lead, trail),
+            grid=(lead, trail // many),
             in_specs=anywhere(len(after)) + [part_of(True)] * 2 + [part_of(False)] * 2,
             out_specs=[out, out],
         ),
@@ -894,31 +963,56 @@
     )(*after, *vectors, codes)
 
 
+def rotary_rates(lanes):
+    rates, parts, signs = [], [], []
+    for index, size in enumerate((HD // 4, 3 * HD // 8, 3 * HD // 8)):
+        half = size // 2
+        rate = 10000.0 ** (-np.arange(half, dtype=np.float32) / np.float32(half))
+        rates += [rate, rate]
+        parts += [np.full(size, index)]
+        signs += [-np.ones(half), np.ones(half)]
+    rows = [np.concatenate(rows).astype(np.float32) for rows in (rates, parts, signs)]
+    return np.tile(np.stack(rows), (1, lanes // HD))
+
+
+def tables_kernel(places, times, rates, place_cosine, place_sine, time_cosine, time_sine, cosine, sine, *, local):
+    count, lanes = cosine.shape
+    frames = time_cosine.shape[0]
+    rate, parts, sign = rates[0:1], rates[1:2], rates[2:3]
+    token = lax.broadcasted_iota(jnp.int32, (count, lanes), 0)
+    few = local * PC
+    row = jnp.where(token < few, places[0], places[1] - local) + token // PC
+    spot = jnp.where(parts == 1.0, row, token % PC).astype(WIDE)
+    timed = parts == 0.0
+    cos = jnp.where(timed, 0.0, jnp.cos(spot * rate))
+    sin = jnp.where(timed, 0.0, jnp.sin(spot * rate) * sign)
+    place_cosine[...] = cos
+    place_sine[...] = sin
+    for f in range(frames):
+        angle = times[f].astype(WIDE) * rate
+        time_cosine[f] = jnp.where(timed, jnp.cos(angle), 0.0)
+        time_sine[f] = jnp.where(timed, jnp.sin(angle) * sign, 0.0)
+    cosine[...] = cos + time_cosine[places[2]]
+    sine[...] = sin + time_sine[places[2]]
+
+
+def rotary_tables(places, times, count, local, lanes):
+    flat = jax.ShapeDtypeStruct((count, lanes), WIDE)
+    timed = jax.ShapeDtypeStruct((times.shape[0], 1, lanes), WIDE)
+    return pl.pallas_call(
+        functools.partial(tables_kernel, local=local),
+        out_shape=[flat, flat, timed, timed, flat, flat],
+        in_specs=[smem(), smem(), vmem()],
+        out_specs=[vmem()] * 6,
+        name="rotary_tables",
+    )(places, times, jnp.asarray(rotary_rates(lanes)))
+
+
 def sinusoid(levels):
     half_size = D // 2
     freq_table = 10000.0 ** (-jnp.arange(half_size, dtype=WIDE) / half_size)
     angle_table = levels.astype(WIDE)[..., None] * freq_table
     return jnp.concatenate([jnp.cos(angle_table), jnp.sin(angle_table)], axis=-1)
-
-
-def turn_tables(positions, heads):
-    count = next(position.shape[0] for position in positions if position is not None)
-    cosines, sines = [], []
-    for position, part_size in zip(positions, (HD // 4, 3 * HD // 8, 3 * HD // 8)):
-        half_size = part_size // 2
-        if position is None:
-            cosine = sine = jnp.zeros((count, half_size), WIDE)
-        else:
-            freq_table = 10000.0 ** (-jnp.arange(half_size, dtype=WIDE) / half_size)
-            angle_table = position[:, None] * freq_table
-            cosine = jnp.cos(angle_table)
-            sine = jnp.sin(angle_table)
-        cosines += [cosine, cosine]
-        sines += [-sine, sine]
-    return (
-        jnp.concatenate(cosines * heads, axis=-1),
-        jnp.concatenate(sines * heads, axis=-1),
-    )
 
 
 def shards(
@@ -936,12 +1030,8 @@
     clips = block_in.shape[1]
     local_rows = block_in.shape[2]
     lanes = D // frames
-    heads = max(lanes // HD, 1)
     order = jnp.argsort(block_map).astype(jnp.int32)
     slot = frame_slot.astype(jnp.int32).reshape(1)
-
-    def tie(*arrays):
-        return lax.optimization_barrier(arrays)
 
     def clip_tokens(tokens, clip):
         return lax.dynamic_index_in_dim(tokens[0], clip, 0, keepdims=False).reshape(-1, D)
@@ -1007,8 +1097,6 @@
 
     source_own = clip_tokens(block_in, half)
     source_came = other_half(clip_tokens(block_in, 1 - half))
-    grad_going, source_came = tie(clip_tokens(cotangent, 1 - half), source_came)
-    grad_came = other_half(grad_going)
     source = jnp.concatenate([source_own, source_came])
     half_count = source_own.shape[0]
 
@@ -1016,29 +1104,32 @@
     embed = jax.nn.silu(sinusoid(level)).astype(LOW)
     mod = jnp.dot(embed, w_mod, preferred_element_type=WIDE)
 
-    blocks = jnp.stack([half, 1 - half])[:, None, None]
-    rows = (blocks * sides + side) * local_rows + jnp.arange(local_rows)[None, :, None]
-    row_pos = jnp.broadcast_to(rows, (clips, local_rows, PC)).reshape(-1).astype(WIDE)
-    col_pos = jnp.broadcast_to(jnp.arange(PC), (clips, local_rows, PC)).reshape(-1).astype(WIDE)
-    place_cosine, place_sine = turn_tables((None, row_pos, col_pos), heads)
-    time_cosine, time_sine = turn_tables((block_map.astype(WIDE), None, None), heads)
-    cosine = place_cosine + time_cosine[frame_slot]
-    sine = place_sine + time_sine[frame_slot]
-    tables = (place_cosine, place_sine, time_cosine[:, None], time_sine[:, None])
-
-    hidden_one, query, pair = input_projections(
-        source, mod, w_query, w_key, w_value, cosine, sine, frames
-    )
-    pair = swap_groups(pair)
-    query = swap_groups(query)
-    hidden_all = lax.all_gather(turn_hidden(hidden_one), "frames", axis=0)
+    places = jnp.stack(
+        [(half * sides + side) * local_rows, ((1 - half) * sides + side) * local_rows, frame_slot]
+    ).astype(jnp.int32)
+    tables = rotary_tables(places, block_map, 2 * half_count, local_rows, max(lanes, HD))
+    cosine, sine = tables[4:]
+    tables = tables[:4]
+
+    hidden, trios = [], []
+    for at, tokens in ((0, source_own), (half_count, source_came)):
+        rows = slice(at, at + half_count)
+        h, trio = input_projections(
+            tokens, mod, w_query, w_key, w_value, cosine[rows], sine[rows], frames
+        )
+        hidden.append(h)
+        trios.append(swap_groups(order_after(trio, (source_came,)) if at == 0 else trio))
+    hidden_all = lax.all_gather(turn_hidden(hidden), "frames", axis=0)
+    pairs = [None] + [
+        [pass_on(trio[:, :2], step) for trio in trios] for step in range(1, sides)
+    ]
+    state = None
+    passed = tuple(trios) if sides == 1 else tuple(pairs[-1])
+    grad_came = other_half(order_after(clip_tokens(cotangent, 1 - half), passed))
     grad_result = jnp.concatenate([clip_tokens(cotangent, half), grad_came])
     pulled, scaled_turned = pull_down(grad_result, mod, w_down)
-
-    pairs = [pair] + [pass_on(pair, step) for step in range(1, sides)]
-    state = None
     for step in range(sides):
-        state = attention_forward(order, state, query, pairs[step], step == sides - 1)
+        state = attention_forward(order, state, trios, pairs[step], step == sides - 1, ())
     attn_heads, log_total = state
     attn = swap_groups(attn_heads)
 
@@ -1061,19 +1152,15 @@
         packed = pack(vectors, codes, after)
         return lax.all_to_all(packed, everyone, split_axis=0, concat_axis=0, tiled=True)
 
-    def mod_gradient(came):
-        share_of = D // devices
-        return jnp.einsum(
-            "nd,ne->de",
-            came[:, -share_of:],
-            came[:, :-share_of],
-            precision=lax.Precision.HIGHEST,
+    def mod_gradient(codes, vectors):
+        return lax.dot_general(
+            codes, vectors, (((0,), (0,)), ((), ())), precision=lax.Precision.HIGHEST
         )
 
     codes = embed.astype(WIDE).reshape(devices, D // devices)
     dq = None
     arrived = []
-    cut = frames * 3 // 8
+    cut = max(frames // 4 // BACKWARD_GROUP, 1) * BACKWARD_GROUP
     calls = [(step, span) for step in range(sides - 1, -1, -1) for span in (0, 1)]
     for index, (step, span) in enumerate(calls):
         after = ()
@@ -1102,7 +1189,7 @@
             for more in arrived[1:]:
                 came = add(came, more)
         answer = attention_backward(
-            order, dq, None if span == 0 else partial, came, query, pairs[step], grad_attn,
+            order, dq, None if span == 0 else partial, came, trios, pairs[step], grad_attn,
             attn_heads, log_total, begin, end, last, after,
         )
         if last:
@@ -1121,24 +1208,33 @@
         head_product.reshape(devices, D // devices, 3 * lanes),
         everyone, split_axis=0, concat_axis=0, tiled=True,
     )
-    product = jnp.sum(
-        product.reshape(frames, row_total, D // devices, 3, lanes).astype(WIDE), axis=1
-    )
-    product = jnp.transpose(product, (2, 1, 0, 3)).reshape(3, D // devices, D)
     grad_source, grad_shift_one, grad_scale_one = input_gradients(
         grads_back, w_query, w_key, w_value, cosine, sine, source, mod, grad_middle,
         (head_product,),
     )
     in_came = other_half(grad_source[half_count:])
-    late_came = spread([grad_shift_one, grad_scale_one], (product,))
+    total = jnp.sum(
+        product.reshape(frames, row_total, D // devices, 3, lanes).astype(WIDE), axis=1
+    )
+    total = jnp.transpose(total, (2, 1, 0, 3)).reshape(3, D // devices, D)
+    late = jnp.concatenate([grad_shift_one, grad_scale_one], axis=-1).reshape(1, -1, 128)
+    late = jnp.broadcast_to(late, (devices,) + late.shape[1:])
+    late_came = lax.all_to_all(order_after(late, (product,)), everyone, split_axis=0, concat_axis=0, tiled=True)
+    all_codes = mod_came[:, 4 * D :]
 
     grad_down = down.finish((grad_source,)).reshape(D, FF // devices).T
     up_proj = up.finish((grad_source,)).reshape(D // devices, FF + D)
-    grad_mod = jnp.concatenate([mod_gradient(late_came), mod_gradient(mod_came)], axis=-1)
+    grad_mod = jnp.concatenate(
+        [
+            mod_gradient(all_codes, late_came.reshape(devices, 2 * D)),
+            mod_gradient(all_codes, mod_came[:, : 4 * D]),
+        ],
+        axis=-1,
+    )
     return (
         return_clip(result[:half_count], out_came, LOW),
         return_clip(grad_source[:half_count], in_came, WIDE),
-        product[0], product[1], product[2],
+        total[0], total[1], total[2],
         up_proj[:, FF:], up_proj[:, :FF], grad_down, grad_mod,
     )
 

time: 579 us -> 542 us (0.936)
  blocking collectives: 30.2 us -> 0 us
  Pallas kernels: 348 us -> 322 us
  waiting for transfers between devices: 54.7 us -> 69.1 us
    all_to_all x1 -> x0, blocking collectives: 30.2 us -> none  [swap_groups(): lax.all_to_all(grouped, 'frames', split_axis=0, concat_axis=0, tiled=True)]
    pallas_call x7 -> x8, Pallas kernels: 217 us -> 196 us  [the longest x4 131 us: attention_backward(): pl.pallas_call(behind(functools.partial(backward_kernel, parts=parts, own...]
    all_to_all x4 -> x5, waiting for transfers between devices: 17.5 us -> 38.4 us  [swap_groups(): lax.all_to_all(grouped, 'frames', split_axis=0, concat_axis=0, tiled=True)]
    ppermute x2 -> x3, waiting for transfers between devices: 9.47 us -> 0.57 us  [pass_on(): lax.ppermute(array, 'side', [(i, (i + step) % sides) for i in range(sides)])]
    unnamed x90 -> x87, local copies, waits for them, and re-layouts: 24.8 us -> 28.8 us
    all_to_all x4 -> x5, starting transfers between devices: 17.5 us -> 20.7 us  [swap_groups(): lax.all_to_all(grouped, 'frames', split_axis=0, concat_axis=0, tiled=True)]
  transfers between devices with their start and end apart: 24 -> 26, of which waited for: 9 -> 10; matrix products, arithmetic and copies ran while one was open for 7% -> 7% of each run, Pallas kernels for 53% -> 53%
where the time goes in v3:
time: 542 us; the launch traced here: 533 us
  Pallas kernels  322 us (59%)
  waiting for transfers between devices  69.1 us (13%)
  starting transfers between devices  58.6 us (11%)
  local copies, waits for them, and re-layouts  48.8 us (9%)
  between operations  16.1 us (3%)
  other arithmetic  10.8 us (2%)
  matrix products  7.49 us (1%)
    pallas_call x4, Pallas kernels, attention_backward(): pl.pallas_call(behind(functools.partial(backward_kernel, parts=parts, own...  131 us
    pallas_call x2, Pallas kernels, attention_forward(): pl.pallas_call(behind(functools.partial(forward_kernel, parts=parts, own=...  61.1 us
    all_to_all x5, waiting for transfers between devices, swap_groups(): lax.all_to_all(grouped, 'frames', split_axis=0, concat_axis=0, tiled=True)  38.4 us
    pallas_call x2, Pallas kernels, weight_gradients(): pl.pallas_call(functools.partial(weights_kernel, keep=keep), grid_spec=pl...  32.3 us
    pallas_call x8, Pallas kernels, add_halves(): pl.pallas_call(ordered, grid_spec=pltpu.PrefetchScalarGridSpec(num_scalar...  29.2 us
    unnamed x87, local copies, waits for them, and re-layouts  28.8 us
    pallas_call x1, Pallas kernels, middle_block(): pl.pallas_call(middle_kernel, grid=(FF // wide,), out_shape=[of((count, D...  25.1 us
    all_to_all x5, starting transfers between devices, swap_groups(): lax.all_to_all(grouped, 'frames', split_axis=0, concat_axis=0, tiled=True)  20.7 us
  transfers between devices with their start and end apart: 26, of which 10 were waited for; matrix products, arithmetic and copies ran while one was open for 7% of the time, Pallas kernels for 53%

profile of v3, /device:TPU:0, one launch (start us, length us, event | category | flops | bytes accessed | tf_op | source)
XLA Modules:
  0.0 532.9 jit_solution(18258768840029118488)
XLA Ops:
  7.2 2.7 constant_dynamic-slice_fusion.1
  9.9 4.0 collective-permute-start
  15.9 6.5 %fusion.16.mod.refs_3_.refs_8_ = f32[1,6144]{1,0:T(1,128)S(1)} fusion(bf16[1024,1]{0,1:T(2,128)(2,1)S(1)} %reshape.217, bf16[1024,6144]{1,0:T(8,128)(2,1)} %param.21), kind=kOutput, calls=%fused_computation.41 | convolution fusion | flops 12582912 | bytes 12609536 | tf_op jit(solution)/shard_map/dot_general | solution.py:1105
  23.0 2.8 rotary_tables.1
  26.9 5.7 %input_projections.2 = (bf16[256,1024]{1,0:T(8,128)(2,1)S(1)}, bf16[8,3,256,128]{3,2,1,0:T(8,128)(2,1)S(1)}) custom-call(bf16[256,1024]{1,0:T(8,128)(2,1)S(1)} %bitcast.76, f32[1,6144]{1,0:T(1,128)S(1)} %fusion.16.mod.refs_3_.refs_8_, bf16[1024,1024]{1,0:T(8,128)(2,1)S(1)} %copy-done.1, bf16[1024,1024]{1,0:T(8,128)(2,1)} %refs_3_.1, ...), custom_call_target="tpu_custom_call" | custom-call | flops 1610612736 | bytes 12582912 | tf_op jit(solution)/shard_map/input_projections/pallas_call | solution.py:501
  34.5 2.8 collective-permute-done.unused_0_.tokens
  38.1 4.4 all-to-all-start
  42.5 5.7 %input_projections.3 = (bf16[256,1024]{1,0:T(8,128)(2,1)S(1)}, bf16[8,3,256,128]{3,2,1,0:T(8,128)(2,1)S(1)}) custom-call(bf16[256,1024]{1,0:T(8,128)(2,1)S(1)} %copy-done.10, f32[1,6144]{1,0:T(1,128)S(1)} %fusion.16.mod.refs_3_.refs_8_, bf16[1024,1024]{1,0:T(8,128)(2,1)S(1)} %copy-done.1, bf16[1024,1024]{1,0:T(8,128)(2,1)} %refs_3_.1, ...), custom_call_target="tpu_custom_call" | custom-call | flops 1610612736 | bytes 12582912 | tf_op jit(solution)/shard_map/input_projections/pallas_call | solution.py:501
  50.2 13.4 %all-to-all-done.refs_2_.refs_6_.refs_4_.refs_8_ = bf16[8,3,256,128]{3,2,1,0:T(8,128)(2,1)} async-done(((bf16[8,3,256,128]{3,2,1,0:T(8,128)(2,1)}), bf16[8,3,256,128]{3,2,1,0:T(8,128)(2,1)}, u32[]{:S(2)}, u32[]{:S(2)}) %all-to-all-start) | async-done | bytes 1572896 | tf_op jit(solution)/shard_map/all_to_all | solution.py:1048
  63.6 3.6 all-to-all-start.1
  68.2 2.3 slice.79
  71.4 16.8 %all-to-all-done.1.refs_3_.refs_7_.refs_5_.refs_9_ = bf16[8,3,256,128]{3,2,1,0:T(8,128)(2,1)S(1)} async-done(((bf16[8,3,256,128]{3,2,1,0:T(8,128)(2,1)}), bf16[8,3,256,128]{3,2,1,0:T(8,128)(2,1)S(1)}, u32[]{:S(2)}, u32[]{:S(2)}) %all-to-all-start.1) | async-done | bytes 1572896 | tf_op jit(solution)/shard_map/all_to_all | solution.py:1048
  89.3 28.9 %attention_forward.2 = (s32[1]{0:T(128)}, f32[8,512,128]{2,1,0:T(8,128)}, f32[8,512,128]{2,1,0:T(8,128)}, f32[8,512,128]{2,1,0:T(8,128)}) custom-call(s32[8]{0:T(128)} %get-tuple-element.69.refs_0_.refs_2_.refs_4_, s32[1]{0:T(128)} %constant.41.clone.1.refs_1_.mine, bf16[8,3,256,128]{3,2,1,0:T(8,128)(2,1)} %all-to-all-done.refs_2_.refs_6_.refs_4_.refs_8_, ...), custom_call_target="tpu_custom_call" | custom-call | flops 38654705664 | bytes 16777216 | tf_op jit(solution)/shard_map/attention_forward/pallas_call | solution.py:254
  118.7 2.6 collective-permute-start.3
  121.4 32.2 %attention_forward.3 = (bf16[8,512,128]{2,1,0:T(8,128)(2,1)}, f32[8,8,512]{2,1,0:T(8,128)}) custom-call(s32[8]{0:T(128)} %get-tuple-element.69.refs_0_.refs_2_.refs_4_, s32[1]{0:T(128)} %get-tuple-element.74.refs_1_, bf16[8,3,256,128]{3,2,1,0:T(8,128)(2,1)} %all-to-all-done.refs_2_.refs_6_.refs_4_.refs_8_, bf16[8,3,256,128]{3,2,1,0:T(8,128)(2,1)} %copy-done.35, ...), custom_call_target="tpu_custom_call" | custom-call | flops 38654705664 | bytes 16777216 | tf_op jit(solution)/shard_map/attention_forward/pallas_call | solution.py:254
  153.6 3.7 all-to-all-start.2
  158.7 3.4 copy-done.28
  162.1 6.6 %pull_down.1 = (bf16[512,4096]{1,0:T(8,128)(2,1)S(1)}, bf16[1024,512]{1,0:T(8,128)(2,1)S(1)}) custom-call(bf16[512,1024]{1,0:T(8,128)(2,1)S(1)} %pad_maximum_fusion.1.cotangent.refs_2_, f32[1,6144]{1,0:T(1,128)S(1)} %fusion.16.mod.refs_3_.refs_8_, bf16[4096,1024]{1,0:T(8,128)(2,1)S(1)} %copy-done.28), custom_call_target="tpu_custom_call" | custom-call | flops 4294967296 | bytes 14680064 | tf_op jit(solution)/shard_map/pull_down/pallas_call | solution.py:531
  173.8 25.1 %middle_block.1 = (f32[512,1024]{1,0:T(8,128)}, bf16[512,1024]{1,0:T(8,128)(2,1)}, bf16[512,4096]{1,0:T(8,128)(2,1)}, bf16[512,4096]{1,0:T(8,128)(2,1)}, f32[512...) custom-call(bf16[8,512,128]{2,1,0:T(8,128)(2,1)} %copy-done.38, ...), custom_call_target="tpu_custom_call" | custom-call | flops 10737418240 | bytes 31457280 | tf_op jit(solution)/shard_map/middle_block/pallas_call | solution.py:613
  198.9 12.3 %weight_gradients.3 = (bf16[4,4,1024,128]{3,2,1,0:T(8,128)(2,1)}, bf16[4,128,5120]{2,1,0:T(8,128)(2,1)}) custom-call(s32[1]{0:T(128)} %bitcast.slot, bf16[512,4096]{1,0:T(8,128)(2,1)} %get-tuple-element.80.active.refs_0_, bf16[512,4096]{1,0:T(8,128)(2,1)} %get-tuple-element.81.grad_up_in, bf16[512,1024]{1,0:T(8,128)(2,1)} %get-tuple-element.82.hidden, ...), custom_call_target="tpu_custom_call" | custom-call | flops 4831838208 | bytes 25165824 | tf_op jit(solution)/shard_map/weight_gradients/pallas_call | solution.py:742
  213.2 4.5 all-to-all-start.3
  218.3 20.1 %weight_gradients.2 = (bf16[512,1024]{1,0:T(8,128)(2,1)}, f32[1,1024]{1,0:T(1,128)}, bf16[4,4,1024,128]{3,2,1,0:T(8,128)(2,1)}, bf16[4,128,5120]{2,1,0:T(8,128)(2,1)}) custom-call(s32[1]{0:T(128)} %bitcast.slot, bf16[512,4096]{1,0:T(8,128)(2,1)} %get-tuple-element.80.active.refs_0_, bf16[512,4096]{1,0:T(8,128)(2,1)} %get-tuple-element.81.grad_up_in, ...), custom_call_target="tpu_custom_call" | custom-call | flops 9126805504 | bytes 25165824 | tf_op jit(solution)/shard_map/weight_gradients/pallas_call | solution.py:742
  241.3 5.9 %add_halves.8 = (bf16[2,4,1024,128]{3,2,1,0:T(8,128)(2,1)}, bf16[2,4,1024,128]{3,2,1,0:T(8,128)(2,1)}) custom-call(s32[1]{0:T(128)} %constant.41.clone.1.refs_1_.mine, bf16[2,2,4,1024,128]{4,3,2,1,0:T(8,128)(2,1)} %bitcast.84, bf16[2,2,4,1024,128]{4,3,2,1,0:T(8,128)(2,1)} %bitcast.16.refs_1_.refs_3_, bf16[2,2,4,1024,128]{4,3,2,1,0:T(8,128)(2,1)} %bitcast.85, ...), custom_call_target="tpu_custom_call" | custom-call | flops 2097152 | bytes 12582912 | tf_op jit(solution)/shard_map/add_halves/pallas_call | solution.py:901
  249.1 6.8 %add_halves.9 = (bf16[1,8,32,5120]{3,2,1,0:T(8,128)(2,1)}, bf16[1,8,32,5120]{3,2,1,0:T(8,128)(2,1)}) custom-call(s32[1]{0:T(128)} %constant.41.clone.1.refs_1_.mine, bf16[1,2,8,32,5120]{4,3,2,1,0:T(8,128)(2,1)} %bitcast.82, bf16[1,2,8,32,5120]{4,3,2,1,0:T(8,128)(2,1)} %bitcast.19.refs_1_.refs_3_, bf16[1,2,8,32,5120]{4,3,2,1,0:T(8,128)(2,1)} %bitcast.83, ...), custom_call_target="tpu_custom_call" | custom-call | flops 2621440 | bytes 15728640 | tf_op jit(solution)/shard_map/add_halves/pallas_call | solution.py:901
  257.4 27.3 %attention_backward.4 = (f32[8,128,512]{2,1,0:T(8,128)}, bf16[8,2,512,128]{3,2,1,0:T(8,128)(2,1)}) custom-call(bf16[2,2,2,1024,128]{4,3,2,1,0:T(8,128)(2,1)} %bitcast.131, bf16[2,2,2,32,5120]{4,3,2,1,0:T(8,128)(2,1)} %bitcast.129, s32[8]{0:T(128)} %get-tuple-element.69.refs_0_.refs_2_.refs_4_, bf16[8,512,128]{2,1,0:T(8,128)(2,1)} %all-to-all-done.3.refs_3_.refs_1_.refs_5_, ...), custom_call_target="tpu_custom_call" | custom-call | flops 25165824000 | bytes 16777216 | tf_op jit(solution)/shard_map/attention_backward/pallas_call | solution.py:409
  286.2 2.4 copy.30
  288.7 4.1 all-to-all-start.4
  292.8 37.4 %attention_backward.5 = (f32[8,128,512]{2,1,0:T(8,128)}, bf16[8,2,512,128]{3,2,1,0:T(8,128)(2,1)}) custom-call(s32[8]{0:T(128)} %get-tuple-element.69.refs_0_.refs_2_.refs_4_, bf16[8,512,128]{2,1,0:T(8,128)(2,1)} %all-to-all-done.3.refs_3_.refs_1_.refs_5_, bf16[8,512,128]{2,1,0:T(8,128)(2,1)} %get-tuple-element.78.refs_4_.refs_2_.refs_6_, ...), custom_call_target="tpu_custom_call" | custom-call | flops 35232153600 | bytes 16777216 | tf_op jit(solution)/shard_map/attention_backward/pallas_call | solution.py:409
  334.7 3.4 add_halves.10
  339.8 3.8 add_halves.11
  345.3 27.7 %attention_backward.6 = (f32[8,128,512]{2,1,0:T(8,128)}, bf16[8,2,512,128]{3,2,1,0:T(8,128)(2,1)}) custom-call(bf16[2,2,1024,128]{3,2,1,0:T(8,128)(2,1)} %bitcast.135, bf16[2,2,32,5120]{3,2,1,0:T(8,128)(2,1)} %bitcast.133, f32[32,4128]{1,0:T(8,128)} %bitcast.104, bf16[256,1024]{1,0:T(8,128)(2,1)} %collective-permute-done.4.refs_3_, ...), custom_call_target="tpu_custom_call" | custom-call | flops 25165824000 | bytes 16777216 | tf_op jit(solution)/shard_map/attention_backward/pallas_call | solution.py:409
  373.0 2.4 add_halves.12
  378.0 2.6 add_halves.13
  381.1 38.2 %attention_backward.7.unused_2_ = bf16[8,3,512,128]{3,2,1,0:T(8,128)(2,1)} custom-call(bf16[2,1024,128]{2,1,0:T(8,128)(2,1)} %bitcast.139, bf16[2,32,5120]{2,1,0:T(8,128)(2,1)} %bitcast.137, s32[8]{0:T(128)} %get-tuple-element.69.refs_0_.refs_2_.refs_4_, bf16[8,512,128]{2,1,0:T(8,128)(2,1)} %all-to-all-done.3.refs_3_.refs_1_.refs_5_, ...), custom_call_target="tpu_custom_call" | custom-call | flops 35232153600 | bytes 16777216 | tf_op jit(solution)/shard_map/attention_backward/pallas_call | solution.py:409
  421.0 4.4 all-to-all-start.5
  425.4 2.2 add_halves.15
  427.6 2.4 collective-permute-start.15
  432.8 3.4 copy-done.7
  439.0 7.2 %head_gradients.1.unused_3_ = bf16[1024,384]{1,0:T(8,128)(2,1)S(1)} custom-call(bf16[1024,128]{1,0:T(8,128)(2,1)S(1)} %bitcast.81, bf16[32,5120]{1,0:T(8,128)(2,1)S(1)} %bitcast.79, bf16[8,3,512,128]{3,2,1,0:T(8,128)(2,1)S(1)} %copy-done, bf16[8,1024,512]{2,1,0:T(8,128)(2,1)S(1)} %bitcast.75, f32[512,128]{1,0:T(8,128)S(1)} %copy-done.23, ...), custom_call_target="tpu_custom_call" | custom-call | flops 3221225472 | bytes 12582912 | tf_op jit(solution)/shard_map/head_gradients/pallas_call | solution.py:799
  447.2 9.9 %collective-permute-done.14.unused_1_.refs_2_ = bf16[1024,128]{1,0:T(8,128)(2,1)} collective-permute-done((bf16[1024,128]{1,0:T(8,128)(2,1)}, bf16[1024,128]{1,0:T(8,128)(2,1)}, u32[]{:S(2)}, u32[]{:S(2)}) %collective-permute-start.14) | collective-permute-done | bytes 262176 | tf_op jit(solution)/shard_map/ppermute | solution.py:1089
  457.1 6.2 %all-to-all-done.5.unused_0_.refs_1_ = bf16[8,3,512,128]{3,2,1,0:T(8,128)(2,1)} async-done(((bf16[8,3,512,128]{3,2,1,0:T(8,128)(2,1)}), bf16[8,3,512,128]{3,2,1,0:T(8,128)(2,1)}, u32[]{:S(2)}, u32[]{:S(2)}) %all-to-all-start.5) | async-done | bytes 3145760 | tf_op jit(solution)/shard_map/all_to_all | solution.py:1048
  463.3 4.1 all-to-all-start.6
  469.9 9.0 %input_gradients.1 = (bf16[512,1024]{1,0:T(8,128)(2,1)S(1)}, f32[1,1024]{1,0:T(1,128)S(1)}, f32[1,1024]{1,0:T(1,128)S(1)}) custom-call(bf16[1024,384]{1,0:T(8,128)(2,1)S(1)} %copy-done.4, bf16[8,3,512,128]{3,2,1,0:T(8,128)(2,1)} %all-to-all-done.5.unused_0_.refs_1_, bf16[1024,1024]{1,0:T(8,128)(2,1)S(1)} %copy-done.2, bf16[1024,1024]{1,0:T(8,128)(2,1)} %refs_3_.1, ...), custom_call_target="tpu_custom_call" | custom-call | flops 3221225472 | bytes 14680064 | tf_op jit(solution)/shard_map/input_gradients/pallas_call | solution.py:856
  479.0 2.9 collective-permute-start.16
  493.0 5.2 all-to-all-done.6.unused_0_
  499.0 4.4 all-to-all-start.7
  503.3 10.5 %collective-permute-done.16 = bf16[256,1024]{1,0:T(8,128)(2,1)} collective-permute-done((bf16[256,1024]{1,0:T(8,128)(2,1)S(1)}, bf16[256,1024]{1,0:T(8,128)(2,1)}, u32[]{:S(2)}, u32[]{:S(2)}) %collective-permute-start.16) | collective-permute-done | bytes 524320 | tf_op jit(solution)/shard_map/ppermute | solution.py:1040
  516.4 2.4 reshape.215
  (162 shorter events, 70.8 us)
Async XLA Ops:
  7.2 6.8 %copy-start.39 = (s32[1,2]{1,0:T(1,128)S(1)}, s32[1,2]{1,0:T(1,128)}, u32[]{:S(2)}) copy-start(s32[1,2]{1,0:T(1,128)} %param.14) | copy-start | bytes 28
  9.9 27.4 %collective-permute-start = (bf16[256,1024]{1,0:T(8,128)(2,1)}, bf16[256,1024]{1,0:T(8,128)(2,1)S(1)}, u32[]{:S(2)}, u32[]{:S(2)}) collective-permute-start(bf16[256,1024]{1,0:T(8,128)(2,1)} %bitcast.1), channel_id=1, source_target_pairs={{0,2},{2,0},{1,3},{3,1},{4,6},{6,4},{5,7},{7,5},{8,10},{10,8},{9,1... | collective-permute-start | bytes 1572872 | tf_op jit(solution)/shard_map/ppermute | solution.py:1040
  15.9 11.0 %copy-start.1 = (bf16[1024,1024]{1,0:T(8,128)(2,1)S(1)}, bf16[1024,1024]{1,0:T(8,128)(2,1)}, u32[]{:S(2)}) copy-start(bf16[1024,1024]{1,0:T(8,128)(2,1)} %refs_2_.1) | copy-start | bytes 6291460
  22.4 136.3 %copy-start.20 = (f32[1,6144]{1,0:T(1,128)}, f32[1,6144]{1,0:T(1,128)S(1)}, u32[]{:S(2)}) copy-start(f32[1,6144]{1,0:T(1,128)S(1)} %fusion.16.mod.refs_3_.refs_8_) | copy-start | bytes 73732
  38.1 4.4 copy-start.10
  38.1 25.5 %all-to-all-start = ((bf16[8,3,256,128]{3,2,1,0:T(8,128)(2,1)}), bf16[8,3,256,128]{3,2,1,0:T(8,128)(2,1)}, u32[]{:S(2)}, u32[]{:S(2)}) async-start(bf16[8,3,256,128]{3,2,1,0:T(8,128)(2,1)} %order_after.5), calls=%async_computation | async-start | bytes 3145728 | tf_op jit(solution)/shard_map/all_to_all | solution.py:1048
  50.2 17.0 %copy-start.40 = (s32[8]{0:T(128)S(1)}, s32[8]{0:T(128)}, u32[]{:S(2)}) copy-start(s32[8]{0:T(128)} %times.1) | copy-start | bytes 100
  63.6 24.5 %all-to-all-start.1 = ((bf16[8,3,256,128]{3,2,1,0:T(8,128)(2,1)}), bf16[8,3,256,128]{3,2,1,0:T(8,128)(2,1)S(1)}, u32[]{:S(2)}, u32[]{:S(2)}) async-start(bf16[8,3,256,128]{3,2,1,0:T(8,128)(2,1)} %copy-done.12), calls=%async_computation.1 | async-start | bytes 3145728 | tf_op jit(solution)/shard_map/all_to_all | solution.py:1048
  70.5 47.7 %collective-permute-start.1 = (bf16[8,2,256,128]{3,2,1,0:T(8,128)(2,1)}, bf16[8,2,256,128]{3,2,1,0:T(8,128)(2,1)}, u32[]{:S(2)}, u32[]{:S(2)}) collective-permute-start(bf16[8,2,256,128]{3,2,1,0:T(8,128)(2,1)} %slice.79), channel_id=1, source_target_pairs={{0,1},{1,0},{2,3},{3,2},{4,5},{5,4},{6,7},{7,6},{8,9},{9,8},{10,11... | collective-permute-start | bytes 3145736 | tf_op jit(solution)/shard_map/ppermute | solution.py:1051
  88.2 30.5 %collective-permute-start.2 = (bf16[8,2,256,128]{3,2,1,0:T(8,128)(2,1)S(1)}, bf16[8,2,256,128]{3,2,1,0:T(8,128)(2,1)}, u32[]{:S(2)}, u32[]{:S(2)}) collective-permute-start(bf16[8,2,256,128]{3,2,1,0:T(8,128)(2,1)S(1)} %slice.80), channel_id=1, source_target_pairs={{0,1},{1,0},{2,3},{3,2},{4,5},{5,4},{6,7},{7,6},{8,9},{9,8},{10,11... | collective-permute-start | bytes 3145736 | tf_op jit(solution)/shard_map/ppermute | solution.py:1051
  118.7 39.9 %collective-permute-start.3 = (bf16[256,1024]{1,0:T(8,128)(2,1)}, bf16[256,1024]{1,0:T(8,128)(2,1)S(1)}, u32[]{:S(2)}, u32[]{:S(2)}) collective-permute-start(bf16[256,1024]{1,0:T(8,128)(2,1)} %order_after.6), channel_id=1, source_target_pairs={{0,2},{2,0},{1,3},{3,1},{4,6},{6,4},{5,7},{7,5},{8,10},{10,8},{9,1... | collective-permute-start | bytes 1572872 | tf_op jit(solution)/shard_map/ppermute | solution.py:1040
  153.6 5.0 copy-start.37
  153.6 19.2 %all-to-all-start.2 = ((bf16[8,512,128]{2,1,0:T(8,128)(2,1)}), bf16[8,512,128]{2,1,0:T(8,128)(2,1)S(1)}, u32[]{:S(2)}, u32[]{:S(2)}) async-start(bf16[8,512,128]{2,1,0:T(8,128)(2,1)} %get-tuple-element.78.refs_4_.refs_2_.refs_6_), calls=%async_computation.2 | async-start | bytes 2097152 | tf_op jit(solution)/shard_map/all_to_all | solution.py:1048
  157.4 275.4 %all-gather.3.cloned.1.call-start = ((), (), s32[]{:S(2)}) async-start(), calls=%async_computation.8 | async-start | bytes 9437184 | tf_op jit(solution)/shard_map/all_gather | solution.py:1122
  158.7 3.4 copy-start.28
  162.1 6.6 %copy-start.13 = (bf16[512,1024]{1,0:T(8,128)(2,1)}, bf16[512,1024]{1,0:T(8,128)(2,1)S(1)}, u32[]{:S(2)}) copy-start(bf16[512,1024]{1,0:T(8,128)(2,1)S(1)} %pad_maximum_fusion.1.cotangent.refs_2_) | copy-start | bytes 3145732
  170.7 28.2 %copy-start.30 = (bf16[1024,512]{1,0:T(8,128)(2,1)}, bf16[1024,512]{1,0:T(8,128)(2,1)S(1)}, u32[]{:S(2)}) copy-start(bf16[1024,512]{1,0:T(8,128)(2,1)S(1)} %get-tuple-element.83.scaled_turned) | copy-start | bytes 3145732
  198.9 13.0 %copy-start.17 = (bf16[256,1024]{1,0:T(8,128)(2,1)S(1)}, bf16[256,1024]{1,0:T(8,128)(2,1)}, u32[]{:S(2)}) copy-start(bf16[256,1024]{1,0:T(8,128)(2,1)} %copy-done.16) | copy-start | bytes 1572868
  198.9 13.0 %copy-start.19 = (bf16[256,1024]{1,0:T(8,128)(2,1)S(1)}, bf16[256,1024]{1,0:T(8,128)(2,1)}, u32[]{:S(2)}) copy-start(bf16[256,1024]{1,0:T(8,128)(2,1)} %copy-done.18) | copy-start | bytes 1572868
  211.2 38.0 %collective-permute-start.6 = (bf16[4,128,5120]{2,1,0:T(8,128)(2,1)}, bf16[4,128,5120]{2,1,0:T(8,128)(2,1)}, u32[]{:S(2)}, u32[]{:S(2)}) collective-permute-start(bf16[4,128,5120]{2,1,0:T(8,128)(2,1)} %get-tuple-element.93), channel_id=1, source_target_pairs={{0,4},{4,0},{8,12},{12,8},{16,20},{20,16},{24,28},{28,24},{1,5},{5... | collective-permute-start | bytes 15728648 | tf_op jit(solution)/shard_map/ppermute | solution.py:1054
  211.2 30.2 %collective-permute-start.5 = (bf16[4,4,1024,128]{3,2,1,0:T(8,128)(2,1)}, bf16[4,4,1024,128]{3,2,1,0:T(8,128)(2,1)}, u32[]{:S(2)}, u32[]{:S(2)}) collective-permute-start(bf16[4,4,1024,128]{3,2,1,0:T(8,128)(2,1)} %get-tuple-element.90), channel_id=1, source_target_pairs={{0,4},{4,0},{8,12},{12,8},{16,20},{20,16},{24,28},{28,24},{1,5},{5... | collective-permute-start | bytes 12582920 | tf_op jit(solution)/shard_map/ppermute | solution.py:1054
  213.2 44.1 %all-to-all-start.3 = ((bf16[8,512,128]{2,1,0:T(8,128)(2,1)}), bf16[8,512,128]{2,1,0:T(8,128)(2,1)}, u32[]{:S(2)}, u32[]{:S(2)}) async-start(bf16[8,512,128]{2,1,0:T(8,128)(2,1)} %get-tuple-element.87), calls=%async_computation.3 | async-start | bytes 2097152 | tf_op jit(solution)/shard_map/all_to_all | solution.py:1048
  240.3 105.1 %collective-permute-start.4 = (bf16[256,1024]{1,0:T(8,128)(2,1)}, bf16[256,1024]{1,0:T(8,128)(2,1)}, u32[]{:S(2)}, u32[]{:S(2)}) collective-permute-start(bf16[256,1024]{1,0:T(8,128)(2,1)} %slice.69), channel_id=1, source_target_pairs={{0,2},{2,0},{1,3},{3,1},{4,6},{6,4},{5,7},{7,5},{8,10},{10,8},{9,1... | collective-permute-start | bytes 1572872 | tf_op jit(solution)/shard_map/ppermute | solution.py:1040
  247.2 87.5 %collective-permute-start.7 = (bf16[2,2,2,1024,128]{4,3,2,1,0:T(8,128)(2,1)}, bf16[2,2,2,1024,128]{4,3,2,1,0:T(8,128)(2,1)}, u32[]{:S(2)}, u32[]{:S(2)}) collective-permute-start(bf16[2,2,2,1024,128]{4,3,2,1,0:T(8,128)(2,1)} %bitcast.130), channel_id=1, source_target_pairs={{0,8},{4,12},{8,0},{12,4},{16,24},{20,28},{24,16},{28,20},{1,9},{5... | collective-permute-start | bytes 6291464 | tf_op jit(solution)/shard_map/ppermute | solution.py:1089
  255.9 82.4 %collective-permute-start.8 = (bf16[2,2,2,32,5120]{4,3,2,1,0:T(8,128)(2,1)}, bf16[2,2,2,32,5120]{4,3,2,1,0:T(8,128)(2,1)S(1)}, u32[]{:S(2)}, u32[]{:S(2)}) collective-permute-start(bf16[2,2,2,32,5120]{4,3,2,1,0:T(8,128)(2,1)} %bitcast.128), channel_id=1, source_target_pairs={{0,16},{4,20},{8,24},{12,28},{16,0},{20,4},{24,8},{28,12},{1,17},{... | collective-permute-start | bytes 7864328 | tf_op jit(solution)/shard_map/ppermute | solution.py:1089
  288.7 45.2 %all-to-all-start.4 = ((f32[32,1,4128]{2,1,0:T(1,128)}), f32[32,1,4128]{2,1,0:T(1,128)S(1)}, u32[]{:S(2)}, u32[]{:S(2)}) async-start(f32[32,1,4128]{2,1,0:T(1,128)} %copy.30), calls=%async_computation.4 | async-start | bytes 1081344 | tf_op jit(solution)/shard_map/all_to_all | solution.py:1153
  330.3 50.8 %collective-permute-start.13 = (bf16[8,2,512,128]{3,2,1,0:T(8,128)(2,1)}, bf16[8,2,512,128]{3,2,1,0:T(8,128)(2,1)}, u32[]{:S(2)}, u32[]{:S(2)}) collective-permute-start(bf16[8,2,512,128]{3,2,1,0:T(8,128)(2,1)} %get-tuple-element.112), channel_id=1, source_target_pairs={{0,1},{1,0},{2,3},{3,2},{4,5},{5,4},{6,7},{7,6},{8,9},{9,8},{10,11... | collective-permute-start | bytes 6291464 | tf_op jit(solution)/shard_map/ppermute | solution.py:1051
  338.0 34.9 %collective-permute-start.9 = (bf16[2,2,1024,128]{3,2,1,0:T(8,128)(2,1)}, bf16[2,2,1024,128]{3,2,1,0:T(8,128)(2,1)}, u32[]{:S(2)}, u32[]{:S(2)}) collective-permute-start(bf16[2,2,1024,128]{3,2,1,0:T(8,128)(2,1)} %bitcast.134), channel_id=1, source_target_pairs={{0,16},{4,20},{8,24},{12,28},{16,0},{20,4},{24,8},{28,12},{1,17},{... | collective-permute-start | bytes 3145736 | tf_op jit(solution)/shard_map/ppermute | solution.py:1089
  343.6 33.3 %collective-permute-start.11 = (bf16[2,2,32,5120]{3,2,1,0:T(8,128)(2,1)}, bf16[2,2,32,5120]{3,2,1,0:T(8,128)(2,1)S(1)}, u32[]{:S(2)}, u32[]{:S(2)}) collective-permute-start(bf16[2,2,32,5120]{3,2,1,0:T(8,128)(2,1)} %bitcast.132), channel_id=1, source_target_pairs={{0,8},{4,12},{8,0},{12,4},{16,24},{20,28},{24,16},{28,20},{1,9},{5... | collective-permute-start | bytes 3932168 | tf_op jit(solution)/shard_map/ppermute | solution.py:1089
  375.4 44.0 %collective-permute-start.10 = (bf16[2,1024,128]{2,1,0:T(8,128)(2,1)}, bf16[2,1024,128]{2,1,0:T(8,128)(2,1)S(1)}, u32[]{:S(2)}, u32[]{:S(2)}) collective-permute-start(bf16[2,1024,128]{2,1,0:T(8,128)(2,1)} %bitcast.138), channel_id=1, source_target_pairs={{0,1},{1,0},{2,3},{3,2},{4,5},{5,4},{6,7},{7,6},{8,9},{9,8},{10,11... | collective-permute-start | bytes 1572872 | tf_op jit(solution)/shard_map/ppermute | solution.py:1089
  380.6 38.8 %collective-permute-start.12 = (bf16[2,32,5120]{2,1,0:T(8,128)(2,1)}, bf16[2,32,5120]{2,1,0:T(8,128)(2,1)S(1)}, u32[]{:S(2)}, u32[]{:S(2)}) collective-permute-start(bf16[2,32,5120]{2,1,0:T(8,128)(2,1)} %bitcast.136), channel_id=1, source_target_pairs={{0,1},{1,0},{2,3},{3,2},{4,5},{5,4},{6,7},{7,6},{8,9},{9,8},{10,11... | collective-permute-start | bytes 1966088 | tf_op jit(solution)/shard_map/ppermute | solution.py:1089
  421.0 42.3 %all-to-all-start.5 = ((bf16[8,3,512,128]{3,2,1,0:T(8,128)(2,1)}), bf16[8,3,512,128]{3,2,1,0:T(8,128)(2,1)}, u32[]{:S(2)}, u32[]{:S(2)}) async-start(bf16[8,3,512,128]{3,2,1,0:T(8,128)(2,1)} %order_after.7.refs_0_.refs_2_), calls=%async_computation.5 | async-start | bytes 6291456 | tf_op jit(solution)/shard_map/all_to_all | solution.py:1048
  427.6 29.5 %collective-permute-start.15 = (bf16[32,5120]{1,0:T(8,128)(2,1)}, bf16[32,5120]{1,0:T(8,128)(2,1)}, u32[]{:S(2)}, u32[]{:S(2)}) collective-permute-start(bf16[32,5120]{1,0:T(8,128)(2,1)} %bitcast.78), channel_id=1, source_target_pairs={{0,2},{2,0},{1,3},{3,1},{4,6},{6,4},{5,7},{7,5},{8,10},{10,8},{9,1... | collective-permute-start | bytes 983048 | tf_op jit(solution)/shard_map/ppermute | solution.py:1089
  430.0 2.7 copy-start.26
  430.0 2.7 copy-start.27
  432.2 24.8 %collective-permute-start.14 = (bf16[1024,128]{1,0:T(8,128)(2,1)}, bf16[1024,128]{1,0:T(8,128)(2,1)}, u32[]{:S(2)}, u32[]{:S(2)}) collective-permute-start(bf16[1024,128]{1,0:T(8,128)(2,1)} %bitcast.80), channel_id=1, source_target_pairs={{0,2},{2,0},{1,3},{3,1},{4,6},{6,4},{5,7},{7,5},{8,10},{10,8},{9,1... | collective-permute-start | bytes 786440 | tf_op jit(solution)/shard_map/ppermute | solution.py:1089
  432.8 3.4 copy-start.7
  463.3 5.4 %copy-start.2 = (bf16[1024,1024]{1,0:T(8,128)(2,1)S(1)}, bf16[1024,1024]{1,0:T(8,128)(2,1)}, u32[]{:S(2)}) copy-start(bf16[1024,1024]{1,0:T(8,128)(2,1)} %refs_2_.1) | copy-start | bytes 6291460
  463.3 5.4 %copy-start.4 = (bf16[1024,384]{1,0:T(8,128)(2,1)S(1)}, bf16[1024,384]{1,0:T(8,128)(2,1)}, u32[]{:S(2)}) copy-start(bf16[1024,384]{1,0:T(8,128)(2,1)} %order_after.8.refs_0_) | copy-start | bytes 2359300
  463.3 5.4 %copy-start.14 = (f32[512,128]{1,0:T(8,128)S(1)}, f32[512,128]{1,0:T(8,128)}, u32[]{:S(2)}) copy-start(f32[512,128]{1,0:T(8,128)} %get-tuple-element.70.refs_5_) | copy-start | bytes 786436
  463.3 5.4 %copy-start.15 = (f32[512,128]{1,0:T(8,128)S(1)}, f32[512,128]{1,0:T(8,128)}, u32[]{:S(2)}) copy-start(f32[512,128]{1,0:T(8,128)} %get-tuple-element.71.refs_6_) | copy-start | bytes 786436
  463.3 5.4 %copy-start.21 = (f32[1,6144]{1,0:T(1,128)S(1)}, f32[1,6144]{1,0:T(1,128)}, u32[]{:S(2)}) copy-start(f32[1,6144]{1,0:T(1,128)} %copy-done.20) | copy-start | bytes 73732
  463.3 34.9 %all-to-all-start.6 = ((bf16[32,32,384]{2,1,0:T(8,128)(2,1)}), bf16[32,32,384]{2,1,0:T(8,128)(2,1)}, u32[]{:S(2)}, u32[]{:S(2)}) async-start(bf16[32,32,384]{2,1,0:T(8,128)(2,1)} %bitcast.74), calls=%async_computation.6 | async-start | bytes 1572864 | tf_op jit(solution)/shard_map/all_to_all | solution.py:1207
  479.0 4.6 copy-start.5
  479.0 4.0 copy-start.36
  479.0 34.8 %collective-permute-start.16 = (bf16[256,1024]{1,0:T(8,128)(2,1)S(1)}, bf16[256,1024]{1,0:T(8,128)(2,1)}, u32[]{:S(2)}, u32[]{:S(2)}) collective-permute-start(bf16[256,1024]{1,0:T(8,128)(2,1)S(1)} %slice.71), channel_id=1, source_target_pairs={{0,2},{2,0},{1,3},{3,1},{4,6},{6,4},{5,7},{7,5},{8,10},{10,8},{9,1... | collective-permute-start | bytes 1572872 | tf_op jit(solution)/shard_map/ppermute | solution.py:1040
  490.9 22.9 %copy-start.6 = (bf16[512,1024]{1,0:T(8,128)(2,1)S(1)}, bf16[512,1024]{1,0:T(8,128)(2,1)}, u32[]{:S(2)}) copy-start(bf16[512,1024]{1,0:T(8,128)(2,1)} %copy-done.5) | copy-start | bytes 3145732
  499.0 25.6 %all-to-all-start.7 = ((f32[32,16,128]{2,1,0:T(8,128)}), f32[32,16,128]{2,1,0:T(8,128)S(1)}, u32[]{:S(2)}, u32[]{:S(2)}) async-start(f32[32,16,128]{2,1,0:T(8,128)} %order_after.9), calls=%async_computation.7 | async-start | bytes 524288 | tf_op jit(solution)/shard_map/all_to_all | solution.py:1222
  (19 other events, 23.4 us)
Sparse Core Ops, SparseCore 0:
  213.4 82.1 all-gather.2

commit v4 on v3

--- a/solution.py
+++ b/solution.py
@@ -23,7 +23,7 @@
 SCALE2 = math.log2(math.e) / math.sqrt(HD)
 SAFE_LOG2 = 100.0
 FORWARD_GROUP = 4
-BACKWARD_GROUP = 2
+BACKWARD_GROUP = 4
 ROWS_ROWS = (((1,), (1,)), ((), ()))
 ROWS_COLS = (((1,), (0,)), ((), ()))
 SHIFT_ONE, SCALE_ONE, GATE_ONE, SHIFT_TWO, SCALE_TWO, GATE_TWO = range(6)
@@ -276,27 +276,25 @@
     )(*after, order, flag, *sources, *rest)
 
 
-def backward_kernel(
-    order, grad, out, lse, *refs, parts, own, first, last, begin, end, came, heads
-):
-    trios, pairs, refs = split_sources(refs, parts, own)
+def backward_kernel(order, grad, out, lse, *refs, parts, sources, first, last, came, heads):
+    trios, pairs, refs = refs[:parts], refs[parts : parts + sources], refs[parts + sources :]
     frames, tokens, lanes = grad.shape
+    size = pairs[0].shape[2]
+    few = size * sources
     if not first:
         dq_in = refs[0]
-        refs = refs[1:]
-    if begin > 0:
-        pair_in = refs[0]
         refs = refs[1:]
     if came:
         pair_came = refs[0]
         refs = refs[1:]
+    if not last:
+        dq_sum, refs = refs[0], refs[1:]
+    finals, refs = refs[:sources], refs[sources:]
+    queries, grads, delta, logs, keys, values, key_turned, dk, dv = refs[:9]
     if last:
-        final, queries, grads, delta, logs, keys, values, key_turned, dk, dv, dq_sum = refs
-        places = (1, 2)
-    else:
-        dq_sum, final, queries, grads, delta, logs, keys, values, key_turned, dk, dv = refs
-        places = (0, 1)
-    group = dk.shape[0] // tokens
+        dq_sum = refs[9]
+    places = (parts, parts + 1) if last else (0, 1)
+    group = dk.shape[0] // few
     masks = head_masks(tokens, lanes, heads)
     zero = jnp.zeros((tokens, lanes), LOW)
     lane8 = lax.broadcasted_iota(jnp.int32, (8, lanes), 1) // HD
@@ -311,32 +309,26 @@
             grads[h, t] = jnp.where(masks[h], g, zero)
         keys[t] = k
         values[t] = joined(pairs, slot, 1)
-        key_turned[t // group, :, (t % group) * tokens : (t % group + 1) * tokens] = k.T
+        key_turned[t // group, :, (t % group) * few : (t % group + 1) * few] = k.T
         logs[t] = lse[slot]
         delta[t] = exact_dot(
             pick.astype(WIDE), g.astype(WIDE) * out[slot].astype(WIDE), ROWS_ROWS
         )
         dq_sum[t] = jnp.zeros((lanes, tokens), WIDE) if first else dq_in[t]
-        if begin > 0:
-            for i in range(2):
-                old = pair_in[t, i]
-                if came:
-                    old = (old.astype(WIDE) + pair_came[t, i].astype(WIDE)).astype(LOW)
-                final[t, places[i]] = old
-    group_masks = head_masks(group * tokens, lanes, heads)
-    group_zero = jnp.zeros((group * tokens, lanes), LOW)
+    group_masks = head_masks(group * few, lanes, heads)
+    group_zero = jnp.zeros((group * few, lanes), LOW)
 
     def outer(index, unused):
         base = index * group
-        k = keys[pl.ds(base, group)].reshape(group * tokens, lanes)
-        v = values[pl.ds(base, group)].reshape(group * tokens, lanes)
+        k = keys[pl.ds(base, group)].reshape(group * few, lanes)
+        v = values[pl.ds(base, group)].reshape(group * few, lanes)
         ks = [jnp.where(mask, k, group_zero) for mask in group_masks]
         vs = [jnp.where(mask, v, group_zero) for mask in group_masks]
         dk[...] = jnp.zeros(dk.shape, WIDE)
         dv[...] = jnp.zeros(dv.shape, WIDE)
 
         def tile(j, count):
-            rows = slice(0, count * tokens)
+            rows = slice(0, count * few)
             for h in range(heads):
                 q = queries[h, j]
                 g = grads[h, j]
@@ -357,66 +349,65 @@
             tile(base + count - 1, count)
         lax.fori_loop(base + group - 1, frames, inner, 0)
         for i in range(group):
-            rows = slice(i * tokens, (i + 1) * tokens)
+            rows = slice(i * few, (i + 1) * few)
             slot = order[base + i]
             part_k = dk[rows] * (1.0 / math.sqrt(HD))
             part_v = dv[rows]
             if came:
                 part_k = part_k + pair_came[slot, 0].astype(WIDE)
                 part_v = part_v + pair_came[slot, 1].astype(WIDE)
-            final[slot, places[0]] = part_k.astype(LOW)
-            final[slot, places[1]] = part_v.astype(LOW)
+            for n, final in enumerate(finals):
+                span = slice(n * size, (n + 1) * size)
+                final[slot, places[0]] = part_k[span].astype(LOW)
+                final[slot, places[1]] = part_v[span].astype(LOW)
         return unused
 
-    lax.fori_loop(begin // group, end // group, outer, 0)
+    lax.fori_loop(0, frames // group, outer, 0)
     if last:
         for t in range(frames):
-            final[order[t], 0] = (dq_sum[t].T * (1.0 / math.sqrt(HD))).astype(LOW)
-
-
-def attention_backward(
-    order, dq, partial, came, trios, pairs, grad, out, lse, begin, end, last, after
-):
+            dq = (dq_sum[t].T * (1.0 / math.sqrt(HD))).astype(LOW)
+            for i in range(parts):
+                finals[0][order[t], i] = dq[i * size : (i + 1) * size]
+
+
+def attention_backward(order, dq, came, trios, pairs, grad, out, lse, last, after):
     frames, tokens, lanes = grad.shape
-    parts, own = len(trios), pairs is None
-    sources = tuple(trios) + (() if own else tuple(pairs))
+    size = pairs[0].shape[2]
+    few = size * len(pairs)
+    parts = len(trios)
     heads = lanes // HD
     first = dq is None
     sums = (frames, lanes, tokens)
-    extra = tuple(
-        array for array in (dq, partial if begin > 0 else None, came) if array is not None
-    )
-    steps = sum(frames - t for t in range(begin, end))
-    work = heads * steps * tokens * tokens
+    extra = tuple(array for array in (dq, came) if array is not None)
+    work = heads * frames * (frames + 1) // 2 * tokens * few
+    rows = BACKWARD_GROUP * few
     scratch = [
         pltpu.VMEM((heads, frames, tokens, lanes), LOW),
         pltpu.VMEM((heads, frames, tokens, lanes), LOW),
         pltpu.VMEM((frames, 8, tokens), WIDE),
         pltpu.VMEM((frames, 8, tokens), WIDE),
-        pltpu.VMEM((frames, tokens, lanes), LOW),
-        pltpu.VMEM((frames, tokens, lanes), LOW),
-        pltpu.VMEM((frames // BACKWARD_GROUP, lanes, BACKWARD_GROUP * tokens), LOW),
-        pltpu.VMEM((BACKWARD_GROUP * tokens, lanes), WIDE),
-        pltpu.VMEM((BACKWARD_GROUP * tokens, lanes), WIDE),
+        pltpu.VMEM((frames, few, lanes), LOW),
+        pltpu.VMEM((frames, few, lanes), LOW),
+        pltpu.VMEM((frames // BACKWARD_GROUP, lanes, rows), LOW),
+        pltpu.VMEM((rows, lanes), WIDE),
+        pltpu.VMEM((rows, lanes), WIDE),
     ]
+    pair_shape = jax.ShapeDtypeStruct((frames, (parts if last else 0) + 2, size, lanes), LOW)
     if last:
-        out_shape = [jax.ShapeDtypeStruct((frames, 3, tokens, lanes), LOW)]
+        out_shape = [pair_shape]
         scratch.append(pltpu.VMEM(sums, WIDE))
     else:
-        out_shape = [
-            jax.ShapeDtypeStruct(sums, WIDE), jax.ShapeDtypeStruct((frames, 2, tokens, lanes), LOW)
-        ]
+        out_shape = [jax.ShapeDtypeStruct(sums, WIDE)] + [pair_shape] * len(pairs)
     return pl.pallas_call(
         behind(
             functools.partial(
-                backward_kernel, parts=parts, own=own, first=first, last=last, begin=begin,
-                end=end, came=came is not None, heads=heads,
+                backward_kernel, parts=parts, sources=len(pairs), first=first, last=last,
+                came=came is not None, heads=heads,
             ),
             len(after),
         ),
         out_shape=out_shape,
-        in_specs=anywhere(len(after)) + [smem()]
-        + [vmem()] * (3 + len(sources) + len(extra)),
+        in_specs=anywhere(len(after)) + [smem()] + [vmem()] * (3 + parts + len(pairs) + len(extra)),
         out_specs=[vmem()] * len(out_shape),
         scratch_shapes=scratch,
         compiler_params=pltpu.CompilerParams(vmem_limit_bytes=56 * MIB),
@@ -424,7 +415,7 @@
             flops=work * 10 * HD * 5, bytes_accessed=16 * MIB, transcendentals=work
         ),
         name="attention_backward",
-    )(*after, order, grad, out, lse, *sources, *extra)
+    )(*after, order, grad, out, lse, *trios, *pairs, *extra)
 
 
 def normalize(values):
@@ -773,7 +764,14 @@
     )(*parts)
 
 
-def head_kernel(grads, hidden, cosine, sine, time_cosine, time_sine, product, total):
+def three_gradients(early, late, at):
+    q = jnp.concatenate([late[at, 0], late[at, 1]], axis=0)
+    k = jnp.concatenate([early[at, 0], late[at, 2]], axis=0)
+    v = jnp.concatenate([early[at, 1], late[at, 3]], axis=0)
+    return q, k, v
+
+
+def head_kernel(early, grads, hidden, cosine, sine, time_cosine, time_sine, product, total):
     step = pl.program_id(0)
 
     @pl.when(step == 0)
@@ -782,8 +780,9 @@
 
     cos = cosine[...] + time_cosine[0]
     sin = -(sine[...] + time_sine[0])
+    q, k, v = three_gradients(early, grads, 0)
     block = jnp.concatenate(
-        [turned(grads[0, i].astype(WIDE), cos, sin).astype(LOW) for i in range(2)] + [grads[0, 2]],
+        [turned(q.astype(WIDE), cos, sin).astype(LOW), turned(k.astype(WIDE), cos, sin).astype(LOW), v],
         axis=1,
     )
     total[...] += dot(hidden[0], block)
@@ -793,15 +792,17 @@
         product[...] = total[...].astype(LOW)
 
 
-def head_gradients(grads, hidden_all, tables, after):
-    frames, unused, count, lanes = grads.shape
+def head_gradients(early, grads, hidden_all, tables, after):
+    frames, unused, few, lanes = grads.shape
+    count = 2 * few
     frame = pl.BlockSpec((1, 1, lanes), lambda f: (f, 0, 0))
     return pl.pallas_call(
         behind(head_kernel, len(after)),
         grid=(frames,),
         out_shape=jax.ShapeDtypeStruct((D, 3 * lanes), LOW),
         in_specs=anywhere(len(after)) + [
-            pl.BlockSpec((1, 3, count, lanes), lambda f: (f, 0, 0, 0)),
+            pl.BlockSpec((1, 2, few, lanes), lambda f: (f, 0, 0, 0)),
+            pl.BlockSpec((1, 4, few, lanes), lambda f: (f, 0, 0, 0)),
             pl.BlockSpec((1, D, count), lambda f: (f, 0, 0)),
             whole((count, lanes)), whole((count, lanes)), frame, frame,
         ],
@@ -812,11 +813,11 @@
             flops=6 * frames * count * D * lanes, bytes_accessed=12 * MIB, transcendentals=0
         ),
         name="head_gradients",
-    )(*after, grads, hidden_all, *tables)
+    )(*after, early, grads, hidden_all, *tables)
 
 
 def output_kernel(
-    grads, w_query, w_key, w_value, cosine, sine, tokens, mod, grad_middle,
+    early, grads, w_query, w_key, w_value, cosine, sine, tokens, mod, grad_middle,
     grad_tokens, grad_shift, grad_scale, total
 ):
     step = pl.program_id(0)
@@ -827,8 +828,9 @@
         total[...] = jnp.zeros(total.shape, WIDE)
 
     dh = total[...]
+    blocks = [three_gradients(early, grads, g) for g in range(groups)]
     for i, weight in enumerate((w_query, w_key, w_value)):
-        block = jnp.concatenate([grads[g, i] for g in range(groups)], axis=1)
+        block = jnp.concatenate([three[i] for three in blocks], axis=1)
         if i < 2:
             block = turned(block.astype(WIDE), cosine[...], -sine[...]).astype(LOW)
         dh = dh + dot(block, weight[...], ROWS_ROWS)
@@ -845,8 +847,9 @@
         ).astype(LOW)
 
 
-def input_gradients(grads, w_query, w_key, w_value, cosine, sine, tokens, mod, grad_middle, after):
-    frames, unused, count, lanes = grads.shape
+def input_gradients(early, grads, w_query, w_key, w_value, cosine, sine, tokens, mod, grad_middle, after):
+    frames, unused, few, lanes = grads.shape
+    count = 2 * few
     wide = 256
     groups = wide // lanes
     flat = whole((count, D))
@@ -858,7 +861,8 @@
         grid=(D // wide,),
         out_shape=[jax.ShapeDtypeStruct((count, D), LOW), rows, rows],
         in_specs=anywhere(len(after)) + [
-            pl.BlockSpec((groups, 3, count, lanes), lambda c: (c, 0, 0, 0)),
+            pl.BlockSpec((groups, 2, few, lanes), lambda c: (c, 0, 0, 0)),
+            pl.BlockSpec((groups, 4, few, lanes), lambda c: (c, 0, 0, 0)),
             weight, weight, weight, whole(cosine.shape), whole(sine.shape),
             flat, whole((1, 6 * D)), flat,
         ],
@@ -869,7 +873,7 @@
             flops=6 * count * D * D, bytes_accessed=14 * MIB, transcendentals=0
         ),
         name="input_gradients",
-    )(*after, grads, w_query, w_key, w_value, cosine, sine, tokens, mod, grad_middle)
+    )(*after, early, grads, w_query, w_key, w_value, cosine, sine, tokens, mod, grad_middle)
 
 
 def halves_kernel(mine, keep_give, came_give, keep_hold, came_hold, give, hold):
@@ -1006,6 +1010,49 @@
         out_specs=[vmem()] * 6,
         name="rotary_tables",
     )(places, times, jnp.asarray(rotary_rates(lanes)))
+
+
+def columns_kernel(product, *totals):
+    frames, rows, unused, width = product.shape
+    lanes = width // 3
+    for f in range(frames):
+        total = jnp.sum(product[f].astype(WIDE), axis=0)
+        for i, target in enumerate(totals):
+            target[:, f * lanes : (f + 1) * lanes] = total[:, i * lanes : (i + 1) * lanes]
+
+
+def sum_columns(product):
+    shape = jax.ShapeDtypeStruct((product.shape[2], D), WIDE)
+    return pl.pallas_call(
+        columns_kernel,
+        out_shape=[shape] * 3,
+        in_specs=[vmem()],
+        out_specs=[vmem()] * 3,
+        name="sum_columns",
+    )(product)
+
+
+def mod_kernel(early, late, out):
+    kept = late.shape[1] * late.shape[2]
+    vectors = 6 * D - kept
+    codes = early[:, vectors:]
+    by_rows = (((0,), (0,)), ((), ()))
+    out[:, kept:] = exact_dot(codes, early[:, :vectors], by_rows)
+    wide = late.shape[2]
+    for c in range(late.shape[1]):
+        out[:, c * wide : (c + 1) * wide] = exact_dot(codes, late[:, c, :], by_rows)
+
+
+def mod_gradient(early, late):
+    kept = late.shape[1] * late.shape[2]
+    part_rows = early.shape[1] - (6 * D - kept)
+    return pl.pallas_call(
+        mod_kernel,
+        out_shape=jax.ShapeDtypeStruct((part_rows, 6 * D), WIDE),
+        in_specs=[vmem()] * 2,
+        out_specs=vmem(),
+        name="mod_gradient",
+    )(early, late)
 
 
 def sinusoid(levels):
@@ -1152,89 +1199,65 @@
         packed = pack(vectors, codes, after)
         return lax.all_to_all(packed, everyone, split_axis=0, concat_axis=0, tiled=True)
 
-    def mod_gradient(codes, vectors):
-        return lax.dot_general(
-            codes, vectors, (((0,), (0,)), ((), ())), precision=lax.Precision.HIGHEST
-        )
-
     codes = embed.astype(WIDE).reshape(devices, D // devices)
     dq = None
-    arrived = []
-    cut = max(frames // 4 // BACKWARD_GROUP, 1) * BACKWARD_GROUP
-    calls = [(step, span) for step in range(sides - 1, -1, -1) for span in (0, 1)]
-    for index, (step, span) in enumerate(calls):
+    arrived = [None, None]
+
+    def backward(dq, pairs, came, last, after):
+        return attention_backward(
+            order, dq, came, trios, pairs, grad_attn, attn_heads, log_total, last, after
+        )
+
+    down.advance()
+    up.advance()
+    mod_came = spread(
+        [grad_gate_one, grad_shift_two, grad_scale_two, grad_gate_two],
+        (grad_attn, down.going, up.going),
+    )
+    out_came = other_half(result[half_count:])
+    after = (down.going, up.going)
+    for step in range(sides - 1, 0, -1):
+        dq, *partials = backward(dq, pairs[step], None, False, after)
         after = ()
-        if index == 0:
-            down.advance()
-            up.advance()
-            after = (down.going, up.going)
-            out_came = other_half(result[half_count:])
-        elif index == 1:
-            mod_came = spread(
-                [grad_gate_one, grad_shift_two, grad_scale_two, grad_gate_two], (dq, partial)
-            )
-        elif index == 2:
-            down.advance((dq,))
-            up.advance((dq,))
-            after = (down.going, up.going, mod_came, out_came)
-        elif index == 3:
-            down.advance((dq,))
-            up.advance((dq,))
-            after = (down.going, up.going)
-        begin, end = ((0, cut), (cut, frames))[span]
-        last = index == len(calls) - 1
-        came = None
-        if last and arrived:
-            came = arrived[0]
-            for more in arrived[1:]:
-                came = add(came, more)
-        answer = attention_backward(
-            order, dq, None if span == 0 else partial, came, trios, pairs[step], grad_attn,
-            attn_heads, log_total, begin, end, last, after,
-        )
-        if last:
-            grads = answer[0]
-        else:
-            dq, partial = answer
-            if span == 1:
-                arrived.append(pass_on(partial, -step))
-    grads = order_after(grads, (down.came, up.came))
+        for which, partial in enumerate(partials):
+            came = pass_on(partial, -step)
+            arrived[which] = came if arrived[which] is None else add(arrived[which], came)
+    down.advance((dq,))
+    up.advance((dq,))
+    dq, early = backward(dq, trios[:1], None, False, (down.going, up.going, out_came, mod_came))
+    down.advance((dq,))
+    up.advance((dq,))
+    early = add(early, arrived[0])
+    (grads,) = backward(dq, trios[1:], arrived[1], True, (down.going, up.going, early))
+
+    early_back = swap_groups(early)
+    grads = order_after(grads, (down.came, up.came, early_back))
     grads_back = swap_groups(grads)
     down.advance((grads,))
     up.advance((grads,))
-    head_product = head_gradients(grads, hidden_all, tables, (down.going, up.going))
-    head_product = order_after(head_product, (grads_back, down.came, up.came))
+    head_product = head_gradients(early, grads, hidden_all, tables, (down.going, up.going))
+    ordered = order_after(head_product, (grads_back, down.came, up.came))
     product = lax.all_to_all(
-        head_product.reshape(devices, D // devices, 3 * lanes),
+        ordered.reshape(devices, D // devices, 3 * lanes),
         everyone, split_axis=0, concat_axis=0, tiled=True,
     )
     grad_source, grad_shift_one, grad_scale_one = input_gradients(
-        grads_back, w_query, w_key, w_value, cosine, sine, source, mod, grad_middle,
+        early_back, grads_back, w_query, w_key, w_value, cosine, sine, source, mod, grad_middle,
         (head_product,),
     )
     in_came = other_half(grad_source[half_count:])
-    total = jnp.sum(
-        product.reshape(frames, row_total, D // devices, 3, lanes).astype(WIDE), axis=1
-    )
-    total = jnp.transpose(total, (2, 1, 0, 3)).reshape(3, D // devices, D)
+    totals = sum_columns(product.reshape(frames, row_total, D // devices, 3 * lanes))
     late = jnp.concatenate([grad_shift_one, grad_scale_one], axis=-1).reshape(1, -1, 128)
     late = jnp.broadcast_to(late, (devices,) + late.shape[1:])
     late_came = lax.all_to_all(order_after(late, (product,)), everyone, split_axis=0, concat_axis=0, tiled=True)
-    all_codes = mod_came[:, 4 * D :]
 
     grad_down = down.finish((grad_source,)).reshape(D, FF // devices).T
     up_proj = up.finish((grad_source,)).reshape(D // devices, FF + D)
-    grad_mod = jnp.concatenate(
-        [
-            mod_gradient(all_codes, late_came.reshape(devices, 2 * D)),
-            mod_gradient(all_codes, mod_came[:, : 4 * D]),
-        ],
-        axis=-1,
-    )
+    grad_mod = mod_gradient(mod_came, late_came)
     return (
         return_clip(result[:half_count], out_came, LOW),
         return_clip(grad_source[:half_count], in_came, WIDE),
-        total[0], total[1], total[2],
+        *totals,
         up_proj[:, FF:], up_proj[:, :FF], grad_down, grad_mod,
     )
 

time: 542 us -> 537 us (level)
  local copies, waits for them, and re-layouts: 48.8 us -> 41.2 us
  starting transfers between devices: 58.6 us -> 64.9 us
  Pallas kernels: 322 us -> 316 us
    all_to_all x1, waiting for transfers between devices: 5.22 us -> 16.1 us  [shards(): lax.all_to_all(ordered.reshape(devices, D // devices, 3 * lanes), everyon...]
    ppermute x4, waiting for transfers between devices: 13.2 us -> 2.8 us  [other_half(): return lax.ppermute(array, 'half', [(0, 1), (1, 0)])]
    all_to_all x1, waiting for transfers between devices: 1.71 us -> 11.8 us  [spread(): lax.all_to_all(packed, everyone, split_axis=0, concat_axis=0, tiled=True)]
    pallas_call x4 -> x5, Pallas kernels: 131 us -> 124 us  [the longest x3 119 us: attention_backward(): pl.pallas_call(behind(functools.partial(backward_kernel, parts=parts, sou...]
    all_to_all x5 -> x6, waiting for transfers between devices: 38.4 us -> 32.2 us  [swap_groups(): lax.all_to_all(grouped, 'frames', split_axis=0, concat_axis=0, tiled=True)]
    all_to_all x5 -> x6, starting transfers between devices: 20.7 us -> 25.4 us  [swap_groups(): lax.all_to_all(grouped, 'frames', split_axis=0, concat_axis=0, tiled=True)]
    unnamed x87 -> x85, local copies, waits for them, and re-layouts: 28.8 us -> 25.7 us
  transfers between devices with their start and end apart: 26 -> 28, of which waited for: 10 -> 8; matrix products, arithmetic and copies ran while one was open for 7% -> 6% of each run, Pallas kernels for 53% -> 52%
where the time goes in v4:
time: 537 us; the launch traced here: 528 us
  Pallas kernels  316 us (59%)
  waiting for transfers between devices  73.1 us (14%)
  starting transfers between devices  64.9 us (12%)
  local copies, waits for them, and re-layouts  41.2 us (8%)
  between operations  16.1 us (3%)
  other arithmetic  9.67 us (2%)
  matrix products  6.46 us (1%)
    pallas_call x3, Pallas kernels, attention_backward(): pl.pallas_call(behind(functools.partial(backward_kernel, parts=parts, sou...  119 us
    pallas_call x2, Pallas kernels, attention_forward(): pl.pallas_call(behind(functools.partial(forward_kernel, parts=parts, own=...  61 us
    all_to_all x6, waiting for transfers between devices, swap_groups(): lax.all_to_all(grouped, 'frames', split_axis=0, concat_axis=0, tiled=True)  32.2 us
    pallas_call x2, Pallas kernels, weight_gradients(): pl.pallas_call(functools.partial(weights_kernel, keep=keep), grid_spec=pl...  32.1 us
    pallas_call x8, Pallas kernels, add_halves(): pl.pallas_call(ordered, grid_spec=pltpu.PrefetchScalarGridSpec(num_scalar...  29.4 us
    unnamed x85, local copies, waits for them, and re-layouts  25.7 us
    all_to_all x6, starting transfers between devices, swap_groups(): lax.all_to_all(grouped, 'frames', split_axis=0, concat_axis=0, tiled=True)  25.4 us
    pallas_call x1, Pallas kernels, middle_block(): pl.pallas_call(middle_kernel, grid=(FF // wide,), out_shape=[of((count, D...  25 us
  transfers between devices with their start and end apart: 28, of which 8 were waited for; matrix products, arithmetic and copies ran while one was open for 6% of the time, Pallas kernels for 52%

profile of v4, /device:TPU:0, one launch (start us, length us, event | category | flops | bytes accessed | tf_op | source)
XLA Modules:
  0.0 527.7 jit_solution(11374131521418808930)
XLA Ops:
  7.2 2.7 constant_dynamic-slice_fusion.1
  9.9 4.0 collective-permute-start
  15.9 6.5 %fusion.8.mod.refs_3_.refs_9_ = f32[1,6144]{1,0:T(1,128)S(1)} fusion(bf16[1024,1]{0,1:T(2,128)(2,1)S(1)} %reshape.206, bf16[1024,6144]{1,0:T(8,128)(2,1)} %param.21), kind=kOutput, calls=%fused_computation.30 | convolution fusion | flops 12582912 | bytes 12609536 | tf_op jit(solution)/shard_map/dot_general | solution.py:1152
  23.0 2.8 rotary_tables.1
  26.9 5.7 %input_projections.2 = (bf16[256,1024]{1,0:T(8,128)(2,1)S(1)}, bf16[8,3,256,128]{3,2,1,0:T(8,128)(2,1)S(1)}) custom-call(bf16[256,1024]{1,0:T(8,128)(2,1)S(1)} %bitcast.56, f32[1,6144]{1,0:T(1,128)S(1)} %fusion.8.mod.refs_3_.refs_9_, bf16[1024,1024]{1,0:T(8,128)(2,1)S(1)} %copy-done.1, bf16[1024,1024]{1,0:T(8,128)(2,1)} %refs_4_.3, ...), custom_call_target="tpu_custom_call" | custom-call | flops 1610612736 | bytes 12582912 | tf_op jit(solution)/shard_map/input_projections/pallas_call | solution.py:492
  34.5 2.8 collective-permute-done.unused_0_.tokens
  38.1 4.4 all-to-all-start
  42.6 5.7 %input_projections.3 = (bf16[256,1024]{1,0:T(8,128)(2,1)S(1)}, bf16[8,3,256,128]{3,2,1,0:T(8,128)(2,1)S(1)}) custom-call(bf16[256,1024]{1,0:T(8,128)(2,1)S(1)} %copy-done.9, f32[1,6144]{1,0:T(1,128)S(1)} %fusion.8.mod.refs_3_.refs_9_, bf16[1024,1024]{1,0:T(8,128)(2,1)S(1)} %copy-done.1, bf16[1024,1024]{1,0:T(8,128)(2,1)} %refs_4_.3, ...), custom_call_target="tpu_custom_call" | custom-call | flops 1610612736 | bytes 12582912 | tf_op jit(solution)/shard_map/input_projections/pallas_call | solution.py:492
  50.2 13.4 %all-to-all-done.refs_2_.refs_6_.refs_8_.refs_10_.refs_7_ = bf16[8,3,256,128]{3,2,1,0:T(8,128)(2,1)} async-done(((bf16[8,3,256,128]{3,2,1,0:T(8,128)(2,1)}), bf16[8,3,256,128]{3,2,1,0:T(8,128)(2,1)}, u32[]{:S(2)}, u32[]{:S(2)}) %all-to-all-start) | async-done | bytes 1572896 | tf_op jit(solution)/shard_map/all_to_all | solution.py:1095
  63.6 3.6 all-to-all-start.1
  68.2 2.3 slice.56
  71.3 16.8 %all-to-all-done.1.refs_3_.refs_7_.refs_9_.refs_8_ = bf16[8,3,256,128]{3,2,1,0:T(8,128)(2,1)S(1)} async-done(((bf16[8,3,256,128]{3,2,1,0:T(8,128)(2,1)}), bf16[8,3,256,128]{3,2,1,0:T(8,128)(2,1)S(1)}, u32[]{:S(2)}, u32[]{:S(2)}) %all-to-all-start.1) | async-done | bytes 1572896 | tf_op jit(solution)/shard_map/all_to_all | solution.py:1095
  89.3 29.1 %attention_forward.2 = (s32[1]{0:T(128)}, f32[8,512,128]{2,1,0:T(8,128)}, f32[8,512,128]{2,1,0:T(8,128)}, f32[8,512,128]{2,1,0:T(8,128)}) custom-call(s32[8]{0:T(128)} %get-tuple-element.71.refs_0_.refs_2_.refs_4_.refs_3_, s32[1]{0:T(128)} %constant.40.clone.1.refs_1_.mine, bf16[8,3,256,128]{3,2,1,0:T(8,128)(2,1)} %all-to-all-done.refs_2_.refs_6_.refs_8_.refs_10_.refs_7_, ...), custom_call_target="tpu_custom_call" | custom-call | flops 38654705664 | bytes 16777216 | tf_op jit(solution)/shard_map/attention_forward/pallas_call | solution.py:254
  118.7 2.9 collective-permute-start.3
  121.6 31.9 %attention_forward.3 = (bf16[8,512,128]{2,1,0:T(8,128)(2,1)}, f32[8,8,512]{2,1,0:T(8,128)}) custom-call(s32[8]{0:T(128)} %get-tuple-element.71.refs_0_.refs_2_.refs_4_.refs_3_, s32[1]{0:T(128)} %get-tuple-element.76.refs_1_, bf16[8,3,256,128]{3,2,1,0:T(8,128)(2,1)} %all-to-all-done.refs_2_.refs_6_.refs_8_.refs_10_.refs_7_, ...), custom_call_target="tpu_custom_call" | custom-call | flops 38654705664 | bytes 16777216 | tf_op jit(solution)/shard_map/attention_forward/pallas_call | solution.py:254
  153.5 4.4 all-to-all-start.2
  159.3 3.4 copy-done.27
  162.7 6.6 %pull_down.1 = (bf16[512,4096]{1,0:T(8,128)(2,1)S(1)}, bf16[1024,512]{1,0:T(8,128)(2,1)S(1)}) custom-call(bf16[512,1024]{1,0:T(8,128)(2,1)S(1)} %pad_maximum_fusion.1.cotangent.refs_2_, f32[1,6144]{1,0:T(1,128)S(1)} %fusion.8.mod.refs_3_.refs_9_, bf16[4096,1024]{1,0:T(8,128)(2,1)S(1)} %copy-done.27), custom_call_target="tpu_custom_call" | custom-call | flops 4294967296 | bytes 14680064 | tf_op jit(solution)/shard_map/pull_down/pallas_call | solution.py:522
  173.3 25.0 %middle_block.1 = (f32[512,1024]{1,0:T(8,128)}, bf16[512,1024]{1,0:T(8,128)(2,1)}, bf16[512,4096]{1,0:T(8,128)(2,1)}, bf16[512,4096]{1,0:T(8,128)(2,1)}, f32[512...) custom-call(bf16[8,512,128]{2,1,0:T(8,128)(2,1)} %all-to-all-done.2., ...), custom_call_target="tpu_custom_call" | custom-call | flops 10737418240 | bytes 31457280 | tf_op jit(solution)/shard_map/middle_block/pallas_call | solution.py:604
  198.4 12.2 %weight_gradients.3 = (bf16[4,4,1024,128]{3,2,1,0:T(8,128)(2,1)}, bf16[4,128,5120]{2,1,0:T(8,128)(2,1)}) custom-call(s32[1]{0:T(128)} %bitcast.slot, bf16[512,4096]{1,0:T(8,128)(2,1)} %get-tuple-element.82.active.refs_0_, bf16[512,4096]{1,0:T(8,128)(2,1)} %get-tuple-element.83.grad_up_in, bf16[512,1024]{1,0:T(8,128)(2,1)} %get-tuple-element.84.hidden, ...), custom_call_target="tpu_custom_call" | custom-call | flops 4831838208 | bytes 25165824 | tf_op jit(solution)/shard_map/weight_gradients/pallas_call | solution.py:733
  212.6 4.6 all-to-all-start.3
  217.9 19.9 %weight_gradients.2 = (bf16[512,1024]{1,0:T(8,128)(2,1)}, f32[1,1024]{1,0:T(1,128)}, bf16[4,4,1024,128]{3,2,1,0:T(8,128)(2,1)}, bf16[4,128,5120]{2,1,0:T(8,128)(2,1)}) custom-call(s32[1]{0:T(128)} %bitcast.slot, bf16[512,4096]{1,0:T(8,128)(2,1)} %get-tuple-element.82.active.refs_0_, bf16[512,4096]{1,0:T(8,128)(2,1)} %get-tuple-element.83.grad_up_in, ...), custom_call_target="tpu_custom_call" | custom-call | flops 9126805504 | bytes 25165824 | tf_op jit(solution)/shard_map/weight_gradients/pallas_call | solution.py:733
  240.4 5.9 %add_halves.8 = (bf16[2,4,1024,128]{3,2,1,0:T(8,128)(2,1)}, bf16[2,4,1024,128]{3,2,1,0:T(8,128)(2,1)}) custom-call(s32[1]{0:T(128)} %constant.40.clone.1.refs_1_.mine, bf16[2,2,4,1024,128]{4,3,2,1,0:T(8,128)(2,1)} %bitcast.64, bf16[2,2,4,1024,128]{4,3,2,1,0:T(8,128)(2,1)} %bitcast.17.refs_1_.refs_3_, bf16[2,2,4,1024,128]{4,3,2,1,0:T(8,128)(2,1)} %bitcast.65, ...), custom_call_target="tpu_custom_call" | custom-call | flops 2097152 | bytes 12582912 | tf_op jit(solution)/shard_map/add_halves/pallas_call | solution.py:905
  248.2 6.8 %add_halves.9 = (bf16[1,8,32,5120]{3,2,1,0:T(8,128)(2,1)}, bf16[1,8,32,5120]{3,2,1,0:T(8,128)(2,1)}) custom-call(s32[1]{0:T(128)} %constant.40.clone.1.refs_1_.mine, bf16[1,2,8,32,5120]{4,3,2,1,0:T(8,128)(2,1)} %bitcast.62, bf16[1,2,8,32,5120]{4,3,2,1,0:T(8,128)(2,1)} %bitcast.20.refs_1_.refs_3_, bf16[1,2,8,32,5120]{4,3,2,1,0:T(8,128)(2,1)} %bitcast.63, ...), custom_call_target="tpu_custom_call" | custom-call | flops 2621440 | bytes 15728640 | tf_op jit(solution)/shard_map/add_halves/pallas_call | solution.py:905
  258.0 2.4 copy.27
  260.4 3.8 all-to-all-start.4
  264.2 54.9 %attention_backward.3 = (f32[8,128,512]{2,1,0:T(8,128)}, bf16[8,2,256,128]{3,2,1,0:T(8,128)(2,1)}, bf16[8,2,256,128]{3,2,1,0:T(8,128)(2,1)}) custom-call(bf16[2,2,2,1024,128]{4,3,2,1,0:T(8,128)(2,1)} %bitcast.93, bf16[2,2,2,32,5120]{4,3,2,1,0:T(8,128)(2,1)} %bitcast.87, s32[8]{0:T(128)} %get-tuple-element.71.refs_0_.refs_2_.refs_4_.refs_3_, ...), custom_call_target="tpu_custom_call" | custom-call | flops 60397977600 | bytes 16777216 | tf_op jit(solution)/shard_map/attention_backward/pallas_call | solution.py:401
  321.1 11.8 %all-to-all-done.4 = f32[32,1,4128]{2,1,0:T(1,128)S(1)} async-done(((f32[32,1,4128]{2,1,0:T(1,128)}), f32[32,1,4128]{2,1,0:T(1,128)S(1)}, u32[]{:S(2)}, u32[]{:S(2)}) %all-to-all-start.4) | async-done | bytes 528416 | tf_op jit(solution)/shard_map/all_to_all | solution.py:1200
  333.7 3.6 add_halves.10
  339.1 3.8 add_halves.11
  344.6 31.7 %attention_backward.4 = (f32[8,128,512]{2,1,0:T(8,128)}, bf16[8,2,256,128]{3,2,1,0:T(8,128)(2,1)}) custom-call(bf16[2,2,1024,128]{3,2,1,0:T(8,128)(2,1)} %bitcast.109, bf16[2,2,32,5120]{3,2,1,0:T(8,128)(2,1)} %bitcast.107, bf16[256,1024]{1,0:T(8,128)(2,1)} %collective-permute-done.4.refs_2_, f32[32,4128]{1,0:T(8,128)} %bitcast.89, ...), custom_call_target="tpu_custom_call" | custom-call | flops 30198988800 | bytes 16777216 | tf_op jit(solution)/shard_map/attention_backward/pallas_call | solution.py:401
  376.2 2.5 add_halves.12
  380.2 2.5 add_convert_fusion.refs_2_
  382.7 4.0 all-to-all-start.5
  387.7 2.6 add_halves.13
  390.9 32.3 %attention_backward.5.unused_3_ = bf16[8,4,256,128]{3,2,1,0:T(8,128)(2,1)} custom-call(bf16[2,1024,128]{2,1,0:T(8,128)(2,1)} %bitcast.113, bf16[2,32,5120]{2,1,0:T(8,128)(2,1)} %bitcast.111, bf16[8,2,256,128]{3,2,1,0:T(8,128)(2,1)} %add_convert_fusion.refs_2_, s32[8]{0:T(128)} %get-tuple-element.71.refs_0_.refs_2_.refs_4_.refs_3_, ...), custom_call_target="tpu_custom_call" | custom-call | flops 30198988800 | bytes 16777216 | tf_op jit(solution)/shard_map/attention_backward/pallas_call | solution.py:401
  425.1 4.4 all-to-all-start.6
  429.5 2.2 add_halves.15
  431.7 2.4 collective-permute-start.17
  436.9 3.4 copy-done.6
  442.2 8.2 %head_gradients.1.refs_0_ = bf16[1024,384]{1,0:T(8,128)(2,1)S(1)} custom-call(bf16[1024,128]{1,0:T(8,128)(2,1)S(1)} %bitcast.61, bf16[32,5120]{1,0:T(8,128)(2,1)S(1)} %bitcast.59, bf16[8,2,256,128]{3,2,1,0:T(8,128)(2,1)} %add_convert_fusion.refs_2_, bf16[8,4,256,128]{3,2,1,0:T(8,128)(2,1)S(1)} %copy-done, bf16[8,1024,512]{2,1,0:T(8,128)(2,1)S(1)} %bitcast.55, ...), custom_call_target="tpu_custom_call" | custom-call | flops 3221225472 | bytes 12582912 | tf_op jit(solution)/shard_map/head_gradients/pallas_call | solution.py:799
  451.3 9.9 %collective-permute-done.16.unused_1_.refs_2_ = bf16[1024,128]{1,0:T(8,128)(2,1)} collective-permute-done((bf16[1024,128]{1,0:T(8,128)(2,1)}, bf16[1024,128]{1,0:T(8,128)(2,1)}, u32[]{:S(2)}, u32[]{:S(2)}) %collective-permute-start.16) | collective-permute-done | bytes 262176 | tf_op jit(solution)/shard_map/ppermute | solution.py:1136
  461.2 6.0 %all-to-all-start.7 = ((bf16[32,32,384]{2,1,0:T(8,128)(2,1)}), bf16[32,32,384]{2,1,0:T(8,128)(2,1)}, u32[]{:S(2)}, u32[]{:S(2)}) async-start(bf16[32,32,384]{2,1,0:T(8,128)(2,1)} %bitcast.72), calls=%async_computation.7 | async-start | bytes 1572864 | tf_op jit(solution)/shard_map/all_to_all | solution.py:1240
  468.4 9.4 %input_gradients.1 = (bf16[512,1024]{1,0:T(8,128)(2,1)S(1)}, f32[1,1024]{1,0:T(1,128)S(1)}, f32[1,1024]{1,0:T(1,128)S(1)}) custom-call(bf16[1024,384]{1,0:T(8,128)(2,1)S(1)} %head_gradients.1.refs_0_, bf16[8,2,256,128]{3,2,1,0:T(8,128)(2,1)S(1)} %copy-done.3, bf16[8,4,256,128]{3,2,1,0:T(8,128)(2,1)} %all-to-all-done.6.refs_2_.unused_0_, ...), custom_call_target="tpu_custom_call" | custom-call | flops 3221225472 | bytes 14680064 | tf_op jit(solution)/shard_map/input_gradients/pallas_call | solution.py:859
  477.9 2.9 collective-permute-start.15
  481.9 16.1 %all-to-all-done.7.unused_0_ = bf16[32,32,384]{2,1,0:T(8,128)(2,1)} async-done(((bf16[32,32,384]{2,1,0:T(8,128)(2,1)}), bf16[32,32,384]{2,1,0:T(8,128)(2,1)}, u32[]{:S(2)}, u32[]{:S(2)}) %all-to-all-start.7) | async-done | bytes 786464 | tf_op jit(solution)/shard_map/all_to_all | solution.py:1240
  498.7 4.4 all-to-all-start.8
  517.8 2.9 mod_gradient.1
  (157 shorter events, 60.6 us)
Async XLA Ops:
  7.2 6.8 %copy-start.39 = (s32[1,2]{1,0:T(1,128)S(1)}, s32[1,2]{1,0:T(1,128)}, u32[]{:S(2)}) copy-start(s32[1,2]{1,0:T(1,128)} %param.14) | copy-start | bytes 28
  9.9 27.4 %collective-permute-start = (bf16[256,1024]{1,0:T(8,128)(2,1)}, bf16[256,1024]{1,0:T(8,128)(2,1)S(1)}, u32[]{:S(2)}, u32[]{:S(2)}) collective-permute-start(bf16[256,1024]{1,0:T(8,128)(2,1)} %bitcast.1), channel_id=1, source_target_pairs={{0,2},{2,0},{1,3},{3,1},{4,6},{6,4},{5,7},{7,5},{8,10},{10,8},{9,1... | collective-permute-start | bytes 1572872 | tf_op jit(solution)/shard_map/ppermute | solution.py:1087
  15.9 11.0 %copy-start.1 = (bf16[1024,1024]{1,0:T(8,128)(2,1)S(1)}, bf16[1024,1024]{1,0:T(8,128)(2,1)}, u32[]{:S(2)}) copy-start(bf16[1024,1024]{1,0:T(8,128)(2,1)} %refs_3_.1) | copy-start | bytes 6291460
  22.4 136.9 %copy-start.19 = (f32[1,6144]{1,0:T(1,128)}, f32[1,6144]{1,0:T(1,128)S(1)}, u32[]{:S(2)}) copy-start(f32[1,6144]{1,0:T(1,128)S(1)} %fusion.8.mod.refs_3_.refs_9_) | copy-start | bytes 73732
  38.1 4.4 copy-start.9
  38.1 25.5 %all-to-all-start = ((bf16[8,3,256,128]{3,2,1,0:T(8,128)(2,1)}), bf16[8,3,256,128]{3,2,1,0:T(8,128)(2,1)}, u32[]{:S(2)}, u32[]{:S(2)}) async-start(bf16[8,3,256,128]{3,2,1,0:T(8,128)(2,1)} %order_after.5), calls=%async_computation | async-start | bytes 3145728 | tf_op jit(solution)/shard_map/all_to_all | solution.py:1095
  50.2 17.0 %copy-start.40 = (s32[8]{0:T(128)S(1)}, s32[8]{0:T(128)}, u32[]{:S(2)}) copy-start(s32[8]{0:T(128)} %times.1) | copy-start | bytes 100
  63.6 24.5 %all-to-all-start.1 = ((bf16[8,3,256,128]{3,2,1,0:T(8,128)(2,1)}), bf16[8,3,256,128]{3,2,1,0:T(8,128)(2,1)S(1)}, u32[]{:S(2)}, u32[]{:S(2)}) async-start(bf16[8,3,256,128]{3,2,1,0:T(8,128)(2,1)} %copy-done.11), calls=%async_computation.1 | async-start | bytes 3145728 | tf_op jit(solution)/shard_map/all_to_all | solution.py:1095
  70.4 47.9 %collective-permute-start.1 = (bf16[8,2,256,128]{3,2,1,0:T(8,128)(2,1)}, bf16[8,2,256,128]{3,2,1,0:T(8,128)(2,1)}, u32[]{:S(2)}, u32[]{:S(2)}) collective-permute-start(bf16[8,2,256,128]{3,2,1,0:T(8,128)(2,1)} %slice.56), channel_id=1, source_target_pairs={{0,1},{1,0},{2,3},{3,2},{4,5},{5,4},{6,7},{7,6},{8,9},{9,8},{10,11... | collective-permute-start | bytes 3145736 | tf_op jit(solution)/shard_map/ppermute | solution.py:1098
  88.2 30.5 %collective-permute-start.2 = (bf16[8,2,256,128]{3,2,1,0:T(8,128)(2,1)S(1)}, bf16[8,2,256,128]{3,2,1,0:T(8,128)(2,1)}, u32[]{:S(2)}, u32[]{:S(2)}) collective-permute-start(bf16[8,2,256,128]{3,2,1,0:T(8,128)(2,1)S(1)} %slice.57), channel_id=1, source_target_pairs={{0,1},{1,0},{2,3},{3,2},{4,5},{5,4},{6,7},{7,6},{8,9},{9,8},{10,11... | collective-permute-start | bytes 3145736 | tf_op jit(solution)/shard_map/ppermute | solution.py:1098
  118.7 40.5 %collective-permute-start.3 = (bf16[256,1024]{1,0:T(8,128)(2,1)}, bf16[256,1024]{1,0:T(8,128)(2,1)S(1)}, u32[]{:S(2)}, u32[]{:S(2)}) collective-permute-start(bf16[256,1024]{1,0:T(8,128)(2,1)} %order_after.6), channel_id=1, source_target_pairs={{0,2},{2,0},{1,3},{3,1},{4,6},{6,4},{5,7},{7,5},{8,10},{10,8},{9,1... | collective-permute-start | bytes 1572872 | tf_op jit(solution)/shard_map/ppermute | solution.py:1087
  153.5 5.7 %copy-start.35 = (bf16[1,1,8,32,1024]{4,3,2,1,0:T(8,128)(2,1)S(1)}, bf16[1,1,8,32,1024]{4,3,2,1,0:T(8,128)(2,1)}, u32[]{:S(2)}) copy-start(bf16[1,1,8,32,1024]{4,3,2,1,0:T(8,128)(2,1)} %get-tuple-element.155) | copy-start | bytes 1572868
  153.5 19.8 %all-to-all-start.2 = ((bf16[8,512,128]{2,1,0:T(8,128)(2,1)}), bf16[8,512,128]{2,1,0:T(8,128)(2,1)}, u32[]{:S(2)}, u32[]{:S(2)}) async-start(bf16[8,512,128]{2,1,0:T(8,128)(2,1)} %get-tuple-element.80.refs_4_.refs_6_.refs_5_), calls=%async_computation.2 | async-start | bytes 2097152 | tf_op jit(solution)/shard_map/all_to_all | solution.py:1095
  157.9 279.0 %all-gather.3.cloned.1.call-start = ((), (), s32[]{:S(2)}) async-start(), calls=%async_computation.9 | async-start | bytes 9437184 | tf_op jit(solution)/shard_map/all_gather | solution.py:1169
  159.3 3.4 copy-start.27
  162.6 6.6 %copy-start.12 = (bf16[512,1024]{1,0:T(8,128)(2,1)}, bf16[512,1024]{1,0:T(8,128)(2,1)S(1)}, u32[]{:S(2)}) copy-start(bf16[512,1024]{1,0:T(8,128)(2,1)S(1)} %pad_maximum_fusion.1.cotangent.refs_2_) | copy-start | bytes 3145732
  171.2 27.1 %copy-start.29 = (bf16[1024,512]{1,0:T(8,128)(2,1)}, bf16[1024,512]{1,0:T(8,128)(2,1)S(1)}, u32[]{:S(2)}) copy-start(bf16[1024,512]{1,0:T(8,128)(2,1)S(1)} %get-tuple-element.85.scaled_turned) | copy-start | bytes 3145732
  198.3 12.8 %copy-start.16 = (bf16[256,1024]{1,0:T(8,128)(2,1)S(1)}, bf16[256,1024]{1,0:T(8,128)(2,1)}, u32[]{:S(2)}) copy-start(bf16[256,1024]{1,0:T(8,128)(2,1)} %copy-done.15) | copy-start | bytes 1572868
  198.3 12.8 %copy-start.18 = (bf16[256,1024]{1,0:T(8,128)(2,1)S(1)}, bf16[256,1024]{1,0:T(8,128)(2,1)}, u32[]{:S(2)}) copy-start(bf16[256,1024]{1,0:T(8,128)(2,1)} %copy-done.17) | copy-start | bytes 1572868
  210.6 37.6 %collective-permute-start.6 = (bf16[4,128,5120]{2,1,0:T(8,128)(2,1)}, bf16[4,128,5120]{2,1,0:T(8,128)(2,1)}, u32[]{:S(2)}, u32[]{:S(2)}) collective-permute-start(bf16[4,128,5120]{2,1,0:T(8,128)(2,1)} %get-tuple-element.93), channel_id=1, source_target_pairs={{0,4},{4,0},{8,12},{12,8},{16,20},{20,16},{24,28},{28,24},{1,5},{5... | collective-permute-start | bytes 15728648 | tf_op jit(solution)/shard_map/ppermute | solution.py:1101
  210.6 29.8 %collective-permute-start.5 = (bf16[4,4,1024,128]{3,2,1,0:T(8,128)(2,1)}, bf16[4,4,1024,128]{3,2,1,0:T(8,128)(2,1)}, u32[]{:S(2)}, u32[]{:S(2)}) collective-permute-start(bf16[4,4,1024,128]{3,2,1,0:T(8,128)(2,1)} %get-tuple-element.90), channel_id=1, source_target_pairs={{0,4},{4,0},{8,12},{12,8},{16,20},{20,16},{24,28},{28,24},{1,5},{5... | collective-permute-start | bytes 12582920 | tf_op jit(solution)/shard_map/ppermute | solution.py:1101
  212.6 43.8 %all-to-all-start.3 = ((bf16[8,512,128]{2,1,0:T(8,128)(2,1)}), bf16[8,512,128]{2,1,0:T(8,128)(2,1)}, u32[]{:S(2)}, u32[]{:S(2)}) async-start(bf16[8,512,128]{2,1,0:T(8,128)(2,1)} %get-tuple-element.95), calls=%async_computation.3 | async-start | bytes 2097152 | tf_op jit(solution)/shard_map/all_to_all | solution.py:1095
  239.7 104.9 %collective-permute-start.4 = (bf16[256,1024]{1,0:T(8,128)(2,1)}, bf16[256,1024]{1,0:T(8,128)(2,1)}, u32[]{:S(2)}, u32[]{:S(2)}) collective-permute-start(bf16[256,1024]{1,0:T(8,128)(2,1)} %slice.51), channel_id=1, source_target_pairs={{0,2},{2,0},{1,3},{3,1},{4,6},{6,4},{5,7},{7,5},{8,10},{10,8},{9,1... | collective-permute-start | bytes 1572872 | tf_op jit(solution)/shard_map/ppermute | solution.py:1087
  246.3 87.4 %collective-permute-start.7 = (bf16[2,2,2,1024,128]{4,3,2,1,0:T(8,128)(2,1)}, bf16[2,2,2,1024,128]{4,3,2,1,0:T(8,128)(2,1)}, u32[]{:S(2)}, u32[]{:S(2)}) collective-permute-start(bf16[2,2,2,1024,128]{4,3,2,1,0:T(8,128)(2,1)} %bitcast.91), channel_id=1, source_target_pairs={{0,8},{4,12},{8,0},{12,4},{16,24},{20,28},{24,16},{28,20},{1,9},{5... | collective-permute-start | bytes 6291464 | tf_op jit(solution)/shard_map/ppermute | solution.py:1136
  254.9 82.7 %collective-permute-start.8 = (bf16[2,2,2,32,5120]{4,3,2,1,0:T(8,128)(2,1)}, bf16[2,2,2,32,5120]{4,3,2,1,0:T(8,128)(2,1)S(1)}, u32[]{:S(2)}, u32[]{:S(2)}) collective-permute-start(bf16[2,2,2,32,5120]{4,3,2,1,0:T(8,128)(2,1)} %bitcast.85), channel_id=1, source_target_pairs={{0,16},{4,20},{8,24},{12,28},{16,0},{20,4},{24,8},{28,12},{1,17},{... | collective-permute-start | bytes 7864328 | tf_op jit(solution)/shard_map/ppermute | solution.py:1136
  260.4 72.5 %all-to-all-start.4 = ((f32[32,1,4128]{2,1,0:T(1,128)}), f32[32,1,4128]{2,1,0:T(1,128)S(1)}, u32[]{:S(2)}, u32[]{:S(2)}) async-start(f32[32,1,4128]{2,1,0:T(1,128)} %copy.27), calls=%async_computation.4 | async-start | bytes 1081344 | tf_op jit(solution)/shard_map/all_to_all | solution.py:1200
  319.1 61.1 %collective-permute-start.13 = (bf16[8,2,256,128]{3,2,1,0:T(8,128)(2,1)}, bf16[8,2,256,128]{3,2,1,0:T(8,128)(2,1)}, u32[]{:S(2)}, u32[]{:S(2)}) collective-permute-start(bf16[8,2,256,128]{3,2,1,0:T(8,128)(2,1)} %get-tuple-element.112), channel_id=1, source_target_pairs={{0,1},{1,0},{2,3},{3,2},{4,5},{5,4},{6,7},{7,6},{8,9},{9,8},{10,11... | collective-permute-start | bytes 3145736 | tf_op jit(solution)/shard_map/ppermute | solution.py:1098
  320.9 70.0 %collective-permute-start.14 = (bf16[8,2,256,128]{3,2,1,0:T(8,128)(2,1)}, bf16[8,2,256,128]{3,2,1,0:T(8,128)(2,1)}, u32[]{:S(2)}, u32[]{:S(2)}) collective-permute-start(bf16[8,2,256,128]{3,2,1,0:T(8,128)(2,1)} %get-tuple-element.113), channel_id=1, source_target_pairs={{0,1},{1,0},{2,3},{3,2},{4,5},{5,4},{6,7},{7,6},{8,9},{9,8},{10,11... | collective-permute-start | bytes 3145736 | tf_op jit(solution)/shard_map/ppermute | solution.py:1098
  337.3 38.9 %collective-permute-start.9 = (bf16[2,2,1024,128]{3,2,1,0:T(8,128)(2,1)}, bf16[2,2,1024,128]{3,2,1,0:T(8,128)(2,1)}, u32[]{:S(2)}, u32[]{:S(2)}) collective-permute-start(bf16[2,2,1024,128]{3,2,1,0:T(8,128)(2,1)} %bitcast.108), channel_id=1, source_target_pairs={{0,16},{4,20},{8,24},{12,28},{16,0},{20,4},{24,8},{28,12},{1,17},{... | collective-permute-start | bytes 3145736 | tf_op jit(solution)/shard_map/ppermute | solution.py:1136
  342.8 43.8 %collective-permute-start.11 = (bf16[2,2,32,5120]{3,2,1,0:T(8,128)(2,1)}, bf16[2,2,32,5120]{3,2,1,0:T(8,128)(2,1)S(1)}, u32[]{:S(2)}, u32[]{:S(2)}) collective-permute-start(bf16[2,2,32,5120]{3,2,1,0:T(8,128)(2,1)} %bitcast.106), channel_id=1, source_target_pairs={{0,8},{4,12},{8,0},{12,4},{16,24},{20,28},{24,16},{28,20},{1,9},{5... | collective-permute-start | bytes 3932168 | tf_op jit(solution)/shard_map/ppermute | solution.py:1136
  376.2 4.0 copy-start.36
  378.7 44.4 %collective-permute-start.10 = (bf16[2,1024,128]{2,1,0:T(8,128)(2,1)}, bf16[2,1024,128]{2,1,0:T(8,128)(2,1)S(1)}, u32[]{:S(2)}, u32[]{:S(2)}) collective-permute-start(bf16[2,1024,128]{2,1,0:T(8,128)(2,1)} %bitcast.112), channel_id=1, source_target_pairs={{0,1},{1,0},{2,3},{3,2},{4,5},{5,4},{6,7},{7,6},{8,9},{9,8},{10,11... | collective-permute-start | bytes 1572872 | tf_op jit(solution)/shard_map/ppermute | solution.py:1136
  382.7 40.5 %all-to-all-start.5 = ((bf16[8,2,256,128]{3,2,1,0:T(8,128)(2,1)}), bf16[8,2,256,128]{3,2,1,0:T(8,128)(2,1)S(1)}, u32[]{:S(2)}, u32[]{:S(2)}) async-start(bf16[8,2,256,128]{3,2,1,0:T(8,128)(2,1)} %add_convert_fusion.refs_2_), calls=%async_computation.5 | async-start | bytes 2097152 | tf_op jit(solution)/shard_map/all_to_all | solution.py:1095
  390.3 32.9 %collective-permute-start.12 = (bf16[2,32,5120]{2,1,0:T(8,128)(2,1)}, bf16[2,32,5120]{2,1,0:T(8,128)(2,1)S(1)}, u32[]{:S(2)}, u32[]{:S(2)}) collective-permute-start(bf16[2,32,5120]{2,1,0:T(8,128)(2,1)} %bitcast.110), channel_id=1, source_target_pairs={{0,1},{1,0},{2,3},{3,2},{4,5},{5,4},{6,7},{7,6},{8,9},{9,8},{10,11... | collective-permute-start | bytes 1966088 | tf_op jit(solution)/shard_map/ppermute | solution.py:1136
  425.1 36.0 %all-to-all-start.6 = ((bf16[8,4,256,128]{3,2,1,0:T(8,128)(2,1)}), bf16[8,4,256,128]{3,2,1,0:T(8,128)(2,1)}, u32[]{:S(2)}, u32[]{:S(2)}) async-start(bf16[8,4,256,128]{3,2,1,0:T(8,128)(2,1)} %order_after.7.refs_0_.refs_3_), calls=%async_computation.6 | async-start | bytes 4194304 | tf_op jit(solution)/shard_map/all_to_all | solution.py:1095
  431.7 29.5 %collective-permute-start.17 = (bf16[32,5120]{1,0:T(8,128)(2,1)}, bf16[32,5120]{1,0:T(8,128)(2,1)}, u32[]{:S(2)}, u32[]{:S(2)}) collective-permute-start(bf16[32,5120]{1,0:T(8,128)(2,1)} %bitcast.58), channel_id=1, source_target_pairs={{0,2},{2,0},{1,3},{3,1},{4,6},{6,4},{5,7},{7,5},{8,10},{10,8},{9,1... | collective-permute-start | bytes 983048 | tf_op jit(solution)/shard_map/ppermute | solution.py:1136
  436.3 24.8 %collective-permute-start.16 = (bf16[1024,128]{1,0:T(8,128)(2,1)}, bf16[1024,128]{1,0:T(8,128)(2,1)}, u32[]{:S(2)}, u32[]{:S(2)}) collective-permute-start(bf16[1024,128]{1,0:T(8,128)(2,1)} %bitcast.60), channel_id=1, source_target_pairs={{0,2},{2,0},{1,3},{3,1},{4,6},{6,4},{5,7},{7,5},{8,10},{10,8},{9,1... | collective-permute-start | bytes 786440 | tf_op jit(solution)/shard_map/ppermute | solution.py:1136
  436.9 3.4 copy-start.6
  451.3 15.9 %copy-start.3 = (bf16[8,2,256,128]{3,2,1,0:T(8,128)(2,1)S(1)}, bf16[8,2,256,128]{3,2,1,0:T(8,128)(2,1)}, u32[]{:S(2)}) copy-start(bf16[8,2,256,128]{3,2,1,0:T(8,128)(2,1)} %copy-done.2) | copy-start | bytes 3145732
  451.3 15.9 %copy-start.13 = (f32[512,128]{1,0:T(8,128)S(1)}, f32[512,128]{1,0:T(8,128)}, u32[]{:S(2)}) copy-start(f32[512,128]{1,0:T(8,128)} %get-tuple-element.72.refs_6_) | copy-start | bytes 786436
  451.3 15.9 %copy-start.14 = (f32[512,128]{1,0:T(8,128)S(1)}, f32[512,128]{1,0:T(8,128)}, u32[]{:S(2)}) copy-start(f32[512,128]{1,0:T(8,128)} %get-tuple-element.73.refs_7_) | copy-start | bytes 786436
  451.3 15.9 %copy-start.20 = (f32[1,6144]{1,0:T(1,128)S(1)}, f32[1,6144]{1,0:T(1,128)}, u32[]{:S(2)}) copy-start(f32[1,6144]{1,0:T(1,128)} %copy-done.19) | copy-start | bytes 73732
  461.2 36.8 %all-to-all-start.7 = ((bf16[32,32,384]{2,1,0:T(8,128)(2,1)}), bf16[32,32,384]{2,1,0:T(8,128)(2,1)}, u32[]{:S(2)}, u32[]{:S(2)}) async-start(bf16[32,32,384]{2,1,0:T(8,128)(2,1)} %bitcast.72), calls=%async_computation.7 | async-start | bytes 1572864 | tf_op jit(solution)/shard_map/all_to_all | solution.py:1240
  468.4 12.3 %copy-start.37 = (bf16[512,1024]{1,0:T(8,128)(2,1)S(1)}, bf16[512,1024]{1,0:T(8,128)(2,1)}, u32[]{:S(2)}) copy-start(bf16[512,1024]{1,0:T(8,128)(2,1)} %get-tuple-element.88) | copy-start | bytes 3145732
  477.8 20.9 %copy-start.4 = (bf16[512,1024]{1,0:T(8,128)(2,1)}, bf16[512,1024]{1,0:T(8,128)(2,1)S(1)}, u32[]{:S(2)}) copy-start(bf16[512,1024]{1,0:T(8,128)(2,1)S(1)} %get-tuple-element.125.refs_0_) | copy-start | bytes 3145732
  477.9 35.7 %collective-permute-start.15 = (bf16[256,1024]{1,0:T(8,128)(2,1)S(1)}, bf16[256,1024]{1,0:T(8,128)(2,1)S(1)}, u32[]{:S(2)}, u32[]{:S(2)}) collective-permute-start(bf16[256,1024]{1,0:T(8,128)(2,1)S(1)} %slice.53), channel_id=1, source_target_pairs={{0,2},{2,0},{1,3},{3,1},{4,6},{6,4},{5,7},{7,5},{8,10},{10,8},{9,1... | collective-permute-start | bytes 1572872 | tf_op jit(solution)/shard_map/ppermute | solution.py:1087
  498.7 18.3 %all-to-all-start.8 = ((f32[32,16,128]{2,1,0:T(8,128)}), f32[32,16,128]{2,1,0:T(8,128)S(1)}, u32[]{:S(2)}, u32[]{:S(2)}) async-start(f32[32,16,128]{2,1,0:T(8,128)} %order_after.9), calls=%async_computation.8 | async-start | bytes 524288 | tf_op jit(solution)/shard_map/all_to_all | solution.py:1252
  507.7 5.9 %copy-start.5 = (bf16[512,1024]{1,0:T(8,128)(2,1)S(1)}, bf16[512,1024]{1,0:T(8,128)(2,1)}, u32[]{:S(2)}) copy-start(bf16[512,1024]{1,0:T(8,128)(2,1)} %copy-done.4) | copy-start | bytes 3145732
  (21 other events, 30.6 us)
Sparse Core Ops, SparseCore 0:
  212.6 86.2 all-gather.2

commit v5 on v4

--- a/solution.py
+++ b/solution.py
@@ -952,15 +952,15 @@
     *vectors, codes, packed = refs
     at = 0
     for vector in vectors:
-        packed[:, at : at + D] = jnp.broadcast_to(vector[...], (packed.shape[0], D))
+        packed[:, at : at + D] = jnp.broadcast_to(vector[...], (packed.shape[0], D)).astype(LOW)
         at += D
-    packed[:, at:] = codes[...]
+    packed[:, at:] = codes[...].astype(LOW)
 
 
 def pack(vectors, codes, after):
     return pl.pallas_call(
         behind(pack_kernel, len(after)),
-        out_shape=jax.ShapeDtypeStruct((codes.shape[0], len(vectors) * D + codes.shape[1]), WIDE),
+        out_shape=jax.ShapeDtypeStruct((codes.shape[0], len(vectors) * D + codes.shape[1]), LOW),
         in_specs=anywhere(len(after)) + [vmem()] * (len(vectors) + 1),
         out_specs=vmem(),
         name="pack",
@@ -1035,12 +1035,13 @@
 def mod_kernel(early, late, out):
     kept = late.shape[1] * late.shape[2]
     vectors = 6 * D - kept
-    codes = early[:, vectors:]
+    first, second = early[...].astype(WIDE), late[...].astype(WIDE)
+    codes = first[:, vectors:]
     by_rows = (((0,), (0,)), ((), ()))
-    out[:, kept:] = exact_dot(codes, early[:, :vectors], by_rows)
+    out[:, kept:] = exact_dot(codes, first[:, :vectors], by_rows)
     wide = late.shape[2]
     for c in range(late.shape[1]):
-        out[:, c * wide : (c + 1) * wide] = exact_dot(codes, late[:, c, :], by_rows)
+        out[:, c * wide : (c + 1) * wide] = exact_dot(codes, second[:, c, :], by_rows)
 
 
 def mod_gradient(early, late):
@@ -1248,7 +1249,7 @@
     in_came = other_half(grad_source[half_count:])
     totals = sum_columns(product.reshape(frames, row_total, D // devices, 3 * lanes))
     late = jnp.concatenate([grad_shift_one, grad_scale_one], axis=-1).reshape(1, -1, 128)
-    late = jnp.broadcast_to(late, (devices,) + late.shape[1:])
+    late = jnp.broadcast_to(late.astype(LOW), (devices,) + late.shape[1:])
     late_came = lax.all_to_all(order_after(late, (product,)), everyone, split_axis=0, concat_axis=0, tiled=True)
 
     grad_down = down.finish((grad_source,)).reshape(D, FF // devices).T

time: 537 us -> 532 us (level)
    all_to_all x1, waiting for transfers between devices: 16.1 us -> 6.76 us  [shards(): lax.all_to_all(ordered.reshape(devices, D // devices, 3 * lanes), everyon...]
    ppermute x4, waiting for transfers between devices: 2.8 us -> 11.8 us  [other_half(): return lax.ppermute(array, 'half', [(0, 1), (1, 0)])]
    unnamed x85 -> x87, local copies, waits for them, and re-layouts: 25.7 us -> 25.6 us
  transfers between devices with their start and end apart: 28 -> 28, of which waited for: 8 -> 9; matrix products, arithmetic and copies ran while one was open for 6% -> 6% of each run, Pallas kernels for 52% -> 53%
where the time goes in v5:
time: 532 us; the launch traced here: 523 us
  Pallas kernels  316 us (59%)
  waiting for transfers between devices  69.3 us (13%)
  starting transfers between devices  64.8 us (12%)
  local copies, waits for them, and re-layouts  39 us (7%)
  between operations  16.1 us (3%)
  other arithmetic  11.4 us (2%)
  matrix products  6.46 us (1%)
    pallas_call x3, Pallas kernels, attention_backward(): pl.pallas_call(behind(functools.partial(backward_kernel, parts=parts, sou...  119 us
    pallas_call x2, Pallas kernels, attention_forward(): pl.pallas_call(behind(functools.partial(forward_kernel, parts=parts, own=...  61 us
    all_to_all x6, waiting for transfers between devices, swap_groups(): lax.all_to_all(grouped, 'frames', split_axis=0, concat_axis=0, tiled=True)  32.2 us
    pallas_call x2, Pallas kernels, weight_gradients(): pl.pallas_call(functools.partial(weights_kernel, keep=keep), grid_spec=pl...  32.2 us
    pallas_call x8, Pallas kernels, add_halves(): pl.pallas_call(ordered, grid_spec=pltpu.PrefetchScalarGridSpec(num_scalar...  29.4 us
    unnamed x87, local copies, waits for them, and re-layouts  25.6 us
    all_to_all x6, starting transfers between devices, swap_groups(): lax.all_to_all(grouped, 'frames', split_axis=0, concat_axis=0, tiled=True)  25.3 us
    pallas_call x1, Pallas kernels, middle_block(): pl.pallas_call(middle_kernel, grid=(FF // wide,), out_shape=[of((count, D...  25 us
  transfers between devices with their start and end apart: 28, of which 9 were waited for; matrix products, arithmetic and copies ran while one was open for 6% of the time, Pallas kernels for 53%

profile of v5, /device:TPU:0, one launch (start us, length us, event | category | flops | bytes accessed | tf_op | source)
XLA Modules:
  0.0 523.4 jit_solution(15350777373736657940)
XLA Ops:
  7.2 2.7 constant_dynamic-slice_fusion.1
  9.9 4.0 collective-permute-start
  15.9 6.5 %fusion.8.mod.refs_3_.refs_9_ = f32[1,6144]{1,0:T(1,128)S(1)} fusion(bf16[1024,1]{0,1:T(2,128)(2,1)S(1)} %reshape.213, bf16[1024,6144]{1,0:T(8,128)(2,1)} %param.21), kind=kOutput, calls=%fused_computation.30 | convolution fusion | flops 12582912 | bytes 12609536 | tf_op jit(solution)/shard_map/dot_general | solution.py:1153
  23.0 2.8 rotary_tables.1
  26.9 5.7 %input_projections.2 = (bf16[256,1024]{1,0:T(8,128)(2,1)S(1)}, bf16[8,3,256,128]{3,2,1,0:T(8,128)(2,1)S(1)}) custom-call(bf16[256,1024]{1,0:T(8,128)(2,1)S(1)} %bitcast.56, f32[1,6144]{1,0:T(1,128)S(1)} %fusion.8.mod.refs_3_.refs_9_, bf16[1024,1024]{1,0:T(8,128)(2,1)S(1)} %copy-done.1, bf16[1024,1024]{1,0:T(8,128)(2,1)} %refs_4_.3, ...), custom_call_target="tpu_custom_call" | custom-call | flops 1610612736 | bytes 12582912 | tf_op jit(solution)/shard_map/input_projections/pallas_call | solution.py:492
  34.5 2.8 collective-permute-done.unused_0_.tokens
  38.1 4.4 all-to-all-start
  42.5 5.7 %input_projections.3 = (bf16[256,1024]{1,0:T(8,128)(2,1)S(1)}, bf16[8,3,256,128]{3,2,1,0:T(8,128)(2,1)S(1)}) custom-call(bf16[256,1024]{1,0:T(8,128)(2,1)S(1)} %copy-done.9, f32[1,6144]{1,0:T(1,128)S(1)} %fusion.8.mod.refs_3_.refs_9_, bf16[1024,1024]{1,0:T(8,128)(2,1)S(1)} %copy-done.1, bf16[1024,1024]{1,0:T(8,128)(2,1)} %refs_4_.3, ...), custom_call_target="tpu_custom_call" | custom-call | flops 1610612736 | bytes 12582912 | tf_op jit(solution)/shard_map/input_projections/pallas_call | solution.py:492
  50.2 13.4 %all-to-all-done.refs_2_.refs_6_.refs_8_.refs_10_.refs_7_ = bf16[8,3,256,128]{3,2,1,0:T(8,128)(2,1)} async-done(((bf16[8,3,256,128]{3,2,1,0:T(8,128)(2,1)}), bf16[8,3,256,128]{3,2,1,0:T(8,128)(2,1)}, u32[]{:S(2)}, u32[]{:S(2)}) %all-to-all-start) | async-done | bytes 1572896 | tf_op jit(solution)/shard_map/all_to_all | solution.py:1096
  63.6 3.6 all-to-all-start.1
  68.1 2.3 slice.56
  71.3 16.8 %all-to-all-done.1.refs_3_.refs_7_.refs_9_.refs_8_ = bf16[8,3,256,128]{3,2,1,0:T(8,128)(2,1)S(1)} async-done(((bf16[8,3,256,128]{3,2,1,0:T(8,128)(2,1)}), bf16[8,3,256,128]{3,2,1,0:T(8,128)(2,1)S(1)}, u32[]{:S(2)}, u32[]{:S(2)}) %all-to-all-start.1) | async-done | bytes 1572896 | tf_op jit(solution)/shard_map/all_to_all | solution.py:1096
  89.3 29.1 %attention_forward.2 = (s32[1]{0:T(128)}, f32[8,512,128]{2,1,0:T(8,128)}, f32[8,512,128]{2,1,0:T(8,128)}, f32[8,512,128]{2,1,0:T(8,128)}) custom-call(s32[8]{0:T(128)} %get-tuple-element.71.refs_0_.refs_2_.refs_4_.refs_3_, s32[1]{0:T(128)} %constant.40.clone.1.refs_1_.mine, bf16[8,3,256,128]{3,2,1,0:T(8,128)(2,1)} %all-to-all-done.refs_2_.refs_6_.refs_8_.refs_10_.refs_7_, ...), custom_call_target="tpu_custom_call" | custom-call | flops 38654705664 | bytes 16777216 | tf_op jit(solution)/shard_map/attention_forward/pallas_call | solution.py:254
  118.7 2.9 collective-permute-start.3
  121.6 31.9 %attention_forward.3 = (bf16[8,512,128]{2,1,0:T(8,128)(2,1)}, f32[8,8,512]{2,1,0:T(8,128)}) custom-call(s32[8]{0:T(128)} %get-tuple-element.71.refs_0_.refs_2_.refs_4_.refs_3_, s32[1]{0:T(128)} %get-tuple-element.76.refs_1_, bf16[8,3,256,128]{3,2,1,0:T(8,128)(2,1)} %all-to-all-done.refs_2_.refs_6_.refs_8_.refs_10_.refs_7_, ...), custom_call_target="tpu_custom_call" | custom-call | flops 38654705664 | bytes 16777216 | tf_op jit(solution)/shard_map/attention_forward/pallas_call | solution.py:254
  153.5 4.4 all-to-all-start.2
  159.3 3.4 copy-done.27
  162.7 6.6 %pull_down.1 = (bf16[512,4096]{1,0:T(8,128)(2,1)S(1)}, bf16[1024,512]{1,0:T(8,128)(2,1)S(1)}) custom-call(bf16[512,1024]{1,0:T(8,128)(2,1)S(1)} %pad_maximum_fusion.1.cotangent.refs_2_, f32[1,6144]{1,0:T(1,128)S(1)} %fusion.8.mod.refs_3_.refs_9_, bf16[4096,1024]{1,0:T(8,128)(2,1)S(1)} %copy-done.27), custom_call_target="tpu_custom_call" | custom-call | flops 4294967296 | bytes 14680064 | tf_op jit(solution)/shard_map/pull_down/pallas_call | solution.py:522
  173.3 25.0 %middle_block.1 = (f32[512,1024]{1,0:T(8,128)}, bf16[512,1024]{1,0:T(8,128)(2,1)}, bf16[512,4096]{1,0:T(8,128)(2,1)}, bf16[512,4096]{1,0:T(8,128)(2,1)}, f32[512...) custom-call(bf16[8,512,128]{2,1,0:T(8,128)(2,1)} %all-to-all-done.2., ...), custom_call_target="tpu_custom_call" | custom-call | flops 10737418240 | bytes 31457280 | tf_op jit(solution)/shard_map/middle_block/pallas_call | solution.py:604
  198.4 12.2 %weight_gradients.3 = (bf16[4,4,1024,128]{3,2,1,0:T(8,128)(2,1)}, bf16[4,128,5120]{2,1,0:T(8,128)(2,1)}) custom-call(s32[1]{0:T(128)} %bitcast.slot, bf16[512,4096]{1,0:T(8,128)(2,1)} %get-tuple-element.82.active.refs_0_, bf16[512,4096]{1,0:T(8,128)(2,1)} %get-tuple-element.83.grad_up_in, bf16[512,1024]{1,0:T(8,128)(2,1)} %get-tuple-element.84.hidden, ...), custom_call_target="tpu_custom_call" | custom-call | flops 4831838208 | bytes 25165824 | tf_op jit(solution)/shard_map/weight_gradients/pallas_call | solution.py:733
  212.7 4.6 all-to-all-start.3
  218.0 20.0 %weight_gradients.2 = (bf16[512,1024]{1,0:T(8,128)(2,1)}, f32[1,1024]{1,0:T(1,128)}, bf16[4,4,1024,128]{3,2,1,0:T(8,128)(2,1)}, bf16[4,128,5120]{2,1,0:T(8,128)(2,1)}) custom-call(s32[1]{0:T(128)} %bitcast.slot, bf16[512,4096]{1,0:T(8,128)(2,1)} %get-tuple-element.82.active.refs_0_, bf16[512,4096]{1,0:T(8,128)(2,1)} %get-tuple-element.83.grad_up_in, ...), custom_call_target="tpu_custom_call" | custom-call | flops 9126805504 | bytes 25165824 | tf_op jit(solution)/shard_map/weight_gradients/pallas_call | solution.py:733
  240.5 5.9 %add_halves.8 = (bf16[2,4,1024,128]{3,2,1,0:T(8,128)(2,1)}, bf16[2,4,1024,128]{3,2,1,0:T(8,128)(2,1)}) custom-call(s32[1]{0:T(128)} %constant.40.clone.1.refs_1_.mine, bf16[2,2,4,1024,128]{4,3,2,1,0:T(8,128)(2,1)} %bitcast.64, bf16[2,2,4,1024,128]{4,3,2,1,0:T(8,128)(2,1)} %bitcast.17.refs_1_.refs_3_, bf16[2,2,4,1024,128]{4,3,2,1,0:T(8,128)(2,1)} %bitcast.65, ...), custom_call_target="tpu_custom_call" | custom-call | flops 2097152 | bytes 12582912 | tf_op jit(solution)/shard_map/add_halves/pallas_call | solution.py:905
  248.3 6.8 %add_halves.9 = (bf16[1,8,32,5120]{3,2,1,0:T(8,128)(2,1)}, bf16[1,8,32,5120]{3,2,1,0:T(8,128)(2,1)}) custom-call(s32[1]{0:T(128)} %constant.40.clone.1.refs_1_.mine, bf16[1,2,8,32,5120]{4,3,2,1,0:T(8,128)(2,1)} %bitcast.62, bf16[1,2,8,32,5120]{4,3,2,1,0:T(8,128)(2,1)} %bitcast.20.refs_1_.refs_3_, bf16[1,2,8,32,5120]{4,3,2,1,0:T(8,128)(2,1)} %bitcast.63, ...), custom_call_target="tpu_custom_call" | custom-call | flops 2621440 | bytes 15728640 | tf_op jit(solution)/shard_map/add_halves/pallas_call | solution.py:905
  261.1 3.7 all-to-all-start.4
  264.8 54.9 %attention_backward.3 = (f32[8,128,512]{2,1,0:T(8,128)}, bf16[8,2,256,128]{3,2,1,0:T(8,128)(2,1)}, bf16[8,2,256,128]{3,2,1,0:T(8,128)(2,1)}) custom-call(bf16[2,2,2,1024,128]{4,3,2,1,0:T(8,128)(2,1)} %bitcast.92, bf16[2,2,2,32,5120]{4,3,2,1,0:T(8,128)(2,1)} %bitcast.87, s32[8]{0:T(128)} %get-tuple-element.71.refs_0_.refs_2_.refs_4_.refs_3_, ...), custom_call_target="tpu_custom_call" | custom-call | flops 60397977600 | bytes 16777216 | tf_op jit(solution)/shard_map/attention_backward/pallas_call | solution.py:401
  321.7 8.4 %all-to-all-done.4 = bf16[32,2,2064]{2,1,0:T(2,128)(2,1)S(1)} async-done(((bf16[32,2,2064]{2,1,0:T(2,128)(2,1)}), bf16[32,2,2064]{2,1,0:T(2,128)(2,1)S(1)}, u32[]{:S(2)}, u32[]{:S(2)}) %all-to-all-start.4) | async-done | bytes 264224 | tf_op jit(solution)/shard_map/all_to_all | solution.py:1201
  331.2 3.6 add_halves.10
  336.5 3.8 add_halves.11
  342.0 31.7 %attention_backward.4 = (f32[8,128,512]{2,1,0:T(8,128)}, bf16[8,2,256,128]{3,2,1,0:T(8,128)(2,1)}) custom-call(bf16[2,2,1024,128]{3,2,1,0:T(8,128)(2,1)} %bitcast.109, bf16[2,2,32,5120]{3,2,1,0:T(8,128)(2,1)} %bitcast.107, bf16[256,1024]{1,0:T(8,128)(2,1)} %collective-permute-done.4.refs_2_, bf16[32,4128]{1,0:T(8,128)(2,1)} %bitcast.101, ...), custom_call_target="tpu_custom_call" | custom-call | flops 30198988800 | bytes 16777216 | tf_op jit(solution)/shard_map/attention_backward/pallas_call | solution.py:401
  373.7 2.5 add_halves.12
  377.6 2.5 add_convert_fusion.refs_2_
  380.1 4.0 all-to-all-start.5
  385.2 2.6 add_halves.13
  388.3 32.3 %attention_backward.5.unused_3_ = bf16[8,4,256,128]{3,2,1,0:T(8,128)(2,1)} custom-call(bf16[2,1024,128]{2,1,0:T(8,128)(2,1)} %bitcast.113, bf16[2,32,5120]{2,1,0:T(8,128)(2,1)} %bitcast.111, bf16[8,2,256,128]{3,2,1,0:T(8,128)(2,1)} %add_convert_fusion.refs_2_, s32[8]{0:T(128)} %get-tuple-element.71.refs_0_.refs_2_.refs_4_.refs_3_, ...), custom_call_target="tpu_custom_call" | custom-call | flops 30198988800 | bytes 16777216 | tf_op jit(solution)/shard_map/attention_backward/pallas_call | solution.py:401
  422.6 4.3 all-to-all-start.6
  429.1 2.4 collective-permute-start.17
  431.6 2.2 add_halves.14
  434.3 3.4 copy-done.6
  439.6 8.2 %head_gradients.1.refs_0_ = bf16[1024,384]{1,0:T(8,128)(2,1)S(1)} custom-call(bf16[1024,128]{1,0:T(8,128)(2,1)S(1)} %bitcast.61, bf16[32,5120]{1,0:T(8,128)(2,1)S(1)} %bitcast.59, bf16[8,2,256,128]{3,2,1,0:T(8,128)(2,1)} %add_convert_fusion.refs_2_, bf16[8,4,256,128]{3,2,1,0:T(8,128)(2,1)S(1)} %copy-done, bf16[8,1024,512]{2,1,0:T(8,128)(2,1)S(1)} %bitcast.55, ...), custom_call_target="tpu_custom_call" | custom-call | flops 3221225472 | bytes 12582912 | tf_op jit(solution)/shard_map/head_gradients/pallas_call | solution.py:799
  448.8 9.8 %collective-permute-done.16.unused_1_.refs_2_ = bf16[1024,128]{1,0:T(8,128)(2,1)} collective-permute-done((bf16[1024,128]{1,0:T(8,128)(2,1)}, bf16[1024,128]{1,0:T(8,128)(2,1)}, u32[]{:S(2)}, u32[]{:S(2)}) %collective-permute-start.16) | collective-permute-done | bytes 262176 | tf_op jit(solution)/shard_map/ppermute | solution.py:1137
  458.6 6.0 %all-to-all-start.7 = ((bf16[32,32,384]{2,1,0:T(8,128)(2,1)}), bf16[32,32,384]{2,1,0:T(8,128)(2,1)}, u32[]{:S(2)}, u32[]{:S(2)}) async-start(bf16[32,32,384]{2,1,0:T(8,128)(2,1)} %bitcast.72), calls=%async_computation.7 | async-start | bytes 1572864 | tf_op jit(solution)/shard_map/all_to_all | solution.py:1241
  464.7 9.4 %input_gradients.1 = (bf16[512,1024]{1,0:T(8,128)(2,1)S(1)}, f32[1,1024]{1,0:T(1,128)S(1)}, f32[1,1024]{1,0:T(1,128)S(1)}) custom-call(bf16[1024,384]{1,0:T(8,128)(2,1)S(1)} %head_gradients.1.refs_0_, bf16[8,2,256,128]{3,2,1,0:T(8,128)(2,1)S(1)} %copy-done.3, bf16[8,4,256,128]{3,2,1,0:T(8,128)(2,1)} %all-to-all-done.6.refs_2_.unused_0_, ...), custom_call_target="tpu_custom_call" | custom-call | flops 3221225472 | bytes 14680064 | tf_op jit(solution)/shard_map/input_gradients/pallas_call | solution.py:859
  474.2 2.9 collective-permute-start.15
  488.7 6.8 %all-to-all-done.7.unused_0_ = bf16[32,32,384]{2,1,0:T(8,128)(2,1)} async-done(((bf16[32,32,384]{2,1,0:T(8,128)(2,1)}), bf16[32,32,384]{2,1,0:T(8,128)(2,1)}, u32[]{:S(2)}, u32[]{:S(2)}) %all-to-all-start.7) | async-done | bytes 786464 | tf_op jit(solution)/shard_map/all_to_all | solution.py:1241
  496.1 4.4 all-to-all-start.8
  500.5 9.0 %collective-permute-done.15 = bf16[256,1024]{1,0:T(8,128)(2,1)S(1)} collective-permute-done((bf16[256,1024]{1,0:T(8,128)(2,1)S(1)}, bf16[256,1024]{1,0:T(8,128)(2,1)S(1)}, u32[]{:S(2)}, u32[]{:S(2)}) %collective-permute-start.15) | collective-permute-done | bytes 524320 | tf_op jit(solution)/shard_map/ppermute | solution.py:1088
  513.6 2.8 mod_gradient.1
  (162 shorter events, 62.5 us)
Async XLA Ops:
  7.2 6.8 %copy-start.39 = (s32[1,2]{1,0:T(1,128)S(1)}, s32[1,2]{1,0:T(1,128)}, u32[]{:S(2)}) copy-start(s32[1,2]{1,0:T(1,128)} %param.14) | copy-start | bytes 28
  9.9 27.4 %collective-permute-start = (bf16[256,1024]{1,0:T(8,128)(2,1)}, bf16[256,1024]{1,0:T(8,128)(2,1)S(1)}, u32[]{:S(2)}, u32[]{:S(2)}) collective-permute-start(bf16[256,1024]{1,0:T(8,128)(2,1)} %bitcast.1), channel_id=1, source_target_pairs={{0,2},{2,0},{1,3},{3,1},{4,6},{6,4},{5,7},{7,5},{8,10},{10,8},{9,1... | collective-permute-start | bytes 1572872 | tf_op jit(solution)/shard_map/ppermute | solution.py:1088
  15.9 11.0 %copy-start.1 = (bf16[1024,1024]{1,0:T(8,128)(2,1)S(1)}, bf16[1024,1024]{1,0:T(8,128)(2,1)}, u32[]{:S(2)}) copy-start(bf16[1024,1024]{1,0:T(8,128)(2,1)} %refs_3_.1) | copy-start | bytes 6291460
  22.4 136.9 %copy-start.19 = (f32[1,6144]{1,0:T(1,128)}, f32[1,6144]{1,0:T(1,128)S(1)}, u32[]{:S(2)}) copy-start(f32[1,6144]{1,0:T(1,128)S(1)} %fusion.8.mod.refs_3_.refs_9_) | copy-start | bytes 73732
  38.1 4.4 copy-start.9
  38.1 25.5 %all-to-all-start = ((bf16[8,3,256,128]{3,2,1,0:T(8,128)(2,1)}), bf16[8,3,256,128]{3,2,1,0:T(8,128)(2,1)}, u32[]{:S(2)}, u32[]{:S(2)}) async-start(bf16[8,3,256,128]{3,2,1,0:T(8,128)(2,1)} %order_after.5), calls=%async_computation | async-start | bytes 3145728 | tf_op jit(solution)/shard_map/all_to_all | solution.py:1096
  50.2 17.0 %copy-start.40 = (s32[8]{0:T(128)S(1)}, s32[8]{0:T(128)}, u32[]{:S(2)}) copy-start(s32[8]{0:T(128)} %times.1) | copy-start | bytes 100
  63.6 24.5 %all-to-all-start.1 = ((bf16[8,3,256,128]{3,2,1,0:T(8,128)(2,1)}), bf16[8,3,256,128]{3,2,1,0:T(8,128)(2,1)S(1)}, u32[]{:S(2)}, u32[]{:S(2)}) async-start(bf16[8,3,256,128]{3,2,1,0:T(8,128)(2,1)} %copy-done.11), calls=%async_computation.1 | async-start | bytes 3145728 | tf_op jit(solution)/shard_map/all_to_all | solution.py:1096
  70.4 48.0 %collective-permute-start.1 = (bf16[8,2,256,128]{3,2,1,0:T(8,128)(2,1)}, bf16[8,2,256,128]{3,2,1,0:T(8,128)(2,1)}, u32[]{:S(2)}, u32[]{:S(2)}) collective-permute-start(bf16[8,2,256,128]{3,2,1,0:T(8,128)(2,1)} %slice.56), channel_id=1, source_target_pairs={{0,1},{1,0},{2,3},{3,2},{4,5},{5,4},{6,7},{7,6},{8,9},{9,8},{10,11... | collective-permute-start | bytes 3145736 | tf_op jit(solution)/shard_map/ppermute | solution.py:1099
  88.2 30.5 %collective-permute-start.2 = (bf16[8,2,256,128]{3,2,1,0:T(8,128)(2,1)S(1)}, bf16[8,2,256,128]{3,2,1,0:T(8,128)(2,1)}, u32[]{:S(2)}, u32[]{:S(2)}) collective-permute-start(bf16[8,2,256,128]{3,2,1,0:T(8,128)(2,1)S(1)} %slice.57), channel_id=1, source_target_pairs={{0,1},{1,0},{2,3},{3,2},{4,5},{5,4},{6,7},{7,6},{8,9},{9,8},{10,11... | collective-permute-start | bytes 3145736 | tf_op jit(solution)/shard_map/ppermute | solution.py:1099
  118.7 40.5 %collective-permute-start.3 = (bf16[256,1024]{1,0:T(8,128)(2,1)}, bf16[256,1024]{1,0:T(8,128)(2,1)S(1)}, u32[]{:S(2)}, u32[]{:S(2)}) collective-permute-start(bf16[256,1024]{1,0:T(8,128)(2,1)} %order_after.6), channel_id=1, source_target_pairs={{0,2},{2,0},{1,3},{3,1},{4,6},{6,4},{5,7},{7,5},{8,10},{10,8},{9,1... | collective-permute-start | bytes 1572872 | tf_op jit(solution)/shard_map/ppermute | solution.py:1088
  153.5 5.7 %copy-start.35 = (bf16[1,1,8,32,1024]{4,3,2,1,0:T(8,128)(2,1)S(1)}, bf16[1,1,8,32,1024]{4,3,2,1,0:T(8,128)(2,1)}, u32[]{:S(2)}) copy-start(bf16[1,1,8,32,1024]{4,3,2,1,0:T(8,128)(2,1)} %get-tuple-element.164) | copy-start | bytes 1572868
  153.5 19.8 %all-to-all-start.2 = ((bf16[8,512,128]{2,1,0:T(8,128)(2,1)}), bf16[8,512,128]{2,1,0:T(8,128)(2,1)}, u32[]{:S(2)}, u32[]{:S(2)}) async-start(bf16[8,512,128]{2,1,0:T(8,128)(2,1)} %get-tuple-element.80.refs_4_.refs_6_.refs_5_), calls=%async_computation.2 | async-start | bytes 2097152 | tf_op jit(solution)/shard_map/all_to_all | solution.py:1096
  157.9 276.4 %all-gather.3.cloned.1.call-start = ((), (), s32[]{:S(2)}) async-start(), calls=%async_computation.9 | async-start | bytes 9437184 | tf_op jit(solution)/shard_map/all_gather | solution.py:1170
  162.7 6.6 %copy-start.12 = (bf16[512,1024]{1,0:T(8,128)(2,1)}, bf16[512,1024]{1,0:T(8,128)(2,1)S(1)}, u32[]{:S(2)}) copy-start(bf16[512,1024]{1,0:T(8,128)(2,1)S(1)} %pad_maximum_fusion.1.cotangent.refs_2_) | copy-start | bytes 3145732
  171.3 27.1 %copy-start.29 = (bf16[1024,512]{1,0:T(8,128)(2,1)}, bf16[1024,512]{1,0:T(8,128)(2,1)S(1)}, u32[]{:S(2)}) copy-start(bf16[1024,512]{1,0:T(8,128)(2,1)S(1)} %get-tuple-element.85.scaled_turned) | copy-start | bytes 3145732
  198.4 12.8 %copy-start.16 = (bf16[256,1024]{1,0:T(8,128)(2,1)S(1)}, bf16[256,1024]{1,0:T(8,128)(2,1)}, u32[]{:S(2)}) copy-start(bf16[256,1024]{1,0:T(8,128)(2,1)} %copy-done.15) | copy-start | bytes 1572868
  198.4 12.8 %copy-start.18 = (bf16[256,1024]{1,0:T(8,128)(2,1)S(1)}, bf16[256,1024]{1,0:T(8,128)(2,1)}, u32[]{:S(2)}) copy-start(bf16[256,1024]{1,0:T(8,128)(2,1)} %copy-done.17) | copy-start | bytes 1572868
  210.6 37.6 %collective-permute-start.6 = (bf16[4,128,5120]{2,1,0:T(8,128)(2,1)}, bf16[4,128,5120]{2,1,0:T(8,128)(2,1)}, u32[]{:S(2)}, u32[]{:S(2)}) collective-permute-start(bf16[4,128,5120]{2,1,0:T(8,128)(2,1)} %get-tuple-element.93), channel_id=1, source_target_pairs={{0,4},{4,0},{8,12},{12,8},{16,20},{20,16},{24,28},{28,24},{1,5},{5... | collective-permute-start | bytes 15728648 | tf_op jit(solution)/shard_map/ppermute | solution.py:1102
  210.6 29.9 %collective-permute-start.5 = (bf16[4,4,1024,128]{3,2,1,0:T(8,128)(2,1)}, bf16[4,4,1024,128]{3,2,1,0:T(8,128)(2,1)}, u32[]{:S(2)}, u32[]{:S(2)}) collective-permute-start(bf16[4,4,1024,128]{3,2,1,0:T(8,128)(2,1)} %get-tuple-element.90), channel_id=1, source_target_pairs={{0,4},{4,0},{8,12},{12,8},{16,20},{20,16},{24,28},{28,24},{1,5},{5... | collective-permute-start | bytes 12582920 | tf_op jit(solution)/shard_map/ppermute | solution.py:1102
  212.7 43.8 %all-to-all-start.3 = ((bf16[8,512,128]{2,1,0:T(8,128)(2,1)}), bf16[8,512,128]{2,1,0:T(8,128)(2,1)}, u32[]{:S(2)}, u32[]{:S(2)}) async-start(bf16[8,512,128]{2,1,0:T(8,128)(2,1)} %get-tuple-element.95), calls=%async_computation.3 | async-start | bytes 2097152 | tf_op jit(solution)/shard_map/all_to_all | solution.py:1096
  239.8 102.2 %collective-permute-start.4 = (bf16[256,1024]{1,0:T(8,128)(2,1)}, bf16[256,1024]{1,0:T(8,128)(2,1)}, u32[]{:S(2)}, u32[]{:S(2)}) collective-permute-start(bf16[256,1024]{1,0:T(8,128)(2,1)} %slice.51), channel_id=1, source_target_pairs={{0,2},{2,0},{1,3},{3,1},{4,6},{6,4},{5,7},{7,5},{8,10},{10,8},{9,1... | collective-permute-start | bytes 1572872 | tf_op jit(solution)/shard_map/ppermute | solution.py:1088
  246.4 84.8 %collective-permute-start.7 = (bf16[2,2,2,1024,128]{4,3,2,1,0:T(8,128)(2,1)}, bf16[2,2,2,1024,128]{4,3,2,1,0:T(8,128)(2,1)}, u32[]{:S(2)}, u32[]{:S(2)}) collective-permute-start(bf16[2,2,2,1024,128]{4,3,2,1,0:T(8,128)(2,1)} %bitcast.90), channel_id=1, source_target_pairs={{0,8},{4,12},{8,0},{12,4},{16,24},{20,28},{24,16},{28,20},{1,9},{5... | collective-permute-start | bytes 6291464 | tf_op jit(solution)/shard_map/ppermute | solution.py:1137
  255.0 80.0 %collective-permute-start.8 = (bf16[2,2,2,32,5120]{4,3,2,1,0:T(8,128)(2,1)}, bf16[2,2,2,32,5120]{4,3,2,1,0:T(8,128)(2,1)S(1)}, u32[]{:S(2)}, u32[]{:S(2)}) collective-permute-start(bf16[2,2,2,32,5120]{4,3,2,1,0:T(8,128)(2,1)} %bitcast.85), channel_id=1, source_target_pairs={{0,16},{4,20},{8,24},{12,28},{16,0},{20,4},{24,8},{28,12},{1,17},{... | collective-permute-start | bytes 7864328 | tf_op jit(solution)/shard_map/ppermute | solution.py:1137
  261.1 69.0 %all-to-all-start.4 = ((bf16[32,2,2064]{2,1,0:T(2,128)(2,1)}), bf16[32,2,2064]{2,1,0:T(2,128)(2,1)S(1)}, u32[]{:S(2)}, u32[]{:S(2)}) async-start(bf16[32,2,2064]{2,1,0:T(2,128)(2,1)} %reshape.223), calls=%async_computation.4 | async-start | bytes 557056 | tf_op jit(solution)/shard_map/all_to_all | solution.py:1201
  319.6 58.0 %collective-permute-start.13 = (bf16[8,2,256,128]{3,2,1,0:T(8,128)(2,1)}, bf16[8,2,256,128]{3,2,1,0:T(8,128)(2,1)}, u32[]{:S(2)}, u32[]{:S(2)}) collective-permute-start(bf16[8,2,256,128]{3,2,1,0:T(8,128)(2,1)} %get-tuple-element.112), channel_id=1, source_target_pairs={{0,1},{1,0},{2,3},{3,2},{4,5},{5,4},{6,7},{7,6},{8,9},{9,8},{10,11... | collective-permute-start | bytes 3145736 | tf_op jit(solution)/shard_map/ppermute | solution.py:1099
  321.4 66.9 %collective-permute-start.14 = (bf16[8,2,256,128]{3,2,1,0:T(8,128)(2,1)}, bf16[8,2,256,128]{3,2,1,0:T(8,128)(2,1)}, u32[]{:S(2)}, u32[]{:S(2)}) collective-permute-start(bf16[8,2,256,128]{3,2,1,0:T(8,128)(2,1)} %get-tuple-element.113), channel_id=1, source_target_pairs={{0,1},{1,0},{2,3},{3,2},{4,5},{5,4},{6,7},{7,6},{8,9},{9,8},{10,11... | collective-permute-start | bytes 3145736 | tf_op jit(solution)/shard_map/ppermute | solution.py:1099
  334.7 38.9 %collective-permute-start.9 = (bf16[2,2,1024,128]{3,2,1,0:T(8,128)(2,1)}, bf16[2,2,1024,128]{3,2,1,0:T(8,128)(2,1)}, u32[]{:S(2)}, u32[]{:S(2)}) collective-permute-start(bf16[2,2,1024,128]{3,2,1,0:T(8,128)(2,1)} %bitcast.108), channel_id=1, source_target_pairs={{0,16},{4,20},{8,24},{12,28},{16,0},{20,4},{24,8},{28,12},{1,17},{... | collective-permute-start | bytes 3145736 | tf_op jit(solution)/shard_map/ppermute | solution.py:1137
  340.3 43.8 %collective-permute-start.11 = (bf16[2,2,32,5120]{3,2,1,0:T(8,128)(2,1)}, bf16[2,2,32,5120]{3,2,1,0:T(8,128)(2,1)S(1)}, u32[]{:S(2)}, u32[]{:S(2)}) collective-permute-start(bf16[2,2,32,5120]{3,2,1,0:T(8,128)(2,1)} %bitcast.106), channel_id=1, source_target_pairs={{0,8},{4,12},{8,0},{12,4},{16,24},{20,28},{24,16},{28,20},{1,9},{5... | collective-permute-start | bytes 3932168 | tf_op jit(solution)/shard_map/ppermute | solution.py:1137
  373.7 4.0 copy-start.36
  376.2 44.5 %collective-permute-start.10 = (bf16[2,1024,128]{2,1,0:T(8,128)(2,1)}, bf16[2,1024,128]{2,1,0:T(8,128)(2,1)S(1)}, u32[]{:S(2)}, u32[]{:S(2)}) collective-permute-start(bf16[2,1024,128]{2,1,0:T(8,128)(2,1)} %bitcast.112), channel_id=1, source_target_pairs={{0,1},{1,0},{2,3},{3,2},{4,5},{5,4},{6,7},{7,6},{8,9},{9,8},{10,11... | collective-permute-start | bytes 1572872 | tf_op jit(solution)/shard_map/ppermute | solution.py:1137
  380.1 40.5 %all-to-all-start.5 = ((bf16[8,2,256,128]{3,2,1,0:T(8,128)(2,1)}), bf16[8,2,256,128]{3,2,1,0:T(8,128)(2,1)S(1)}, u32[]{:S(2)}, u32[]{:S(2)}) async-start(bf16[8,2,256,128]{3,2,1,0:T(8,128)(2,1)} %add_convert_fusion.refs_2_), calls=%async_computation.5 | async-start | bytes 2097152 | tf_op jit(solution)/shard_map/all_to_all | solution.py:1096
  387.8 32.9 %collective-permute-start.12 = (bf16[2,32,5120]{2,1,0:T(8,128)(2,1)}, bf16[2,32,5120]{2,1,0:T(8,128)(2,1)S(1)}, u32[]{:S(2)}, u32[]{:S(2)}) collective-permute-start(bf16[2,32,5120]{2,1,0:T(8,128)(2,1)} %bitcast.110), channel_id=1, source_target_pairs={{0,1},{1,0},{2,3},{3,2},{4,5},{5,4},{6,7},{7,6},{8,9},{9,8},{10,11... | collective-permute-start | bytes 1966088 | tf_op jit(solution)/shard_map/ppermute | solution.py:1137
  422.6 36.0 %all-to-all-start.6 = ((bf16[8,4,256,128]{3,2,1,0:T(8,128)(2,1)}), bf16[8,4,256,128]{3,2,1,0:T(8,128)(2,1)}, u32[]{:S(2)}, u32[]{:S(2)}) async-start(bf16[8,4,256,128]{3,2,1,0:T(8,128)(2,1)} %order_after.7.refs_0_.refs_3_), calls=%async_computation.6 | async-start | bytes 4194304 | tf_op jit(solution)/shard_map/all_to_all | solution.py:1096
  429.1 29.5 %collective-permute-start.17 = (bf16[32,5120]{1,0:T(8,128)(2,1)}, bf16[32,5120]{1,0:T(8,128)(2,1)}, u32[]{:S(2)}, u32[]{:S(2)}) collective-permute-start(bf16[32,5120]{1,0:T(8,128)(2,1)} %bitcast.58), channel_id=1, source_target_pairs={{0,2},{2,0},{1,3},{3,1},{4,6},{6,4},{5,7},{7,5},{8,10},{10,8},{9,1... | collective-permute-start | bytes 983048 | tf_op jit(solution)/shard_map/ppermute | solution.py:1137
  433.8 24.8 %collective-permute-start.16 = (bf16[1024,128]{1,0:T(8,128)(2,1)}, bf16[1024,128]{1,0:T(8,128)(2,1)}, u32[]{:S(2)}, u32[]{:S(2)}) collective-permute-start(bf16[1024,128]{1,0:T(8,128)(2,1)} %bitcast.60), channel_id=1, source_target_pairs={{0,2},{2,0},{1,3},{3,1},{4,6},{6,4},{5,7},{7,5},{8,10},{10,8},{9,1... | collective-permute-start | bytes 786440 | tf_op jit(solution)/shard_map/ppermute | solution.py:1137
  434.3 3.4 copy-start.6
  448.8 15.8 %copy-start.3 = (bf16[8,2,256,128]{3,2,1,0:T(8,128)(2,1)S(1)}, bf16[8,2,256,128]{3,2,1,0:T(8,128)(2,1)}, u32[]{:S(2)}) copy-start(bf16[8,2,256,128]{3,2,1,0:T(8,128)(2,1)} %copy-done.2) | copy-start | bytes 3145732
  448.8 15.9 %copy-start.10 = (bf16[512,1024]{1,0:T(8,128)(2,1)S(1)}, bf16[512,1024]{1,0:T(8,128)(2,1)}, u32[]{:S(2)}) copy-start(bf16[512,1024]{1,0:T(8,128)(2,1)} %pad_maximum_fusion.tokens.refs_8_) | copy-start | bytes 3145732
  448.8 15.9 %copy-start.13 = (f32[512,128]{1,0:T(8,128)S(1)}, f32[512,128]{1,0:T(8,128)}, u32[]{:S(2)}) copy-start(f32[512,128]{1,0:T(8,128)} %get-tuple-element.72.refs_6_) | copy-start | bytes 786436
  448.8 15.9 %copy-start.14 = (f32[512,128]{1,0:T(8,128)S(1)}, f32[512,128]{1,0:T(8,128)}, u32[]{:S(2)}) copy-start(f32[512,128]{1,0:T(8,128)} %get-tuple-element.73.refs_7_) | copy-start | bytes 786436
  448.8 15.9 %copy-start.20 = (f32[1,6144]{1,0:T(1,128)S(1)}, f32[1,6144]{1,0:T(1,128)}, u32[]{:S(2)}) copy-start(f32[1,6144]{1,0:T(1,128)} %copy-done.19) | copy-start | bytes 73732
  458.6 36.8 %all-to-all-start.7 = ((bf16[32,32,384]{2,1,0:T(8,128)(2,1)}), bf16[32,32,384]{2,1,0:T(8,128)(2,1)}, u32[]{:S(2)}, u32[]{:S(2)}) async-start(bf16[32,32,384]{2,1,0:T(8,128)(2,1)} %bitcast.72), calls=%async_computation.7 | async-start | bytes 1572864 | tf_op jit(solution)/shard_map/all_to_all | solution.py:1241
  464.7 12.4 %copy-start.37 = (bf16[512,1024]{1,0:T(8,128)(2,1)S(1)}, bf16[512,1024]{1,0:T(8,128)(2,1)}, u32[]{:S(2)}) copy-start(bf16[512,1024]{1,0:T(8,128)(2,1)} %get-tuple-element.88) | copy-start | bytes 3145732
  474.1 5.1 copy-start.4
  474.2 35.3 %collective-permute-start.15 = (bf16[256,1024]{1,0:T(8,128)(2,1)S(1)}, bf16[256,1024]{1,0:T(8,128)(2,1)S(1)}, u32[]{:S(2)}, u32[]{:S(2)}) collective-permute-start(bf16[256,1024]{1,0:T(8,128)(2,1)S(1)} %slice.53), channel_id=1, source_target_pairs={{0,2},{2,0},{1,3},{3,1},{4,6},{6,4},{5,7},{7,5},{8,10},{10,8},{9,1... | collective-permute-start | bytes 1572872 | tf_op jit(solution)/shard_map/ppermute | solution.py:1088
  484.6 24.9 %copy-start.5 = (bf16[512,1024]{1,0:T(8,128)(2,1)S(1)}, bf16[512,1024]{1,0:T(8,128)(2,1)}, u32[]{:S(2)}) copy-start(bf16[512,1024]{1,0:T(8,128)(2,1)} %copy-done.4) | copy-start | bytes 3145732
  496.1 16.8 %all-to-all-start.8 = ((bf16[32,16,128]{2,1,0:T(8,128)(2,1)}), bf16[32,16,128]{2,1,0:T(8,128)(2,1)S(1)}, u32[]{:S(2)}, u32[]{:S(2)}) async-start(bf16[32,16,128]{2,1,0:T(8,128)(2,1)} %order_after.9), calls=%async_computation.8 | async-start | bytes 262144 | tf_op jit(solution)/shard_map/all_to_all | solution.py:1253
  (21 other events, 32.8 us)
Sparse Core Ops, SparseCore 0:
  212.6 84.0 all-gather.2
